TPU v7x, 512 devices: a whole 4x4x16 slice. The times are simulated.
512 devices in a mesh: dp: 32 (over x_hi, z), mp: 16 (over x_lo, y, core).
Axes of the slice: x: 4 (x_hi: 2, x_lo: 2; x = x_hi * 2 + x_lo), y: 4, z: 16, core: 2. Of those that a mesh axis runs over, the one named last changes fastest.
Arguments:
- captions: bfloat16 [65536, 1280], P(('dp', 'mp')), may hold values from -24 to 24
- audio: bfloat16 [512, 32, 1280], P(('dp', 'mp')), may hold values from -6 to 6
- caption_len: int32 [512], P('dp'), may hold values from 1 to 128
- pairing: int32 [32, 16], P('dp'), may hold values from 0 to 15, each once within a row
- enc_gain: float32 [1280], replicated, may hold values from 0.5 to 1.5
- enc_bias: float32 [1280], replicated, may hold values from -2.5 to 2.5
- dec_gain: float32 [1280], replicated, may hold values from 0.5 to 1.5
- dec_bias: float32 [1280], replicated, may hold values from -2.5 to 2.5
- w_query: bfloat16 [1280, 1024], P(None, 'mp'), may hold values from -0.15625 to 0.15625
- w_key: bfloat16 [1280, 1024], P(None, 'mp'), may hold values from -0.15625 to 0.15625
- w_value: bfloat16 [1280, 1024], P(None, 'mp'), may hold values from -0.15625 to 0.15625
- w_out: bfloat16 [1024, 1280], P('mp'), may hold values from -0.1875 to 0.1875
- grad_update: bfloat16 [65536, 1280], P(('dp', 'mp')), may hold values from -24 to 24
Outputs:
- cross_update: bfloat16 [65536, 1280], P(('dp', 'mp'))
- grad_captions: bfloat16 [65536, 1280], P(('dp', 'mp'))
- grad_audio: bfloat16 [512, 32, 1280], P(('dp', 'mp'))
- grad_wq: float32 [1280, 1024], P('dp', 'mp')
- grad_wo: float32 [1024, 1280], P('mp', 'dp')
Inputs may be any that keep to these rules, and one draw needn't show every extreme that they name: Each row of pairing names each of the group's 16 clips exactly once.
All inputs are finite; a program needn't handle non-finite values.
Results may differ from a plain program's by a relative error of at most 0.024.
Values may be sent and summed in bfloat16 or wider, within the bound.
No kernel may reach another device: no remote copies, remote signals or barrier semaphores. Data moves between devices by JAX's collectives and lax.ppermute only.
A program may use at most 64 MiB of HBM per device.

v0:
```python
import math

import jax
import jax.numpy as jnp
from jax import lax
from jax.sharding import PartitionSpec as P

HEAD_DIM = 64


EPSILON = 1e-05


def normalize(values, gain_vec, bias_vec):
    row_mean = jnp.mean(values, axis=-1, keepdims=True)
    centred = values - row_mean
    inverse_std = lax.rsqrt(jnp.mean(centred * centred, axis=-1, keepdims=True) + EPSILON)
    normed = centred * inverse_std
    return (normed * gain_vec + bias_vec, normed, inverse_std)


def norm_backward(upstream, normed, inverse_std, gain_vec):
    scaled = upstream * gain_vec
    mean_term = jnp.mean(scaled, axis=-1, keepdims=True)
    cross_term = jnp.mean(scaled * normed, axis=-1, keepdims=True)
    return inverse_std * (scaled - mean_term - normed * cross_term)


def transposed_dot(left_rows, right_rows):
    return lax.dot_general(
        left_rows, right_rows, (((1,), (1,)), ((), ())), preferred_element_type=jnp.float32
    )


def block_product(rows, full_weight, block_count):
    row_count = rows.shape[0]
    block_width = rows.shape[1] // block_count
    row_blocks = rows.reshape(row_count, block_count, block_width).transpose(1, 0, 2)
    weight_blocks = full_weight.reshape(block_count, block_width, full_weight.shape[1])

    def add_block(running, pieces):
        partial_sum = jnp.dot(pieces[0], pieces[1], preferred_element_type=jnp.float32)
        partial_low = lax.optimization_barrier(partial_sum.astype(jnp.bfloat16))
        return (running + partial_low.astype(jnp.float32), None)

    start_value = jnp.zeros((row_count, full_weight.shape[1]), jnp.float32)
    return lax.scan(add_block, start_value, (row_blocks, weight_blocks))[0]


def body(
    captions,
    audio,
    caption_len,
    pairing,
    enc_gain,
    enc_bias,
    dec_gain,
    dec_bias,
    w_query,
    w_key,
    w_value,
    w_out,
    grad_update,
):
    groups_mp = lax.axis_size("mp")
    model_width = captions.shape[1]
    cap_len = captions.shape[0]
    frames = audio.shape[1]
    local_width = w_query.shape[1]
    local_heads = local_width // HEAD_DIM
    attn_scale = 1.0 / math.sqrt(HEAD_DIM)
    own_index = lax.axis_index("mp")
    state_values, state_normed, state_inverse = normalize(
        audio[0].astype(jnp.float32), enc_gain, enc_bias
    )
    states = state_values.astype(jnp.bfloat16)
    hidden_values, caption_normed, caption_inverse = normalize(
        captions.astype(jnp.float32), dec_gain, dec_bias
    )
    hidden_own = hidden_values.astype(jnp.bfloat16)
    own_len = lax.dynamic_slice_in_dim(caption_len, own_index, 1, 0)
    positions = lax.broadcasted_iota(jnp.int32, (cap_len, 1), 0)
    upstream_own = jnp.where(positions < own_len[None, :], grad_update, jnp.zeros_like(grad_update))
    hidden_all, upstream_all = (
        lax.all_gather(hidden_own, "mp", axis=0, tiled=True),
        lax.all_gather(upstream_own, "mp", axis=0, tiled=True),
    )
    queries = jnp.dot(hidden_all, w_query, preferred_element_type=jnp.float32).astype(jnp.bfloat16)
    joined = jnp.concatenate([w_key, w_value], axis=1)
    shard_rows = lax.all_gather(states[None], "mp", axis=0, tiled=True)
    flat_rows = shard_rows.reshape(-1, model_width)
    product = jnp.dot(flat_rows, joined, preferred_element_type=jnp.float32).astype(jnp.bfloat16)
    both_rows = product.reshape(shard_rows.shape[0], frames, 2 * local_width)
    key_rows = both_rows[:, :, :local_width]
    value_rows = both_rows[:, :, local_width:]
    chosen = pairing[0]
    key_sel = jnp.take(key_rows, chosen, axis=0).reshape(groups_mp, frames, local_heads, HEAD_DIM)
    value_sel = jnp.take(value_rows, chosen, axis=0).reshape(
        groups_mp, frames, local_heads, HEAD_DIM
    )
    query_four = queries.reshape(groups_mp, cap_len, local_heads, HEAD_DIM)
    scores = (
        jnp.einsum("clhe,cfhe->chlf", query_four, key_sel, preferred_element_type=jnp.float32)
        * attn_scale
    )
    weights = jnp.exp(scores)
    softmax = weights / jnp.sum(weights, axis=-1, keepdims=True)
    softmax_low = softmax.astype(jnp.bfloat16)
    attended = jnp.einsum(
        "chlf,cfhe->clhe", softmax_low, value_sel, preferred_element_type=jnp.float32
    )
    attended = attended.astype(jnp.bfloat16).reshape(groups_mp * cap_len, local_width)
    query_trans = w_query.T
    out_full = lax.all_gather(w_out, "mp", axis=0, tiled=True)
    attended_own = lax.all_to_all(
        attended.reshape(groups_mp, cap_len, local_width),
        "mp",
        split_axis=0,
        concat_axis=2,
        tiled=True,
    )[0]
    cross_update = block_product(attended_own, out_full, groups_mp).astype(jnp.bfloat16)
    d_attended = transposed_dot(upstream_all, w_out).astype(jnp.bfloat16)
    wo_term = lax.dot_general(
        attended, upstream_all, (((0,), (0,)), ((), ())), preferred_element_type=jnp.float32
    )
    grad_wo = lax.psum_scatter(
        wo_term.astype(jnp.bfloat16), "dp", scatter_dimension=1, tiled=True
    ).astype(jnp.float32)
    d_att_four = d_attended.reshape(groups_mp, cap_len, local_heads, HEAD_DIM)
    d_softmax = jnp.einsum(
        "clhe,cfhe->chlf", d_att_four, value_sel, preferred_element_type=jnp.float32
    )
    d_scores = (
        softmax * (d_softmax - jnp.sum(softmax * d_softmax, axis=-1, keepdims=True)) * attn_scale
    ).astype(jnp.bfloat16)
    d_queries = jnp.einsum("chlf,cfhe->clhe", d_scores, key_sel, preferred_element_type=jnp.float32)
    d_queries = d_queries.astype(jnp.bfloat16).reshape(groups_mp * cap_len, local_width)
    d_keys = jnp.einsum("chlf,clhe->cfhe", d_scores, query_four, preferred_element_type=jnp.float32)
    d_keys = d_keys.astype(jnp.bfloat16).reshape(groups_mp, frames, local_width)
    d_values = jnp.einsum(
        "chlf,clhe->cfhe", softmax_low, d_att_four, preferred_element_type=jnp.float32
    )
    d_values = d_values.astype(jnp.bfloat16).reshape(groups_mp, frames, local_width)
    owners = jnp.arange(groups_mp, dtype=jnp.int32)
    inverse_map = jnp.sum(jnp.where(chosen[:, None] == owners[None, :], owners[:, None], 0), axis=0)
    keys_flat = jnp.take(d_keys, inverse_map, axis=0).reshape(groups_mp * frames, local_width)
    values_flat = jnp.take(d_values, inverse_map, axis=0).reshape(groups_mp * frames, local_width)
    d_states = lax.psum_scatter(
        (transposed_dot(keys_flat, w_key) + transposed_dot(values_flat, w_value)).astype(
            jnp.bfloat16
        ),
        "mp",
        scatter_dimension=0,
        tiled=True,
    ).astype(jnp.float32)
    grad_audio = norm_backward(d_states, state_normed, state_inverse, enc_gain).astype(
        jnp.bfloat16
    )[None]
    query_full = lax.all_gather(query_trans, "mp", axis=0, tiled=True)
    query_grad_own = lax.all_to_all(
        d_queries.reshape(groups_mp, cap_len, local_width),
        "mp",
        split_axis=0,
        concat_axis=2,
        tiled=True,
    )[0]
    d_hidden = block_product(query_grad_own, query_full, groups_mp)
    grad_captions = norm_backward(d_hidden, caption_normed, caption_inverse, dec_gain).astype(
        jnp.bfloat16
    )
    wq_term = lax.dot_general(
        hidden_all, d_queries, (((0,), (0,)), ((), ())), preferred_element_type=jnp.float32
    )
    grad_wq = lax.psum_scatter(
        wq_term.astype(jnp.bfloat16), "dp", scatter_dimension=0, tiled=True
    ).astype(jnp.float32)
    return (cross_update, grad_captions, grad_audio, grad_wq, grad_wo)


def solution(mesh):
    in_specs = (
        P(("dp", "mp"), None),
        P(("dp", "mp"), None, None),
        P("dp"),
        P("dp", None),
        P(),
        P(),
        P(),
        P(),
        P(None, "mp"),
        P(None, "mp"),
        P(None, "mp"),
        P("mp", None),
        P(("dp", "mp"), None),
    )
    out_specs = (
        P(("dp", "mp"), None),
        P(("dp", "mp"), None),
        P(("dp", "mp"), None, None),
        P("dp", "mp"),
        P("mp", "dp"),
    )
    return jax.shard_map(body, mesh=mesh, in_specs=in_specs, out_specs=out_specs, check_vma=False)
```

profile of v0, /device:TPU:4, one launch (start us, length us, event | category | flops | bytes accessed | tf_op | source)
XLA Modules:
  0.0 989.9 jit_solution(7053975174476560256)
XLA Ops:
  9.4 1.6 fusion.56
  12.3 1.2 fusion.32
  13.5 2.0 fusion.27
  15.6 1.2 dynamic_slice.17
  17.5 1.8 broadcast_select_fusion
  20.7 35.4 %all-gather.6.cloned.1.call-done = bf16[16,32,1280]{2,1,0:T(8,128)(2,1)} async-done(((bf16[1,32,1280]{2,1,0:T(8,128)(2,1)}), bf16[16,32,1280]{2,1,0:T(8,128)(2,1)}) %all-gather.6.cloned.1.call-update) | async-done | bytes 1310736 | tf_op jit(solution)/shard_map/all_gather | solution.py:90
  56.1 1.8 convolution_convert_fusion.10
  59.2 47.0 %all-gather.8.cloned.1.call-done = bf16[2048,1280]{1,0:T(8,128)(2,1)} async-done(((bf16[128,1280]{1,0:T(8,128)(2,1)}), bf16[2048,1280]{1,0:T(8,128)(2,1)}) %all-gather.8.cloned.1.call-update) | async-done | bytes 5242896 | tf_op jit(solution)/shard_map/all_gather | solution.py:85
  106.2 4.2 fusion.16
  111.4 44.7 %all-gather.12.cloned.1.call-done = bf16[2048,1280]{1,0:T(8,128)(2,1)} async-done(((bf16[128,1280]{1,0:T(8,128)(2,1)}), bf16[2048,1280]{1,0:T(8,128)(2,1)}) %all-gather.12.cloned.1.call-update) | async-done | bytes 5242896 | tf_op jit(solution)/shard_map/all_gather | solution.py:86
  156.1 4.2 fusion.17
  160.5 1.3 fusion.19
  163.3 2.2 convolution_convert_fusion.6
  165.5 3.9 all-to-all-start.1
  172.8 4.8 convolution_convert_fusion.3
  177.6 5.5 convolution_convert_fusion.2
  183.2 2.0 fusion.87
  185.3 3.4 fusion.11
  188.6 5.8 all-to-all-start
  194.4 8.0 all-gather.14.cloned.1.call-done
  202.4 22.6 %while.23 = (s32[]{:T(128)}, f32[128,1280]{1,0:T(8,128)S(1)}, bf16[16,128,64]{1,2,0:T(8,128)(2,1)S(1)}, bf16[16,64,1280]{2,1,0:T(8,128)(2,1)}, s32[]{:T(128)}, /*index=5*/s32[]{:T(128)}) while((s32[]{:T(128)}, f32[128,1280]{1,0:T(8,128)S(1)}, bf16[16,128,64]{1,2,0:T(8,128)(2,1)S(1)}, bf16[16,64,1280]{2,1,0:T(8,128)(2,1)}, ...), condition=%wide.region_9.11_spmd.clone, body=%wide.region_8.10_spmd.clone.sunk | while | flops 21626880 | bytes 2147407 | solution.py:47
  225.0 22.4 %all-gather.10.cloned.1.call-done = bf16[1024,1280]{1,0:T(8,128)(2,1)} async-done(((bf16[64,1280]{1,0:T(8,128)(2,1)}), bf16[1024,1280]{1,0:T(8,128)(2,1)}) %all-gather.10.cloned.1.call-update) | async-done | bytes 2621456 | tf_op jit(solution)/shard_map/all_gather | solution.py:114
  247.5 22.7 %while.22 = (s32[]{:T(128)}, f32[128,1280]{1,0:T(8,128)S(1)}, bf16[16,128,64]{1,2,0:T(8,128)(2,1)S(1)}, bf16[16,64,1280]{2,1,0:T(8,128)(2,1)}, s32[]{:T(128)}, /*index=5*/s32[]{:T(128)}) while((s32[]{:T(128)}, f32[128,1280]{1,0:T(8,128)S(1)}, bf16[16,128,64]{1,2,0:T(8,128)(2,1)S(1)}, bf16[16,64,1280]{2,1,0:T(8,128)(2,1)}, ...), condition=%wide.region_6.8_spmd.clone, body=%wide.region_5.7_spmd.clone.sunk | while | flops 21626880 | bytes 2147407 | solution.py:47
  247.5 1.2 convolution_convert_fusion.13
  248.9 1.2 convolution_convert_fusion.13
  260.3 1.2 convolution_convert_fusion.13
  272.2 307.3 %reduce-scatter.10.cloned.1.call-done = bf16[40,64]{1,0:T(8,128)(2,1)} async-done(((bf16[1280,64]{1,0:T(8,128)(2,1)}), bf16[40,64]{1,0:T(8,128)(2,1)}) %reduce-scatter.10.cloned.1.call-update) | async-done | bytes 5136
  579.5 1.3 convert_element_type.137
  580.8 329.2 %reduce-scatter.12.cloned.1.call-done = bf16[64,40]{0,1:T(8,128)(2,1)} async-done(((bf16[64,1280]{0,1:T(8,128)(2,1)}), bf16[64,40]{0,1:T(8,128)(2,1)}) %reduce-scatter.12.cloned.1.call-update) | async-done | bytes 5136
  910.0 1.3 convert_element_type.139
  911.4 69.0 %reduce-scatter.8.cloned.1.call-done = bf16[32,1280]{1,0:T(8,128)(2,1)} async-done(((bf16[512,1280]{1,0:T(8,128)(2,1)}), bf16[32,1280]{1,0:T(8,128)(2,1)}) %reduce-scatter.8.cloned.1.call-update) | async-done | bytes 81936 | tf_op jit(solution)/shard_map/reduce_scatter | solution.py:149
  981.5 1.6 fusion.72
  (133 shorter events, 56.7 us)
Async XLA Ops:
  7.2 13.3 %copy-start.8 = (s32[1,16]{1,0:T(1,128)S(1)}, s32[1,16]{1,0:T(1,128)}, u32[]{:S(2)}) copy-start(s32[1,16]{1,0:T(1,128)} %param.22) | copy-start | bytes 196
  7.2 48.9 %copy-start.4 = (bf16[1280,64]{0,1:T(8,128)(2,1)S(1)}, bf16[1280,64]{0,1:T(8,128)(2,1)}, u32[]{:S(2)}) copy-start(bf16[1280,64]{0,1:T(8,128)(2,1)} %param.28) | copy-start | bytes 491524
  7.2 48.9 %copy-start.5 = (bf16[1280,64]{0,1:T(8,128)(2,1)S(1)}, bf16[1280,64]{0,1:T(8,128)(2,1)}, u32[]{:S(2)}) copy-start(bf16[1280,64]{0,1:T(8,128)(2,1)} %param.29) | copy-start | bytes 491524
  7.2 48.9 %all-gather.6.cloned.1.call-start = ((), (), s32[]{:S(2)}) async-start(), calls=%async_computation.5 | async-start | bytes 1392640 | tf_op jit(solution)/shard_map/all_gather | solution.py:90
  11.1 95.0 %all-gather.8.cloned.1.call-start = ((), (), s32[]{:S(2)}) async-start(), calls=%async_computation.6 | async-start | bytes 5570560 | tf_op jit(solution)/shard_map/all_gather | solution.py:85
  13.5 92.7 %copy-start.2 = (bf16[1280,64]{0,1:T(8,128)(2,1)S(1)}, bf16[1280,64]{0,1:T(8,128)(2,1)}, u32[]{:S(2)}) copy-start(bf16[1280,64]{0,1:T(8,128)(2,1)} %param.27) | copy-start | bytes 491524
  15.5 140.5 %all-gather.12.cloned.1.call-start = ((), (), s32[]{:S(2)}) async-start(), calls=%async_computation.8 | async-start | bytes 5570560 | tf_op jit(solution)/shard_map/all_gather | solution.py:86
  19.3 183.1 %all-gather.14.cloned.1.call-start = ((), (), s32[]{:S(2)}) async-start(), calls=%async_computation.9 | async-start | bytes 2785280 | tf_op jit(solution)/shard_map/all_gather | solution.py:160
  19.9 227.6 %all-gather.10.cloned.1.call-start = ((), (), s32[]{:S(2)}) async-start(), calls=%async_computation.7 | async-start | bytes 2785280 | tf_op jit(solution)/shard_map/all_gather | solution.py:114
  59.2 96.9 %copy-start.3 = (bf16[64,1280]{1,0:T(8,128)(2,1)S(1)}, bf16[64,1280]{1,0:T(8,128)(2,1)}, u32[]{:S(2)}) copy-start(bf16[64,1280]{1,0:T(8,128)(2,1)} %param.30) | copy-start | bytes 491524
  165.5 23.2 %all-to-all-start.1 = ((bf16[16,128,64]{1,2,0:T(8,128)(2,1)}), bf16[16,128,64]{1,2,0:T(8,128)(2,1)S(1)}, u32[]{:S(2)}, u32[]{:S(2)}) async-start(bf16[16,128,64]{1,2,0:T(8,128)(2,1)} %bitcast.11), calls=%async_computation.1 | async-start | bytes 524288 | tf_op jit(solution)/shard_map/all_to_all | solution.py:161
  169.4 410.1 %reduce-scatter.10.cloned.1.call-start = ((), (), s32[]{:S(2)}) async-start(), calls=%async_computation.11 | async-start | bytes 337920
  177.6 732.4 %reduce-scatter.12.cloned.1.call-start = ((), (), s32[]{:S(2)}) async-start(), calls=%async_computation.12 | async-start | bytes 337920
  185.2 795.1 %reduce-scatter.8.cloned.1.call-start = ((), (), s32[]{:S(2)}) async-start(), calls=%async_computation.10 | async-start | bytes 1392640 | tf_op jit(solution)/shard_map/reduce_scatter | solution.py:149
  188.6 58.8 %all-to-all-start = ((bf16[16,128,64]{1,2,0:T(8,128)(2,1)}), bf16[16,128,64]{1,2,0:T(8,128)(2,1)S(1)}, u32[]{:S(2)}, u32[]{:S(2)}) async-start(bf16[16,128,64]{1,2,0:T(8,128)(2,1)} %bitcast.6), calls=%async_computation | async-start | bytes 524288 | tf_op jit(solution)/shard_map/all_to_all | solution.py:115
  247.4 23.5 %copy-start = (bf16[128,1280]{1,0:T(8,128)(2,1)S(1)}, bf16[128,1280]{1,0:T(8,128)(2,1)}, u32[]{:S(2)}) copy-start(bf16[128,1280]{1,0:T(8,128)(2,1)} %param.19) | copy-start | bytes 983044
  247.4 23.5 %copy-start.6 = (f32[1280]{0:T(1024)S(1)}, f32[1280]{0:T(1024)}, u32[]{:S(2)}) copy-start(f32[1280]{0:T(1024)} %param.25) | copy-start | bytes 15364
  270.2 710.2 %copy-start.1 = (bf16[1,32,1280]{2,1,0:T(8,128)(2,1)S(1)}, bf16[1,32,1280]{2,1,0:T(8,128)(2,1)}, u32[]{:S(2)}) copy-start(bf16[1,32,1280]{2,1,0:T(8,128)(2,1)} %param.20) | copy-start | bytes 245764
  270.2 710.2 %copy-start.7 = (f32[1280]{0:T(1024)S(1)}, f32[1280]{0:T(1024)}, u32[]{:S(2)}) copy-start(f32[1280]{0:T(1024)} %param.23) | copy-start | bytes 15364
Sparse Core Ops, SparseCore 0:
  11.2 44.7 all-gather.5
  58.8 47.3 all-gather.7
  108.9 47.1 all-gather.11
  158.1 44.2 all-gather.13
  204.4 43.0 all-gather.9
  251.5 327.9 reduce-scatter.9
  584.2 325.7 reduce-scatter.11
  912.9 67.4 reduce-scatter.7
where the time goes:
time: 992 us; the launch traced here: 990 us
  waiting for transfers between devices  864 us (87%)
  matrix products  69.2 us (7%)
  other arithmetic  25.1 us (3%)
  between operations  14.4 us (1%)
  starting transfers between devices  9.98 us (1%)
    unnamed x10, waiting for transfers between devices  638 us
    reduce_scatter x1, waiting for transfers between devices, body(): lax.psum_scatter((transposed_dot(keys_flat, w_key) + transposed_dot(value...  69 us
    all_gather x1, waiting for transfers between devices, body(): lax.all_gather(hidden_own, 'mp', axis=0, tiled=True)  47 us
    all_gather x1, waiting for transfers between devices, body(): lax.all_gather(upstream_own, 'mp', axis=0, tiled=True)  44.7 us
    dot_general x32, matrix products, add_block(): jnp.dot(pieces[0], pieces[1], preferred_element_type=jnp.float32)  38.1 us
    all_gather x1, waiting for transfers between devices, body(): shard_rows = lax.all_gather(states[None], 'mp', axis=0, tiled=True)  35.4 us
    all_gather x1, waiting for transfers between devices, body(): out_full = lax.all_gather(w_out, 'mp', axis=0, tiled=True)  22.4 us
  transfers between devices with their start and end apart: 10, of which 8 were waited for; matrix products, arithmetic and copies ran while one was open for 9% of the time, Pallas kernels for 0%

commit v1 on v0

v1 whole, which is shorter than its diff:
```python
import functools
import math

import jax
import jax.numpy as jnp
from jax import lax
from jax.experimental import pallas as pl
from jax.experimental.pallas import tpu as pltpu
from jax.sharding import PartitionSpec as P

HEAD_DIM = 64
EPSILON = 1e-05
FRAMES = 32
CAP = 128
HELD = 4
ROWS = HELD * CAP
WIDTH = HELD * HEAD_DIM
BF16 = jnp.bfloat16
F32 = jnp.float32
LARGEST_BF16 = 3.3895313892515355e38

VMEM = pl.BlockSpec(memory_space=pltpu.VMEM)
SMEM = pl.BlockSpec(memory_space=pltpu.SMEM)
MIB = 1 << 20


def params(mib):
    return pltpu.CompilerParams(vmem_limit_bytes=mib * MIB)


def dot(left, right, left_dim=1, right_dim=0):
    return lax.dot_general(
        left, right, (((left_dim,), (right_dim,)), ((), ())), preferred_element_type=F32
    )


def standardize(values):
    row_mean = jnp.mean(values, axis=-1, keepdims=True)
    centred = values - row_mean
    inverse_std = lax.rsqrt(jnp.mean(centred * centred, axis=-1, keepdims=True) + EPSILON)
    return centred * inverse_std, inverse_std


def norm_backward(upstream, normed, inverse_std, gain_vec):
    scaled = upstream * gain_vec
    mean_term = jnp.mean(scaled, axis=-1, keepdims=True)
    cross_term = jnp.mean(scaled * normed, axis=-1, keepdims=True)
    return inverse_std * (scaled - mean_term - normed * cross_term)


def held_caption(own, part):
    return own ^ ((part & 1) * 8) ^ (part >> 1)


def pack_kernel(wq_ref, wk_ref, wv_ref, wo_ref, out_ref):
    for kind, block in enumerate((wq_ref[...].T, wk_ref[...].T, wv_ref[...].T, wo_ref[...])):
        for target in range(out_ref.shape[0]):
            out_ref[target, kind * HEAD_DIM : (kind + 1) * HEAD_DIM, :] = block


def weight_of(w_ref, kind):
    rows = w_ref[:, kind * HEAD_DIM : (kind + 1) * HEAD_DIM, :]
    return rows.reshape(WIDTH, w_ref.shape[2])


def project_kernel(own_ref, len_ref, t0, t1, t2, t3, gain, bias, w_ref, hid_ref, up_ref, q_ref, da_ref):
    own = own_ref[0]
    positions = lax.broadcasted_iota(jnp.int32, (CAP, 1), 0)
    for part, tokens in enumerate((t0, t1, t2, t3)):
        span = slice(part * CAP, (part + 1) * CAP)
        normed, _ = standardize(tokens[0].astype(F32))
        hid_ref[span, :] = (normed * gain[...] + bias[...]).astype(BF16)
        live = positions < len_ref[held_caption(own, part)]
        up_ref[span, :] = jnp.where(live, tokens[1].astype(F32), 0.0).astype(BF16)
    q_ref[...] = dot(hid_ref[...], weight_of(w_ref, 0), 1, 1).astype(BF16)
    da_ref[...] = dot(up_ref[...], weight_of(w_ref, 3), 1, 1).astype(BF16)


def segment_sum(values, ones):
    high = jnp.minimum(values, LARGEST_BF16).astype(BF16)
    low = (values - high.astype(F32)).astype(BF16)
    return dot(high, ones) + dot(low, ones)


def attend_kernel(
    own_ref, pair_ref, audio_ref, gain, bias, w_ref, q_ref, da_ref, att_ref, dq_ref, ds_ref, st_ref, dk_ref, dv_ref
):
    own = own_ref[0]
    scale = 1.0 / math.sqrt(HEAD_DIM)
    for part in range(HELD):
        clip = pair_ref[0, held_caption(own, part)]
        normed, _ = standardize(audio_ref[clip].astype(F32))
        st_ref[part * FRAMES : (part + 1) * FRAMES, :] = (normed * gain[...] + bias[...]).astype(BF16)
    keys = dot(st_ref[...], weight_of(w_ref, 1), 1, 1).astype(BF16)
    values = dot(st_ref[...], weight_of(w_ref, 2), 1, 1).astype(BF16)
    pairs = HELD * FRAMES
    row_head = lax.broadcasted_iota(jnp.int32, (pairs, WIDTH), 0) // FRAMES
    lane_head = lax.broadcasted_iota(jnp.int32, (pairs, WIDTH), 1) // HEAD_DIM
    same = row_head == lane_head
    first = lax.broadcasted_iota(jnp.int32, (pairs, pairs), 0) // FRAMES
    second = lax.broadcasted_iota(jnp.int32, (pairs, pairs), 1) // FRAMES
    ones = jnp.where(first == second, 1.0, 0.0).astype(BF16)

    def spread(rows):
        repeated = jnp.concatenate([rows.astype(F32)] * HELD, axis=0)
        return jnp.where(same, repeated, 0.0).astype(BF16)

    def gather(rows):
        kept = jnp.where(same, rows, 0.0)
        total = kept[0:FRAMES]
        for head in range(1, HELD):
            total = total + kept[head * FRAMES : (head + 1) * FRAMES]
        return total.astype(BF16)

    for part in range(HELD):
        span = slice(part * CAP, (part + 1) * CAP)
        frames = slice(part * FRAMES, (part + 1) * FRAMES)
        key_block = spread(keys[frames])
        value_block = spread(values[frames])
        query = q_ref[span, :]
        d_att = da_ref[span, :]
        weights = jnp.exp(dot(query, key_block, 1, 1) * scale)
        softmax = weights / segment_sum(weights, ones)
        low = softmax.astype(BF16)
        att_ref[span, :] = dot(low, value_block).astype(BF16)
        d_softmax = dot(d_att, value_block, 1, 1)
        inner = segment_sum(softmax * d_softmax, ones)
        d_scores = (softmax * (d_softmax - inner) * scale).astype(BF16)
        dq_ref[span, :] = dot(d_scores, key_block).astype(BF16)
        dk_ref[frames, :] = gather(dot(d_scores, query, 0, 0))
        dv_ref[frames, :] = gather(dot(low, d_att, 0, 0))
    ds_ref[...] = (
        dot(dk_ref[...], weight_of(w_ref, 1)) + dot(dv_ref[...], weight_of(w_ref, 2))
    ).astype(BF16)


def update_kernel(w_ref, att_ref, dq_ref, keep_ref, send_ref):
    w_out = weight_of(w_ref, 3)
    w_query = weight_of(w_ref, 0)
    for part in range(HELD):
        span = slice(part * CAP, (part + 1) * CAP)
        target = send_ref if part >> 1 else keep_ref
        target[part & 1, 0] = dot(att_ref[span, :], w_out).astype(BF16)
        target[part & 1, 1] = dot(dq_ref[span, :], w_query).astype(BF16)


def weight_grad_kernel(hid_ref, up_ref, att_ref, dq_ref, grad_ref):
    half = hid_ref.shape[1] // 2
    for kind, (left, right) in enumerate(((dq_ref, hid_ref), (att_ref, up_ref))):
        product = dot(left[...], right[...], 0, 0).astype(BF16)
        for side in range(2):
            for head in range(HELD):
                grad_ref[side * HELD + head, kind * HEAD_DIM : (kind + 1) * HEAD_DIM, :] = product[
                    head * HEAD_DIM : (head + 1) * HEAD_DIM, side * half : (side + 1) * half
                ]


def grad_sum_kernel(parts_ref, out_ref):
    total = parts_ref[0].astype(F32)
    for part in range(1, parts_ref.shape[0]):
        total = total + parts_ref[part].astype(F32)
    out_ref[...] = total.T.astype(BF16)


def grad_final_kernel(parts_ref, wq_ref, wo_ref):
    total = parts_ref[0].astype(F32)
    for part in range(1, parts_ref.shape[0]):
        total = total + parts_ref[part].astype(F32)
    wq_ref[...] = total[:, :HEAD_DIM]
    wo_ref[...] = total[:, HEAD_DIM:].T


def caption_final_kernel(keep_ref, core_ref, x_ref, caption_ref, gain, update_ref, grad_ref):
    def total(kind):
        near = keep_ref[0, kind].astype(F32) + core_ref[0, kind].astype(F32)
        return near + x_ref[kind].astype(F32)

    update_ref[...] = total(0).astype(BF16)
    normed, inverse_std = standardize(caption_ref[...].astype(F32))
    grad_ref[...] = norm_backward(total(1), normed, inverse_std, gain[...]).astype(BF16)


def audio_final_kernel(own_ref, pair_ref, p0, p1, p2, p3, audio_ref, gain, out_ref):
    del own_ref, pair_ref
    total = (p0[0].astype(F32) + p1[0].astype(F32)) + (p2[0].astype(F32) + p3[0].astype(F32))
    normed, inverse_std = standardize(audio_ref[0].astype(F32))
    out_ref[0] = norm_backward(total, normed, inverse_std, gain[...]).astype(BF16)


def describing_block(part, step, own_ref, pair_ref):
    del step
    caption = 0
    for index in range(pair_ref.shape[1]):
        caption = jnp.where(pair_ref[0, index] == own_ref[0], index, caption)
    return held_caption(caption, part) * HELD + part, 0, 0


def body(
    captions,
    audio,
    caption_len,
    pairing,
    enc_gain,
    enc_bias,
    dec_gain,
    dec_bias,
    w_query,
    w_key,
    w_value,
    w_out,
    grad_update,
    *,
    depth,
    y_groups,
    yx_groups,
    z_groups,
):
    both = ("dp", "mp")
    width = captions.shape[1]
    shape = jax.ShapeDtypeStruct
    own = lax.axis_index("mp").astype(jnp.int32).reshape(1)
    enc_gain, enc_bias, dec_gain, dec_bias = (
        vector.reshape(1, width) for vector in (enc_gain, enc_bias, dec_gain, dec_bias)
    )
    swap_core = [(index, index ^ 1) for index in range(16)]
    swap_x = [(index, index ^ 8) for index in range(16)]

    audio_all = lax.all_gather(audio, "mp", axis=0, tiled=True)
    tokens_own = jnp.stack([captions, grad_update])
    tokens_x = lax.ppermute(tokens_own, "mp", swap_x)
    tokens_core = lax.ppermute(tokens_own, "mp", swap_core)
    tokens_far = lax.ppermute(tokens_x, "mp", swap_core)

    packed = pl.pallas_call(
        pack_kernel,
        out_shape=shape((HELD, 4 * HEAD_DIM, width), BF16),
        in_specs=[VMEM] * 4,
        out_specs=VMEM,
        compiler_params=params(16),
        name="pack_weights",
    )(w_query, w_key, w_value, w_out)
    weights = lax.all_to_all(packed, "mp", 0, 0, axis_index_groups=y_groups, tiled=True)

    hidden, upstream, queries, d_attended = pl.pallas_call(
        project_kernel,
        out_shape=(
            shape((ROWS, width), BF16),
            shape((ROWS, width), BF16),
            shape((ROWS, WIDTH), BF16),
            shape((ROWS, WIDTH), BF16),
        ),
        in_specs=[SMEM, SMEM] + [VMEM] * 7,
        out_specs=(VMEM,) * 4,
        compiler_params=params(32),
        name="project",
    )(own, caption_len, tokens_own, tokens_x, tokens_core, tokens_far, dec_gain, dec_bias, weights)

    attended, d_queries, d_states = pl.pallas_call(
        attend_kernel,
        out_shape=(
            shape((ROWS, WIDTH), BF16),
            shape((ROWS, WIDTH), BF16),
            shape((HELD * FRAMES, width), BF16),
        ),
        in_specs=[SMEM, SMEM] + [VMEM] * 6,
        out_specs=(VMEM,) * 3,
        scratch_shapes=[
            pltpu.VMEM((HELD * FRAMES, width), BF16),
            pltpu.VMEM((HELD * FRAMES, WIDTH), BF16),
            pltpu.VMEM((HELD * FRAMES, WIDTH), BF16),
        ],
        compiler_params=params(32),
        name="attend",
    )(own, pairing, audio_all, enc_gain, enc_bias, weights, queries, d_attended)

    states_all = lax.all_gather(d_states, "mp", axis=0, tiled=True)

    weight_parts = pl.pallas_call(
        weight_grad_kernel,
        out_shape=shape((2 * HELD, 2 * HEAD_DIM, width // 2), BF16),
        in_specs=[VMEM] * 4,
        out_specs=VMEM,
        compiler_params=params(32),
        name="weight_grads",
    )(hidden, upstream, attended, d_queries)
    weight_parts = lax.all_to_all(
        weight_parts, both, 0, 0, axis_index_groups=yx_groups, tiled=True
    )

    keep, send = pl.pallas_call(
        update_kernel,
        out_shape=(shape((2, 2, CAP, width), BF16),) * 2,
        in_specs=[VMEM] * 3,
        out_specs=(VMEM,) * 2,
        compiler_params=params(32),
        name="updates",
    )(weights, attended, d_queries)
    core_parts = lax.ppermute(send, "mp", swap_core)
    x_send = (keep[1].astype(F32) + core_parts[1].astype(F32)).astype(BF16)
    x_parts = lax.ppermute(x_send, "mp", swap_x)

    weight_half = pl.pallas_call(
        grad_sum_kernel,
        out_shape=shape((width // 2, 2 * HEAD_DIM), BF16),
        in_specs=[VMEM],
        out_specs=VMEM,
        compiler_params=params(16),
        name="sum_weight_grads",
    )(weight_parts)
    weight_last = lax.all_to_all(
        weight_half.reshape(depth, width // (2 * depth), 2 * HEAD_DIM),
        both,
        0,
        0,
        axis_index_groups=z_groups,
        tiled=True,
    )
    grad_wq, grad_wo = pl.pallas_call(
        grad_final_kernel,
        out_shape=(
            shape((width // (2 * depth), HEAD_DIM), F32),
            shape((HEAD_DIM, width // (2 * depth)), F32),
        ),
        in_specs=[VMEM],
        out_specs=(VMEM,) * 2,
        compiler_params=params(16),
        name="final_weight_grads",
    )(weight_last)

    near = pl.BlockSpec((1, 2, CAP, width), lambda step: (0, 0, 0, 0))
    cross_update, grad_captions = pl.pallas_call(
        caption_final_kernel,
        grid=(1,),
        out_shape=(shape((CAP, width), BF16),) * 2,
        in_specs=[
            near,
            near,
            pl.BlockSpec((2, CAP, width), lambda step: (0, 0, 0)),
            pl.BlockSpec((CAP, width), lambda step: (0, 0)),
            pl.BlockSpec((1, width), lambda step: (0, 0)),
        ],
        out_specs=(pl.BlockSpec((CAP, width), lambda step: (0, 0)),) * 2,
        compiler_params=params(16),
        name="final_captions",
    )(keep, core_parts, x_parts, captions, dec_gain)

    state_blocks = states_all.reshape(-1, FRAMES, width)
    grad_audio = pl.pallas_call(
        audio_final_kernel,
        grid_spec=pltpu.PrefetchScalarGridSpec(
            num_scalar_prefetch=2,
            grid=(1,),
            in_specs=[
                pl.BlockSpec((1, FRAMES, width), functools.partial(describing_block, part))
                for part in range(HELD)
            ]
            + [
                pl.BlockSpec((1, FRAMES, width), lambda step, own_ref, pair_ref: (0, 0, 0)),
                pl.BlockSpec((1, width), lambda step, own_ref, pair_ref: (0, 0)),
            ],
            out_specs=pl.BlockSpec((1, FRAMES, width), lambda step, own_ref, pair_ref: (0, 0, 0)),
        ),
        out_shape=shape((1, FRAMES, width), BF16),
        compiler_params=params(16),
        name="final_audio",
    )(own, pairing, *([state_blocks] * HELD), audio, enc_gain)

    return (cross_update, grad_captions, grad_audio, grad_wq, grad_wo)


def device_groups(dp_size):
    depth = dp_size // 2

    def device(x_hi, z, x_lo, y, core):
        return (x_hi * depth + z) * 16 + (x_lo * 4 + y) * 2 + core

    y_groups = [[(x * 4 + y) * 2 + core for y in range(4)] for x in range(2) for core in range(2)]
    yx_groups = [
        [device(x_hi, z, x_lo, y, core) for x_hi in range(2) for y in range(4)]
        for z in range(depth)
        for x_lo in range(2)
        for core in range(2)
    ]
    z_groups = [
        [device(x_hi, z, x_lo, y, core) for z in range(depth)]
        for x_hi in range(2)
        for x_lo in range(2)
        for y in range(4)
        for core in range(2)
    ]
    return dict(depth=depth, y_groups=y_groups, yx_groups=yx_groups, z_groups=z_groups)


def solution(mesh):
    in_specs = (
        P(("dp", "mp"), None),
        P(("dp", "mp"), None, None),
        P("dp"),
        P("dp", None),
        P(),
        P(),
        P(),
        P(),
        P(None, "mp"),
        P(None, "mp"),
        P(None, "mp"),
        P("mp", None),
        P(("dp", "mp"), None),
    )
    out_specs = (
        P(("dp", "mp"), None),
        P(("dp", "mp"), None),
        P(("dp", "mp"), None, None),
        P("dp", "mp"),
        P("mp", "dp"),
    )
    local = functools.partial(body, **device_groups(mesh.shape["dp"]))
    return jax.shard_map(local, mesh=mesh, in_specs=in_specs, out_specs=out_specs, check_vma=False)
```

time: 992 us -> 157 us (0.16)
  the two profiles are of different devices: /device:TPU:4 before, /device:TPU:32 now
where the time goes in v1:
time: 157 us; the launch traced here: 156 us
  waiting for transfers between devices  50.3 us (32%)
  blocking collectives  31.2 us (20%)
  starting transfers between devices  21.3 us (14%)
  local copies, waits for them, and re-layouts  18.2 us (12%)
  Pallas kernels  17.6 us (11%)
  between operations  14.3 us (9%)
  other arithmetic  3.24 us (2%)
    all_to_all x1, blocking collectives, body(): lax.all_to_all(weight_half.reshape(depth, width // (2 * depth), 2 * HEAD_...  31.2 us
    all_to_all x1, waiting for transfers between devices, body(): lax.all_to_all(weight_parts, both, 0, 0, axis_index_groups=yx_groups, til...  22.3 us
    unnamed x48, local copies, waits for them, and re-layouts  17 us
    ppermute x1, waiting for transfers between devices, body(): tokens_x = lax.ppermute(tokens_own, 'mp', swap_x)  14.6 us
    all_to_all x1, waiting for transfers between devices, body(): lax.all_to_all(packed, 'mp', 0, 0, axis_index_groups=y_groups, tiled=True)  11.5 us
    pallas_call x1, Pallas kernels, body(): pl.pallas_call(attend_kernel, out_shape=(shape((ROWS, WIDTH), BF16), shap...  5.16 us
    all_to_all x1, starting transfers between devices, body(): lax.all_to_all(weight_parts, both, 0, 0, axis_index_groups=yx_groups, til...  5.08 us
    all_to_all x1, starting transfers between devices, body(): lax.all_to_all(packed, 'mp', 0, 0, axis_index_groups=y_groups, tiled=True)  4.46 us
  transfers between devices with their start and end apart: 9, of which 4 were waited for; matrix products, arithmetic and copies ran while one was open for 5% of the time, Pallas kernels for 7%

profile of v1, /device:TPU:32, one launch (start us, length us, event | category | flops | bytes accessed | tf_op | source)
XLA Modules:
  0.0 156.1 jit_solution(14936871094114589464)
XLA Ops:
  7.9 1.1 copy.22.wq_ref
  9.0 1.1 copy.23.wk_ref
  10.2 1.1 copy.24.wv_ref
  11.7 1.5 copy-done.1
  13.1 4.5 %all-to-all-start = ((bf16[4,256,1280]{2,1,0:T(8,128)(2,1)}), bf16[4,256,1280]{2,1,0:T(8,128)(2,1)S(1)}, u32[]{:S(2)}, u32[]{:S(2)}) async-start(bf16[4,256,1280]{2,1,0:T(8,128)(2,1)} %copy-done.1), calls=%async_computation | async-start | bytes 5242880 | tf_op jit(solution)/shard_map/all_to_all | solution.py:242
  17.7 1.1 pad_maximum_fusion.t0
  18.8 3.4 %collective-permute-start = (bf16[2,128,1280]{2,1,0:T(8,128)(2,1)S(1)}, bf16[2,128,1280]{2,1,0:T(8,128)(2,1)}, u32[]{:S(2)}, u32[]{:S(2)}) collective-permute-start(bf16[2,128,1280]{2,1,0:T(8,128)(2,1)S(1)} %pad_maximum_fusion.t0), channel_id=1, source_target_pairs={{0,8},{1,9},{2,10},{3,11},{4,12},{5,13},{6,14},{7,15},{8,0},{9,1},... | collective-permute-start | bytes 1966088 | tf_op jit(solution)/shard_map/ppermute | solution.py:230
  22.2 1.9 %collective-permute-start.1 = (bf16[2,128,1280]{2,1,0:T(8,128)(2,1)S(1)}, bf16[2,128,1280]{2,1,0:T(8,128)(2,1)}, u32[]{:S(2)}, u32[]{:S(2)}) collective-permute-start(bf16[2,128,1280]{2,1,0:T(8,128)(2,1)S(1)} %pad_maximum_fusion.t0), channel_id=1, source_target_pairs={{0,1},{1,0},{2,3},{3,2},{4,5},{5,4},{6,7},{7,6},{8,9},{9,8},{10,11... | collective-permute-start | bytes 1966088 | tf_op jit(solution)/shard_map/ppermute | solution.py:231
  24.1 14.6 %collective-permute-done.t1 = bf16[2,128,1280]{2,1,0:T(8,128)(2,1)} collective-permute-done((bf16[2,128,1280]{2,1,0:T(8,128)(2,1)S(1)}, bf16[2,128,1280]{2,1,0:T(8,128)(2,1)}, u32[]{:S(2)}, u32[]{:S(2)}) %collective-permute-start) | collective-permute-done | bytes 655392 | tf_op jit(solution)/shard_map/ppermute | solution.py:230
  38.7 1.9 %collective-permute-start.2 = (bf16[2,128,1280]{2,1,0:T(8,128)(2,1)}, bf16[2,128,1280]{2,1,0:T(8,128)(2,1)}, u32[]{:S(2)}, u32[]{:S(2)}) collective-permute-start(bf16[2,128,1280]{2,1,0:T(8,128)(2,1)} %collective-permute-done.t1), channel_id=1, source_target_pairs={{0,1},{1,0},{2,3},{3,2},{4,5},{5,4},{6,7},{7,6},{8,9},{9,8},{10,11... | collective-permute-start | bytes 1966088 | tf_op jit(solution)/shard_map/ppermute | solution.py:232
  41.9 1.2 collective-permute-done.2.t3
  43.1 11.5 %all-to-all-done.w_ref = bf16[4,256,1280]{2,1,0:T(8,128)(2,1)S(1)} async-done(((bf16[4,256,1280]{2,1,0:T(8,128)(2,1)}), bf16[4,256,1280]{2,1,0:T(8,128)(2,1)S(1)}, u32[]{:S(2)}, u32[]{:S(2)}) %all-to-all-start) | async-done | bytes 2621472 | tf_op jit(solution)/shard_map/all_to_all | solution.py:242
  54.6 0.7 copy-done.15
  55.9 3.1 %project.1 = (bf16[512,1280]{1,0:T(8,128)(2,1)S(1)}, bf16[512,1280]{1,0:T(8,128)(2,1)S(1)}, bf16[512,256]{1,0:T(8,128)(2,1)S(1)}, bf16[512,256]{1,0:T(8,128)(2,1)S(1)}) custom-call(s32[1]{0:T(128)} %bitcast.own_ref, s32[16]{0:T(128)S(1)} %copy-done.17, bf16[2,128,1280]{2,1,0:T(8,128)(2,1)S(1)} %pad_maximum_fusion.t0, ...), custom_call_target="tpu_custom_call" | custom-call | tf_op jit(solution)/shard_map/project/pallas_call | solution.py:244
  59.1 1.1 copy-done.6
  60.1 1.2 copy-done.8
  61.3 0.7 copy-done.11
  62.0 1.3 copy-done.5
  63.3 0.9 copy-done.12
  65.6 5.2 %attend.1 = (bf16[512,256]{1,0:T(8,128)(2,1)S(1)}, bf16[512,256]{1,0:T(8,128)(2,1)S(1)}, bf16[128,1280]{1,0:T(8,128)(2,1)}) custom-call(s32[1]{0:T(128)} %bitcast.own_ref, s32[1,16]{1,0:T(1,128)S(1)} %copy-done.16, bf16[16,32,1280]{2,1,0:T(8,128)(2,1)S(1)} %copy-done.5, f32[1,1280]{1,0:T(1,128)S(1)} %reshape.36.gain, f32[1,1280]{1,0:T(1,128)S(1)} %copy-done.14, ...), custom_call_target="tpu_custom_call" | custom-call | tf_op jit(solution)/shard_map/attend/pallas_call | solution.py:258
  70.8 1.9 %updates.1 = (bf16[2,2,128,1280]{3,2,1,0:T(8,128)(2,1)S(1)}, bf16[2,2,128,1280]{3,2,1,0:T(8,128)(2,1)}) custom-call(bf16[4,256,1280]{2,1,0:T(8,128)(2,1)S(1)} %all-to-all-done.w_ref, bf16[512,256]{1,0:T(8,128)(2,1)S(1)} %get-tuple-element.20.att_ref, bf16[512,256]{1,0:T(8,128)(2,1)S(1)} %get-tuple-element.21.dq_ref), custom_call_target="tpu_custom_call" | custom-call | tf_op jit(solution)/shard_map/updates/pallas_call | solution.py:290
  72.8 1.0 copy-done.2
  73.8 1.9 %collective-permute-start.3 = (bf16[2,2,128,1280]{3,2,1,0:T(8,128)(2,1)}, bf16[2,2,128,1280]{3,2,1,0:T(8,128)(2,1)}, u32[]{:S(2)}, u32[]{:S(2)}) collective-permute-start(bf16[2,2,128,1280]{3,2,1,0:T(8,128)(2,1)} %get-tuple-element.23), channel_id=1, source_target_pairs={{0,1},{1,0},{2,3},{3,2},{4,5},{5,4},{6,7},{7,6},{8,9},{9,8},{10,11... | collective-permute-start | bytes 3932168 | tf_op jit(solution)/shard_map/ppermute | solution.py:298
  75.7 2.0 %weight_grads.1 = bf16[8,128,640]{2,1,0:T(8,128)(2,1)} custom-call(bf16[512,1280]{1,0:T(8,128)(2,1)S(1)} %copy-done.7, bf16[512,1280]{1,0:T(8,128)(2,1)S(1)} %copy-done.9, bf16[512,256]{1,0:T(8,128)(2,1)S(1)} %get-tuple-element.20.att_ref, bf16[512,256]{1,0:T(8,128)(2,1)S(1)} %get-tuple-element.21.dq_ref), custom_call_target="tpu_custom_call" | custom-call | tf_op jit(solution)/shard_map/weight_grads/pallas_call | solution.py:278
  77.7 5.1 %all-to-all-start.1 = ((bf16[8,128,640]{2,1,0:T(8,128)(2,1)}), bf16[8,128,640]{2,1,0:T(8,128)(2,1)S(1)}, u32[]{:S(2)}, u32[]{:S(2)}) async-start(bf16[8,128,640]{2,1,0:T(8,128)(2,1)} %weight_grads.1), calls=%async_computation.1 | async-start | bytes 2621440 | tf_op jit(solution)/shard_map/all_to_all | solution.py:286
  82.8 2.1 %fusion = bf16[2,128,1280]{2,1,0:T(8,128)(2,1)} fusion(bf16[2,2,128,1280]{3,2,1,0:T(8,128)(2,1)} %collective-permute-done.3.core_ref, bf16[2,2,128,1280]{3,2,1,0:T(8,128)(2,1)S(1)} %copy-done.3), kind=kLoop, calls=%fused_computation.1 | loop fusion | flops 1310720 | bytes 1966080 | tf_op jit(solution)/shard_map/convert_element_type | solution.py:299
  84.9 2.6 %collective-permute-start.4 = (bf16[2,128,1280]{2,1,0:T(8,128)(2,1)}, bf16[2,128,1280]{2,1,0:T(8,128)(2,1)}, u32[]{:S(2)}, u32[]{:S(2)}) collective-permute-start(bf16[2,128,1280]{2,1,0:T(8,128)(2,1)} %fusion), channel_id=1, source_target_pairs={{0,8},{1,9},{2,10},{3,11},{4,12},{5,13},{6,14},{7,15},{8,0},{9,1},... | collective-permute-start | bytes 1966088 | tf_op jit(solution)/shard_map/ppermute | solution.py:300
  87.5 22.3 %all-to-all-done.1.parts_ref = bf16[8,128,640]{2,1,0:T(8,128)(2,1)S(1)} async-done(((bf16[8,128,640]{2,1,0:T(8,128)(2,1)}), bf16[8,128,640]{2,1,0:T(8,128)(2,1)S(1)}, u32[]{:S(2)}, u32[]{:S(2)}) %all-to-all-start.1) | async-done | bytes 1310752 | tf_op jit(solution)/shard_map/all_to_all | solution.py:286
  110.0 31.2 %all_to_all.15.parts_ref = bf16[16,40,128]{2,1,0:T(8,128)(2,1)S(1)} all-to-all(bf16[16,40,128]{2,1,0:T(8,128)(2,1)S(1)} %bitcast.12), channel_id=1, replica_groups={{0,16,32,48,64,80,96,112,128,144,160,176,192,208,224,240},{1,17,33,49,6..., dimensions={0} | all-to-all | bytes 327680 | tf_op jit(solution)/shard_map/all_to_all | solution.py:310
  142.5 2.8 %final_captions.1 = (bf16[128,1280]{1,0:T(8,128)(2,1)}, bf16[128,1280]{1,0:T(8,128)(2,1)}) custom-call(bf16[2,2,128,1280]{3,2,1,0:T(8,128)(2,1)S(1)} %copy-done.3, bf16[2,2,128,1280]{3,2,1,0:T(8,128)(2,1)} %collective-permute-done.3.core_ref, bf16[2,128,1280]{2,1,0:T(8,128)(2,1)} %collective-permute-done.4.x_ref, bf16[128,1280]{1,0:T(8,128)(2,1)S(1)} %copy-done.4, ...), custom_call_target="tpu_custom_call" | custom-call | tf_op jit(solution)/shard_map/final_captions/pallas_call | solution.py:331
  145.3 2.5 %copy-done = bf16[2048,1280]{1,0:T(8,128)(2,1)S(1)} copy-done((bf16[2048,1280]{1,0:T(8,128)(2,1)S(1)}, bf16[2048,1280]{1,0:T(8,128)(2,1)}, u32[]{:S(2)}) %copy-start) | copy-done | bytes 5242904
  147.8 1.5 final_audio.1
  (52 shorter events, 5.9 us)
Async XLA Ops:
  7.2 4.2 %copy-start.13 = (bf16[64,1280]{1,0:T(8,128)(2,1)S(1)}, bf16[64,1280]{1,0:T(8,128)(2,1)}, u32[]{:S(2)}) copy-start(bf16[64,1280]{1,0:T(8,128)(2,1)} %wo_ref.1) | copy-start | bytes 491524
  7.2 54.8 %all-gather.3.cloned.1.call-start = ((), (), s32[]{:S(2)}) async-start(), calls=%async_computation.3 | async-start | bytes 1392640 | tf_op jit(solution)/shard_map/all_gather | solution.py:228
  11.6 1.5 copy-start.1
  13.1 41.5 %all-to-all-start = ((bf16[4,256,1280]{2,1,0:T(8,128)(2,1)}), bf16[4,256,1280]{2,1,0:T(8,128)(2,1)S(1)}, u32[]{:S(2)}, u32[]{:S(2)}) async-start(bf16[4,256,1280]{2,1,0:T(8,128)(2,1)} %copy-done.1), calls=%async_computation | async-start | bytes 5242880 | tf_op jit(solution)/shard_map/all_to_all | solution.py:242
  17.6 23.1 %copy-start.18 = (f32[1280]{0:T(1024)S(1)}, f32[1280]{0:T(1024)}, u32[]{:S(2)}) copy-start(f32[1280]{0:T(1024)} %param.19) | copy-start | bytes 15364
  17.6 23.1 %copy-start.19 = (f32[1280]{0:T(1024)S(1)}, f32[1280]{0:T(1024)}, u32[]{:S(2)}) copy-start(f32[1280]{0:T(1024)} %param.20) | copy-start | bytes 15364
  17.6 23.7 %copy-start.20 = (f32[1280]{0:T(1024)S(1)}, f32[1280]{0:T(1024)}, u32[]{:S(2)}) copy-start(f32[1280]{0:T(1024)} %param.17) | copy-start | bytes 15364
  17.6 23.7 %copy-start.21 = (f32[1280]{0:T(1024)S(1)}, f32[1280]{0:T(1024)}, u32[]{:S(2)}) copy-start(f32[1280]{0:T(1024)} %param.18) | copy-start | bytes 15364
  17.6 127.7 %all-gather.5.cloned.1.call-start = ((), (), s32[]{:S(2)}) async-start(), calls=%async_computation.4 | async-start | bytes 5570560 | tf_op jit(solution)/shard_map/all_gather | solution.py:276
  18.8 19.9 %collective-permute-start = (bf16[2,128,1280]{2,1,0:T(8,128)(2,1)S(1)}, bf16[2,128,1280]{2,1,0:T(8,128)(2,1)}, u32[]{:S(2)}, u32[]{:S(2)}) collective-permute-start(bf16[2,128,1280]{2,1,0:T(8,128)(2,1)S(1)} %pad_maximum_fusion.t0), channel_id=1, source_target_pairs={{0,8},{1,9},{2,10},{3,11},{4,12},{5,13},{6,14},{7,15},{8,0},{9,1},... | collective-permute-start | bytes 1966088 | tf_op jit(solution)/shard_map/ppermute | solution.py:230
  22.2 19.7 %collective-permute-start.1 = (bf16[2,128,1280]{2,1,0:T(8,128)(2,1)S(1)}, bf16[2,128,1280]{2,1,0:T(8,128)(2,1)}, u32[]{:S(2)}, u32[]{:S(2)}) collective-permute-start(bf16[2,128,1280]{2,1,0:T(8,128)(2,1)S(1)} %pad_maximum_fusion.t0), channel_id=1, source_target_pairs={{0,1},{1,0},{2,3},{3,2},{4,5},{5,4},{6,7},{7,6},{8,9},{9,8},{10,11... | collective-permute-start | bytes 1966088 | tf_op jit(solution)/shard_map/ppermute | solution.py:231
  38.7 4.3 %collective-permute-start.2 = (bf16[2,128,1280]{2,1,0:T(8,128)(2,1)}, bf16[2,128,1280]{2,1,0:T(8,128)(2,1)}, u32[]{:S(2)}, u32[]{:S(2)}) collective-permute-start(bf16[2,128,1280]{2,1,0:T(8,128)(2,1)} %collective-permute-done.t1), channel_id=1, source_target_pairs={{0,1},{1,0},{2,3},{3,2},{4,5},{5,4},{6,7},{7,6},{8,9},{9,8},{10,11... | collective-permute-start | bytes 1966088 | tf_op jit(solution)/shard_map/ppermute | solution.py:232
  54.6 0.7 copy-start.15
  55.3 0.7 copy-start.17
  59.0 1.1 copy-start.6
  60.1 1.2 copy-start.8
  61.3 0.7 copy-start.11
  62.0 1.3 copy-start.5
  63.3 0.9 copy-start.12
  64.3 0.7 copy-start.14
  65.0 0.7 copy-start.16
  70.8 4.9 %copy-start.7 = (bf16[512,1280]{1,0:T(8,128)(2,1)S(1)}, bf16[512,1280]{1,0:T(8,128)(2,1)}, u32[]{:S(2)}) copy-start(bf16[512,1280]{1,0:T(8,128)(2,1)} %copy-done.6) | copy-start | bytes 3932164
  70.8 4.9 %copy-start.9 = (bf16[512,1280]{1,0:T(8,128)(2,1)S(1)}, bf16[512,1280]{1,0:T(8,128)(2,1)}, u32[]{:S(2)}) copy-start(bf16[512,1280]{1,0:T(8,128)(2,1)} %copy-done.8) | copy-start | bytes 3932164
  72.8 1.0 copy-start.2
  73.8 9.0 %collective-permute-start.3 = (bf16[2,2,128,1280]{3,2,1,0:T(8,128)(2,1)}, bf16[2,2,128,1280]{3,2,1,0:T(8,128)(2,1)}, u32[]{:S(2)}, u32[]{:S(2)}) collective-permute-start(bf16[2,2,128,1280]{3,2,1,0:T(8,128)(2,1)} %get-tuple-element.23), channel_id=1, source_target_pairs={{0,1},{1,0},{2,3},{3,2},{4,5},{5,4},{6,7},{7,6},{8,9},{9,8},{10,11... | collective-permute-start | bytes 3932168 | tf_op jit(solution)/shard_map/ppermute | solution.py:298
  77.7 5.1 %copy-start.3 = (bf16[2,2,128,1280]{3,2,1,0:T(8,128)(2,1)S(1)}, bf16[2,2,128,1280]{3,2,1,0:T(8,128)(2,1)}, u32[]{:S(2)}) copy-start(bf16[2,2,128,1280]{3,2,1,0:T(8,128)(2,1)} %copy-done.2) | copy-start | bytes 3932164
  77.7 32.1 %all-to-all-start.1 = ((bf16[8,128,640]{2,1,0:T(8,128)(2,1)}), bf16[8,128,640]{2,1,0:T(8,128)(2,1)S(1)}, u32[]{:S(2)}, u32[]{:S(2)}) async-start(bf16[8,128,640]{2,1,0:T(8,128)(2,1)} %weight_grads.1), calls=%async_computation.1 | async-start | bytes 2621440 | tf_op jit(solution)/shard_map/all_to_all | solution.py:286
  84.9 57.6 %copy-start.4 = (bf16[128,1280]{1,0:T(8,128)(2,1)S(1)}, bf16[128,1280]{1,0:T(8,128)(2,1)}, u32[]{:S(2)}) copy-start(bf16[128,1280]{1,0:T(8,128)(2,1)} %caption_ref.1) | copy-start | bytes 983044
  84.9 57.6 %collective-permute-start.4 = (bf16[2,128,1280]{2,1,0:T(8,128)(2,1)}, bf16[2,128,1280]{2,1,0:T(8,128)(2,1)}, u32[]{:S(2)}, u32[]{:S(2)}) collective-permute-start(bf16[2,128,1280]{2,1,0:T(8,128)(2,1)} %fusion), channel_id=1, source_target_pairs={{0,8},{1,9},{2,10},{3,11},{4,12},{5,13},{6,14},{7,15},{8,0},{9,1},... | collective-permute-start | bytes 1966088 | tf_op jit(solution)/shard_map/ppermute | solution.py:300
  142.5 2.8 %copy-start.10 = (bf16[1,32,1280]{2,1,0:T(8,128)(2,1)S(1)}, bf16[1,32,1280]{2,1,0:T(8,128)(2,1)}, u32[]{:S(2)}) copy-start(bf16[1,32,1280]{2,1,0:T(8,128)(2,1)} %audio_ref.1) | copy-start | bytes 245764
  145.3 2.5 %copy-start = (bf16[2048,1280]{1,0:T(8,128)(2,1)S(1)}, bf16[2048,1280]{1,0:T(8,128)(2,1)}, u32[]{:S(2)}) copy-start(bf16[2048,1280]{1,0:T(8,128)(2,1)} %all-gather.5.cloned.1.call-done) | copy-start | bytes 15728644
Sparse Core Ops, SparseCore 0:
  10.2 49.5 all-gather.2
  70.9 68.2 all-gather.4

commit v2 on v1

v2 whole, which is shorter than its diff:
```python
import functools
import math

import jax
import jax.numpy as jnp
from jax import lax
from jax.experimental import pallas as pl
from jax.experimental.pallas import tpu as pltpu
from jax.sharding import PartitionSpec as P

HEAD_DIM = 64
EPSILON = 1e-05
FRAMES = 32
CAP = 128
HELD = 4
ROWS = HELD * CAP
WIDTH = HELD * HEAD_DIM
BF16 = jnp.bfloat16
F32 = jnp.float32
LARGEST_BF16 = 3.3895313892515355e38

HBM = pl.BlockSpec(memory_space=pltpu.HBM)
MIB = 1 << 20
BIG = 60
COST = pl.CostEstimate(flops=1000, bytes_accessed=1000, transcendentals=0)


def params(mib):
    return pltpu.CompilerParams(vmem_limit_bytes=mib * MIB)


def dot(left, right, left_dim=1, right_dim=0):
    return lax.dot_general(
        left, right, (((left_dim,), (right_dim,)), ((), ())), preferred_element_type=F32
    )


def standardize(values):
    row_mean = jnp.mean(values, axis=-1, keepdims=True)
    centred = values - row_mean
    inverse_std = lax.rsqrt(jnp.mean(centred * centred, axis=-1, keepdims=True) + EPSILON)
    return centred * inverse_std, inverse_std


def norm_backward(upstream, normed, inverse_std, gain_vec):
    scaled = upstream * gain_vec
    mean_term = jnp.mean(scaled, axis=-1, keepdims=True)
    cross_term = jnp.mean(scaled * normed, axis=-1, keepdims=True)
    return inverse_std * (scaled - mean_term - normed * cross_term)


def held_caption(own, part):
    return own ^ ((part & 1) * 8) ^ (part >> 1)


def caption_length(meta, caption):
    return meta[1 + caption]


def described_clip(meta, caption):
    return meta[17 + caption]


def row_of_y(own):
    return (own >> 1) & 3


def weight_of(w_ref, kind):
    rows = w_ref[:, kind * HEAD_DIM : (kind + 1) * HEAD_DIM, :]
    return rows.reshape(WIDTH, w_ref.shape[2])


def pack_kernel(io, *refs):
    *blocks, out_ref = refs
    io.take()
    first = 0
    for block in blocks:
        for target in range(HELD):
            out_ref[target, first : first + block.shape[0], :] = block[...]
        first += block.shape[0]


def norm_kernel(io, meta, t0, t1, t2, t3, gain, bias, hid_ref, up_ref):
    width = hid_ref.shape[1]
    io.take(0, 5, 6)
    own = meta[0]
    positions = lax.broadcasted_iota(jnp.int32, (CAP, 1), 0)
    gain_row, bias_row = gain[...].reshape(1, width), bias[...].reshape(1, width)
    for part, tokens in enumerate((t0, t1, t2, t3)):
        io.take(1 + part)
        span = slice(part * CAP, (part + 1) * CAP)
        normed, _ = standardize(tokens[0].astype(F32))
        hid_ref[span, :] = (normed * gain_row + bias_row).astype(BF16)
        live = positions < caption_length(meta, held_caption(own, part))
        up_ref[span, :] = jnp.where(live, tokens[1].astype(F32), 0.0).astype(BF16)


def segment_sum(values, ones):
    high = jnp.minimum(values, LARGEST_BF16).astype(BF16)
    low = (values - high.astype(F32)).astype(BF16)
    return dot(high, ones) + dot(low, ones)


def attend_kernel(
    io,
    meta,
    gain,
    bias,
    kv_ref,
    qo_ref,
    hid_ref,
    up_ref,
    near_ref,
    other_ref,
    dkv_ref,
    att_ref,
    dq_ref,
    states_ref,
):
    width = hid_ref.shape[1]
    io.take(0, 1, 2, 7, 8)
    own = meta[0]
    gain_row, bias_row = gain[...].reshape(1, width), bias[...].reshape(1, width)
    for part in range(HELD):
        clip = described_clip(meta, held_caption(own, part))
        place = row_of_y(clip) + 4 * ((clip ^ own) >> 3)
        near = ((clip ^ own) & 1) == 0
        frames = jnp.where(near, near_ref[place].astype(F32), other_ref[place].astype(F32))
        normed, _ = standardize(frames)
        states_ref[part * FRAMES : (part + 1) * FRAMES, :] = (normed * gain_row + bias_row).astype(BF16)
    io.take(3)
    keys = dot(states_ref[...], weight_of(kv_ref, 0), 1, 1).astype(BF16)
    values = dot(states_ref[...], weight_of(kv_ref, 1), 1, 1).astype(BF16)
    io.take(4, 5, 6)
    queries = dot(hid_ref[...], weight_of(qo_ref, 0), 1, 1).astype(BF16)
    d_attended = dot(up_ref[...], weight_of(qo_ref, 1), 1, 1).astype(BF16)
    scale = 1.0 / math.sqrt(HEAD_DIM)
    pairs = HELD * FRAMES
    row_head = lax.broadcasted_iota(jnp.int32, (pairs, WIDTH), 0) // FRAMES
    lane_head = lax.broadcasted_iota(jnp.int32, (pairs, WIDTH), 1) // HEAD_DIM
    same = row_head == lane_head
    first = lax.broadcasted_iota(jnp.int32, (pairs, pairs), 0) // FRAMES
    second = lax.broadcasted_iota(jnp.int32, (pairs, pairs), 1) // FRAMES
    ones = jnp.where(first == second, 1.0, 0.0).astype(BF16)

    def spread(rows):
        repeated = jnp.concatenate([rows.astype(F32)] * HELD, axis=0)
        return jnp.where(same, repeated, 0.0).astype(BF16)

    def collect(rows):
        kept = jnp.where(same, rows, 0.0)
        total = kept[0:FRAMES]
        for head in range(1, HELD):
            total = total + kept[head * FRAMES : (head + 1) * FRAMES]
        return total.astype(BF16)

    for part in range(HELD):
        span = slice(part * CAP, (part + 1) * CAP)
        frames = slice(part * FRAMES, (part + 1) * FRAMES)
        key_block, value_block = spread(keys[frames]), spread(values[frames])
        query = queries[span]
        d_att = d_attended[span]
        weights = jnp.exp(dot(query, key_block, 1, 1) * scale)
        softmax = weights / segment_sum(weights, ones)
        low = softmax.astype(BF16)
        att_ref[span, :] = dot(low, value_block).astype(BF16)
        d_softmax = dot(d_att, value_block, 1, 1)
        inner = segment_sum(softmax * d_softmax, ones)
        d_scores = (softmax * (d_softmax - inner) * scale).astype(BF16)
        dq_ref[span, :] = dot(d_scores, key_block).astype(BF16)
        d_keys = collect(dot(d_scores, query, 0, 0))
        d_values = collect(dot(low, d_att, 0, 0))
        for row in range(HELD):
            dkv_ref[row, 0, part] = d_keys
            dkv_ref[row, 1, part] = d_values


def weight_grad_kernel(io, att_ref, dq_ref, hid_ref, up_ref, grad_ref):
    io.take()
    half = hid_ref.shape[1] // 2
    for kind, (left, right) in enumerate(((dq_ref, hid_ref), (att_ref, up_ref))):
        for side in range(2):
            product = dot(left[...], right[:, side * half : (side + 1) * half], 0, 0).astype(BF16)
            for head in range(HELD):
                grad_ref[side * HELD + head, kind * HEAD_DIM : (kind + 1) * HEAD_DIM, :] = product[
                    head * HEAD_DIM : (head + 1) * HEAD_DIM
                ]


def update_kernel(io, meta, got_ref, att_ref, dq_ref, kv_ref, qo_ref, send_x, send_own, keep_ref, keys_ref, values_ref):
    io.take()
    own = meta[0]
    for part in range(HELD):
        clip = held_caption(own, part)
        caption = 0
        for index in range(4 * HELD):
            caption = jnp.where(described_clip(meta, index) == clip, index, caption)
        row = row_of_y(caption)
        apart = caption ^ own
        place = (apart >> 3) + 2 * (apart & 1)
        keys_ref[part * FRAMES : (part + 1) * FRAMES, :] = got_ref[row, 0, place]
        values_ref[part * FRAMES : (part + 1) * FRAMES, :] = got_ref[row, 1, place]
    w_query, w_out = weight_of(qo_ref, 0), weight_of(qo_ref, 1)
    d_states = dot(keys_ref[...], weight_of(kv_ref, 0)) + dot(values_ref[...], weight_of(kv_ref, 1))
    for part in reversed(range(HELD)):
        target = (keep_ref.at[0], keep_ref.at[1], send_own, send_x)[part]
        span = slice(part * CAP, (part + 1) * CAP)
        target[:CAP, :] = dot(att_ref[span, :], w_out).astype(BF16)
        target[CAP : 2 * CAP, :] = dot(dq_ref[span, :], w_query).astype(BF16)
        target[2 * CAP :, :] = d_states[part * FRAMES : (part + 1) * FRAMES].astype(BF16)
        if part > 1:
            io.give(3 - part)


def grad_sum_kernel(io, parts_ref, out_ref):
    io.take()
    total = parts_ref[0].astype(F32)
    for part in range(1, parts_ref.shape[0]):
        total = total + parts_ref[part].astype(F32)
    out_ref[...] = total.T.astype(BF16)


def grad_final_kernel(parts_ref, wq_ref, wo_ref):
    total = parts_ref[0].astype(F32)
    for part in range(1, parts_ref.shape[0]):
        total = total + parts_ref[part].astype(F32)
    wq_ref[...] = total[:, :HEAD_DIM]
    wo_ref[...] = total[:, HEAD_DIM:]


def add_kernel(io, left_ref, right_ref, out_ref):
    io.take()
    out_ref[...] = (left_ref[...].astype(F32) + right_ref[...].astype(F32)).astype(BF16)


def final_kernel(
    io, keep_ref, core_ref, x_ref, caption_ref, dec_gain, audio_ref, enc_gain, update_ref, grad_ref, out_ref
):
    io.take()
    width = caption_ref.shape[1]

    def total(start, stop):
        near = keep_ref[start:stop].astype(F32) + core_ref[start:stop].astype(F32)
        return near + x_ref[start:stop].astype(F32)

    update_ref[...] = total(0, CAP).astype(BF16)
    io.give(0)
    normed, inverse_std = standardize(caption_ref[...].astype(F32))
    d_hidden = total(CAP, 2 * CAP)
    grad_ref[...] = norm_backward(d_hidden, normed, inverse_std, dec_gain[...].reshape(1, width)).astype(BF16)
    io.give(1)
    normed, inverse_std = standardize(audio_ref[0].astype(F32))
    d_states = total(2 * CAP, 2 * CAP + FRAMES)
    out_ref[0] = norm_backward(d_states, normed, inverse_std, enc_gain[...].reshape(1, width)).astype(BF16)


class Transfers:
    def __init__(self, takes, gives):
        self.takes, self.gives = dict(enumerate(takes)), dict(enumerate(gives))
        self.given = []
        for copy in takes:
            copy.start()

    def take(self, *places):
        for place in places or tuple(self.takes):
            self.takes.pop(place).wait()

    def give(self, *places):
        for place in places or tuple(self.gives):
            self.given.append(self.gives.pop(place))
            self.given[-1].start()

    def finish(self):
        if self.gives:
            self.give()
        for copy in self.given:
            copy.wait()


def call(kernel, name, outs, operands, mib=BIG, scratch=(), scalars=0):
    takes, gives = len(operands), len(outs)
    places = [operand[1] if isinstance(operand, tuple) else None for operand in operands]
    operands = [operand[0] if isinstance(operand, tuple) else operand for operand in operands]

    def copied(*refs):
        given, wanted, refs = refs[:takes], refs[takes : takes + gives], refs[takes + gives :]
        held, made, refs = refs[:takes], refs[takes : takes + gives], refs[takes + gives :]
        sems, rest = refs[0], refs[1:]
        io = Transfers(
            [
                pltpu.make_async_copy(
                    given[i] if places[i] is None else given[i].at[places[i]], held[i], sems.at[i]
                )
                for i in range(takes)
            ],
            [pltpu.make_async_copy(made[i], wanted[i], sems.at[takes + i]) for i in range(gives)],
        )
        kernel(io, *held, *made, *rest)
        io.finish()

    def space(place, array):
        shape = array.shape if places[place] is None else array.shape[1:]
        return (pltpu.SMEM if place < scalars else pltpu.VMEM)(shape, array.dtype)

    return pl.pallas_call(
        copied,
        out_shape=tuple(jax.ShapeDtypeStruct(*out) for out in outs),
        in_specs=[HBM] * takes,
        out_specs=(HBM,) * gives,
        scratch_shapes=[space(place, operand) for place, operand in enumerate(operands)]
        + [pltpu.VMEM(*out) for out in outs]
        + [pltpu.SemaphoreType.DMA((takes + gives,))]
        + list(scratch),
        compiler_params=params(mib),
        cost_estimate=COST,
        name=name,
    )(*operands)


def body(
    captions,
    audio,
    caption_len,
    pairing,
    enc_gain,
    enc_bias,
    dec_gain,
    dec_bias,
    w_query,
    w_key,
    w_value,
    w_out,
    grad_update,
    *,
    depth,
    y_groups,
    yx_groups,
    z_groups,
):
    both = ("dp", "mp")
    width = captions.shape[1]
    own = lax.axis_index("mp").astype(jnp.int32).reshape(1)
    meta = jnp.concatenate([own, caption_len, pairing[0], jnp.zeros((95,), jnp.int32)])
    swap_core = [(index, index ^ 1) for index in range(16)]
    swap_x = [(index, index ^ 8) for index in range(16)]

    (kv_out,) = call(
        pack_kernel,
        "pack_keys_values",
        [((HELD, 2 * HEAD_DIM + FRAMES, width), BF16)],
        (w_key.T, w_value.T, (audio, 0)),
    )
    kv_got = lax.all_to_all(kv_out, "mp", 0, 0, axis_index_groups=y_groups, tiled=True)
    (qo_out,) = call(
        pack_kernel, "pack_queries_out", [((HELD, 2 * HEAD_DIM, width), BF16)], (w_query.T, w_out)
    )
    kv_got, qo_out = lax.optimization_barrier((kv_got, qo_out))
    qo_got = lax.all_to_all(qo_out, "mp", 0, 0, axis_index_groups=y_groups, tiled=True)
    audio_y = kv_got[:, 2 * HEAD_DIM :]
    audio_near = jnp.concatenate([audio_y, lax.ppermute(audio_y, "mp", swap_x)])
    audio_other = lax.ppermute(audio_near, "mp", swap_core)
    tokens_own = jnp.stack([captions, grad_update])
    tokens_x = lax.ppermute(tokens_own, "mp", swap_x)
    tokens_core = lax.ppermute(tokens_own, "mp", swap_core)
    tokens_far = lax.ppermute(tokens_x, "mp", swap_core)
    hidden, upstream = call(
        norm_kernel,
        "norms",
        [((ROWS, width), BF16), ((ROWS, width), BF16)],
        (meta, tokens_own, tokens_x, tokens_core, tokens_far, dec_gain, dec_bias),
        scalars=1,
    )

    d_kv, attended, d_queries = call(
        attend_kernel,
        "attend",
        [
            ((HELD, 2, HELD, FRAMES, WIDTH), BF16),
            ((ROWS, WIDTH), BF16),
            ((ROWS, WIDTH), BF16),
        ],
        (meta, enc_gain, enc_bias, kv_got, qo_got, hidden, upstream, audio_near, audio_other),
        scratch=[pltpu.VMEM((HELD * FRAMES, width), BF16)],
        scalars=1,
    )
    d_kv_got = lax.all_to_all(d_kv, "mp", 0, 0, axis_index_groups=y_groups, tiled=True)
    (weight_parts,) = call(
        weight_grad_kernel,
        "weight_grads",
        [((2 * HELD, 2 * HEAD_DIM, width // 2), BF16)],
        (attended, d_queries, hidden, upstream),
    )
    weight_parts, d_kv_got = lax.optimization_barrier((weight_parts, d_kv_got))

    weight_got = lax.all_to_all(weight_parts, both, 0, 0, axis_index_groups=yx_groups, tiled=True)
    rows = 2 * CAP + FRAMES
    send_x, send_own, keep = call(
        update_kernel,
        "updates",
        [((rows, width), BF16), ((rows, width), BF16), ((2, rows, width), BF16)],
        (meta, d_kv_got, attended, d_queries, kv_got, qo_got),
        mib=24,
        scratch=[pltpu.VMEM((HELD * FRAMES, WIDTH), BF16), pltpu.VMEM((HELD * FRAMES, WIDTH), BF16)],
        scalars=1,
    )
    core_x = lax.ppermute(send_x, "mp", swap_core)
    core_own = lax.ppermute(send_own, "mp", swap_core)
    (x_out,) = call(add_kernel, "add_updates", [((rows, width), BF16)], ((keep, 1), core_x), mib=8)
    x_parts = lax.ppermute(x_out, "mp", swap_x)
    weight_got, _ = lax.optimization_barrier((weight_got, x_out))

    (weight_half,) = call(
        grad_sum_kernel, "sum_weight_grads", [((width // 2, 2 * HEAD_DIM), BF16)], (weight_got,), mib=8
    )
    weight_last = lax.all_to_all(
        weight_half.reshape(depth, width // (2 * depth), 2 * HEAD_DIM),
        both,
        0,
        0,
        axis_index_groups=z_groups,
        tiled=True,
    )
    x_parts, _ = lax.optimization_barrier((x_parts, weight_half))
    cross_update, grad_captions, grad_audio = call(
        final_kernel,
        "final_rows",
        [((CAP, width), BF16), ((CAP, width), BF16), ((1, FRAMES, width), BF16)],
        ((keep, 0), core_own, x_parts, captions, dec_gain, audio, enc_gain),
        mib=16,
    )
    weight_last, cross_update, grad_captions, grad_audio = lax.optimization_barrier(
        (weight_last, cross_update, grad_captions, grad_audio)
    )
    rows = width // (2 * depth)
    grad_wq, grad_wo = pl.pallas_call(
        grad_final_kernel,
        out_shape=(jax.ShapeDtypeStruct((rows, HEAD_DIM), F32),) * 2,
        compiler_params=params(16),
        name="final_weight_grads",
    )(weight_last)
    return (cross_update, grad_captions, grad_audio, grad_wq, grad_wo.T)


def device_groups(dp_size):
    depth = dp_size // 2

    def device(x_hi, z, x_lo, y, core):
        return (x_hi * depth + z) * 16 + (x_lo * 4 + y) * 2 + core

    y_groups = [[(x * 4 + y) * 2 + core for y in range(4)] for x in range(2) for core in range(2)]
    yx_groups = [
        [device(x_hi, z, x_lo, y, core) for x_hi in range(2) for y in range(4)]
        for z in range(depth)
        for x_lo in range(2)
        for core in range(2)
    ]
    z_groups = [
        [device(x_hi, z, x_lo, y, core) for z in range(depth)]
        for x_hi in range(2)
        for x_lo in range(2)
        for y in range(4)
        for core in range(2)
    ]
    return dict(depth=depth, y_groups=y_groups, yx_groups=yx_groups, z_groups=z_groups)


def solution(mesh):
    in_specs = (
        P(("dp", "mp"), None),
        P(("dp", "mp"), None, None),
        P("dp"),
        P("dp", None),
        P(),
        P(),
        P(),
        P(),
        P(None, "mp"),
        P(None, "mp"),
        P(None, "mp"),
        P("mp", None),
        P(("dp", "mp"), None),
    )
    out_specs = (
        P(("dp", "mp"), None),
        P(("dp", "mp"), None),
        P(("dp", "mp"), None, None),
        P("dp", "mp"),
        P("mp", "dp"),
    )
    local = functools.partial(body, **device_groups(mesh.shape["dp"]))
    return jax.shard_map(local, mesh=mesh, in_specs=in_specs, out_specs=out_specs, check_vma=False)
```

time: 157 us -> 130 us (0.83)
  the two profiles are of different devices: /device:TPU:32 before, /device:TPU:38 now
where the time goes in v2:
time: 130 us; the launch traced here: 129 us
  starting transfers between devices  51.2 us (39%)
  waiting for transfers between devices  37.5 us (29%)
  Pallas kernels  31.7 us (24%)
  local copies, waits for them, and re-layouts  4.84 us (4%)
  other arithmetic  2.53 us (2%)
    pallas_call x9, Pallas kernels, call(): pl.pallas_call(copied, out_shape=tuple((jax.ShapeDtypeStruct(*out) for ou...  31 us
    all_to_all x1, waiting for transfers between devices, body(): lax.all_to_all(kv_out, 'mp', 0, 0, axis_index_groups=y_groups, tiled=True)  15.6 us
    all_to_all x1, starting transfers between devices, body(): lax.all_to_all(weight_half.reshape(depth, width // (2 * depth), 2 * HEAD_...  15.2 us
    all_to_all x1, waiting for transfers between devices, body(): lax.all_to_all(weight_half.reshape(depth, width // (2 * depth), 2 * HEAD_...  12.4 us
    all_to_all x1, starting transfers between devices, body(): lax.all_to_all(weight_parts, both, 0, 0, axis_index_groups=yx_groups, til...  5.46 us
    unnamed x42, local copies, waits for them, and re-layouts  4.81 us
    all_to_all x1, starting transfers between devices, body(): lax.all_to_all(kv_out, 'mp', 0, 0, axis_index_groups=y_groups, tiled=True)  4.61 us
    all_to_all x1, waiting for transfers between devices, body(): lax.all_to_all(d_kv, 'mp', 0, 0, axis_index_groups=y_groups, tiled=True)  4.13 us
  transfers between devices with their start and end apart: 13, of which 5 were waited for; matrix products, arithmetic and copies ran while one was open for 2% of the time, Pallas kernels for 16%

profile of v2, /device:TPU:38, one launch (start us, length us, event | category | flops | bytes accessed | tf_op | source)
XLA Modules:
  0.0 128.9 jit_solution(12879412402254080515)
XLA Ops:
  0.6 2.4 %pack_keys_values.1 = bf16[4,160,1280]{2,1,0:T(8,128)(2,1)} custom-call(bf16[64,1280]{1,0:T(8,128)(2,1)} %bitcast.13, bf16[64,1280]{1,0:T(8,128)(2,1)} %bitcast.14, bf16[1,32,1280]{2,1,0:T(8,128)(2,1)} %refs_5_.3), custom_call_target="tpu_custom_call" | custom-call | flops 1000 | bytes 1000 | tf_op jit(solution)/shard_map/pack_keys_values/pallas_call | solution.py:305
  3.0 4.6 %all-to-all-start = ((bf16[4,160,1280]{2,1,0:T(8,128)(2,1)}), bf16[4,160,1280]{2,1,0:T(8,128)(2,1)S(1)}, u32[]{:S(2)}, u32[]{:S(2)}) async-start(bf16[4,160,1280]{2,1,0:T(8,128)(2,1)} %pack_keys_values.1), calls=%async_computation | async-start | bytes 3276800 | tf_op jit(solution)/shard_map/all_to_all | solution.py:353
  7.7 0.9 pad_maximum_fusion.refs_1_
  8.6 2.7 %collective-permute-start = (bf16[2,128,1280]{2,1,0:T(8,128)(2,1)}, bf16[2,128,1280]{2,1,0:T(8,128)(2,1)}, u32[]{:S(2)}, u32[]{:S(2)}) collective-permute-start(bf16[2,128,1280]{2,1,0:T(8,128)(2,1)} %pad_maximum_fusion.refs_1_), channel_id=1, source_target_pairs={{0,8},{1,9},{2,10},{3,11},{4,12},{5,13},{6,14},{7,15},{8,0},{9,1},... | collective-permute-start | bytes 1966088 | tf_op jit(solution)/shard_map/ppermute | solution.py:363
  11.3 2.2 %pack_queries_out.1 = bf16[4,128,1280]{2,1,0:T(8,128)(2,1)} custom-call(bf16[64,1280]{1,0:T(8,128)(2,1)} %bitcast.12, bf16[64,1280]{1,0:T(8,128)(2,1)} %refs_1_.2), custom_call_target="tpu_custom_call" | custom-call | flops 1000 | bytes 1000 | tf_op jit(solution)/shard_map/pack_queries_out/pallas_call | solution.py:305
  13.5 15.6 %all-to-all-done.refs_3_.refs_4_ = bf16[4,160,1280]{2,1,0:T(8,128)(2,1)S(1)} async-done(((bf16[4,160,1280]{2,1,0:T(8,128)(2,1)}), bf16[4,160,1280]{2,1,0:T(8,128)(2,1)S(1)}, u32[]{:S(2)}, u32[]{:S(2)}) %all-to-all-start) | async-done | bytes 1638432 | tf_op jit(solution)/shard_map/all_to_all | solution.py:353
  29.1 2.7 %collective-permute-start.3 = (bf16[4,32,1280]{2,1,0:T(8,128)(2,1)S(1)}, bf16[4,32,1280]{2,1,0:T(8,128)(2,1)}, u32[]{:S(2)}, u32[]{:S(2)}) collective-permute-start(bf16[4,32,1280]{2,1,0:T(8,128)(2,1)S(1)} %slice.3), channel_id=1, source_target_pairs={{0,8},{1,9},{2,10},{3,11},{4,12},{5,13},{6,14},{7,15},{8,0},{9,1},... | collective-permute-start | bytes 983048 | tf_op jit(solution)/shard_map/ppermute | solution.py:360
  31.9 3.6 %all-to-all-start.1 = ((bf16[4,128,1280]{2,1,0:T(8,128)(2,1)}), bf16[4,128,1280]{2,1,0:T(8,128)(2,1)S(1)}, u32[]{:S(2)}, u32[]{:S(2)}) async-start(bf16[4,128,1280]{2,1,0:T(8,128)(2,1)} %pack_queries_out.1), calls=%async_computation.1 | async-start | bytes 2621440 | tf_op jit(solution)/shard_map/all_to_all | solution.py:358
  35.4 1.9 %collective-permute-start.1 = (bf16[2,128,1280]{2,1,0:T(8,128)(2,1)}, bf16[2,128,1280]{2,1,0:T(8,128)(2,1)S(1)}, u32[]{:S(2)}, u32[]{:S(2)}) collective-permute-start(bf16[2,128,1280]{2,1,0:T(8,128)(2,1)} %pad_maximum_fusion.refs_1_), channel_id=1, source_target_pairs={{0,1},{1,0},{2,3},{3,2},{4,5},{5,4},{6,7},{7,6},{8,9},{9,8},{10,11... | collective-permute-start | bytes 1966088 | tf_op jit(solution)/shard_map/ppermute | solution.py:364
  37.4 2.4 %collective-permute-start.2 = (bf16[2,128,1280]{2,1,0:T(8,128)(2,1)}, bf16[2,128,1280]{2,1,0:T(8,128)(2,1)}, u32[]{:S(2)}, u32[]{:S(2)}) collective-permute-start(bf16[2,128,1280]{2,1,0:T(8,128)(2,1)} %collective-permute-done.refs_2_), channel_id=1, source_target_pairs={{0,1},{1,0},{2,3},{3,2},{4,5},{5,4},{6,7},{7,6},{8,9},{9,8},{10,11... | collective-permute-start | bytes 1966088 | tf_op jit(solution)/shard_map/ppermute | solution.py:365
  39.8 1.0 pad_maximum_fusion.1.refs_7_
  40.8 1.9 %collective-permute-start.4 = (bf16[8,32,1280]{2,1,0:T(8,128)(2,1)S(1)}, bf16[8,32,1280]{2,1,0:T(8,128)(2,1)S(1)}, u32[]{:S(2)}, u32[]{:S(2)}) collective-permute-start(bf16[8,32,1280]{2,1,0:T(8,128)(2,1)S(1)} %pad_maximum_fusion.1.refs_7_), channel_id=1, source_target_pairs={{0,1},{1,0},{2,3},{3,2},{4,5},{5,4},{6,7},{7,6},{8,9},{9,8},{10,11... | collective-permute-start | bytes 1966088 | tf_op jit(solution)/shard_map/ppermute | solution.py:361
  44.3 4.5 %norms.1 = (bf16[512,1280]{1,0:T(8,128)(2,1)}, bf16[512,1280]{1,0:T(8,128)(2,1)}) custom-call(s32[128]{0:T(128)} %pad_add_fusion.refs_0_, bf16[2,128,1280]{2,1,0:T(8,128)(2,1)} %pad_maximum_fusion.refs_1_, bf16[2,128,1280]{2,1,0:T(8,128)(2,1)} %collective-permute-done.refs_2_, bf16[2,128,1280]{2,1,0:T(8,128)(2,1)} %copy-done.16, ...), custom_call_target="tpu_custom_call" | custom-call | flops 1000 | bytes 1000 | tf_op jit(solution)/shard_map/norms/pallas_call | solution.py:305
  48.8 3.3 %all-to-all-done.1.refs_4_.refs_5_ = bf16[4,128,1280]{2,1,0:T(8,128)(2,1)S(1)} async-done(((bf16[4,128,1280]{2,1,0:T(8,128)(2,1)}), bf16[4,128,1280]{2,1,0:T(8,128)(2,1)S(1)}, u32[]{:S(2)}, u32[]{:S(2)}) %all-to-all-start.1) | async-done | bytes 1310752 | tf_op jit(solution)/shard_map/all_to_all | solution.py:358
  52.1 1.1 copy-done.2
  53.4 8.4 %attend.1 = (bf16[4,2,4,32,256]{4,3,2,1,0:T(8,128)(2,1)}, bf16[512,256]{1,0:T(8,128)(2,1)}, bf16[512,256]{1,0:T(8,128)(2,1)}) custom-call(s32[128]{0:T(128)} %pad_add_fusion.refs_0_, f32[1280]{0:T(1024)} %refs_6_.3, f32[1280]{0:T(1024)} %refs_2_.3, bf16[4,160,1280]{2,1,0:T(8,128)(2,1)} %copy-done, bf16[4,128,1280]{2,1,0:T(8,128)(2,1)} %copy-done.2, ...), custom_call_target="tpu_custom_call" | custom-call | flops 1000 | bytes 1000 | tf_op jit(solution)/shard_map/attend/pallas_call | solution.py:305
  61.8 3.5 %all-to-all-start.2 = ((bf16[4,2,4,32,256]{4,3,2,1,0:T(8,128)(2,1)}), bf16[4,2,4,32,256]{4,3,2,1,0:T(8,128)(2,1)S(1)}, u32[]{:S(2)}, u32[]{:S(2)}) async-start(bf16[4,2,4,32,256]{4,3,2,1,0:T(8,128)(2,1)} %get-tuple-element.34), calls=%async_computation.2 | async-start | bytes 1048576 | tf_op jit(solution)/shard_map/all_to_all | solution.py:386
  65.3 4.1 %weight_grads.1 = bf16[8,128,640]{2,1,0:T(8,128)(2,1)} custom-call(bf16[512,256]{1,0:T(8,128)(2,1)} %get-tuple-element.32.refs_0_.refs_2_, bf16[512,256]{1,0:T(8,128)(2,1)} %get-tuple-element.33.refs_1_.refs_3_, bf16[512,1280]{1,0:T(8,128)(2,1)} %get-tuple-element.30.refs_5_.refs_2_, bf16[512,1280]{1,0:T(8,128)(2,1)} %get-tuple-element.31.refs_6_.refs_3_), custom_call_target="tpu_custom_call" | custom-call | flops 1000 | bytes 1000 | tf_op jit(solution)/shard_map/weight_grads/pallas_call | solution.py:305
  69.4 4.1 %all-to-all-done.2.refs_1_ = bf16[4,2,4,32,256]{4,3,2,1,0:T(8,128)(2,1)S(1)} async-done(((bf16[4,2,4,32,256]{4,3,2,1,0:T(8,128)(2,1)}), bf16[4,2,4,32,256]{4,3,2,1,0:T(8,128)(2,1)S(1)}, u32[]{:S(2)}, u32[]{:S(2)}) %all-to-all-start.2) | async-done | bytes 524320 | tf_op jit(solution)/shard_map/all_to_all | solution.py:386
  73.5 5.5 %all-to-all-start.3 = ((bf16[8,128,640]{2,1,0:T(8,128)(2,1)}), bf16[8,128,640]{2,1,0:T(8,128)(2,1)}, u32[]{:S(2)}, u32[]{:S(2)}) async-start(bf16[8,128,640]{2,1,0:T(8,128)(2,1)} %weight_grads.1), calls=%async_computation.3 | async-start | bytes 2621440 | tf_op jit(solution)/shard_map/all_to_all | solution.py:395
  79.0 0.9 copy-done.8
  80.0 0.9 copy-done.9
  80.9 3.0 %updates.1 = (bf16[288,1280]{1,0:T(8,128)(2,1)S(1)}, bf16[288,1280]{1,0:T(8,128)(2,1)}, bf16[2,288,1280]{2,1,0:T(8,128)(2,1)S(1)}) custom-call(s32[128]{0:T(128)S(1)} %copy-done.14, bf16[4,2,4,32,256]{4,3,2,1,0:T(8,128)(2,1)S(1)} %all-to-all-done.2.refs_1_, bf16[512,256]{1,0:T(8,128)(2,1)S(1)} %copy-done.8, bf16[512,256]{1,0:T(8,128)(2,1)S(1)} %copy-done.9, ...), custom_call_target="tpu_custom_call" | custom-call | flops 1000 | bytes 1000 | tf_op jit(solution)/shard_map/updates/pallas_call | solution.py:305
  83.9 1.9 %collective-permute-start.5 = (bf16[288,1280]{1,0:T(8,128)(2,1)S(1)}, bf16[288,1280]{1,0:T(8,128)(2,1)S(1)}, u32[]{:S(2)}, u32[]{:S(2)}) collective-permute-start(bf16[288,1280]{1,0:T(8,128)(2,1)S(1)} %get-tuple-element.38), channel_id=1, source_target_pairs={{0,1},{1,0},{2,3},{3,2},{4,5},{5,4},{6,7},{7,6},{8,9},{9,8},{10,11... | collective-permute-start | bytes 2211848 | tf_op jit(solution)/shard_map/ppermute | solution.py:406
  85.8 2.2 %collective-permute-done.5.refs_1_ = bf16[288,1280]{1,0:T(8,128)(2,1)S(1)} collective-permute-done((bf16[288,1280]{1,0:T(8,128)(2,1)S(1)}, bf16[288,1280]{1,0:T(8,128)(2,1)S(1)}, u32[]{:S(2)}, u32[]{:S(2)}) %collective-permute-start.5) | collective-permute-done | bytes 737312 | tf_op jit(solution)/shard_map/ppermute | solution.py:406
  88.0 1.7 %add_updates.1 = bf16[288,1280]{1,0:T(8,128)(2,1)} custom-call(bf16[2,288,1280]{2,1,0:T(8,128)(2,1)S(1)} %get-tuple-element.37.refs_0_, bf16[288,1280]{1,0:T(8,128)(2,1)S(1)} %collective-permute-done.5.refs_1_), custom_call_target="tpu_custom_call" | custom-call | flops 1000 | bytes 1000 | tf_op jit(solution)/shard_map/add_updates/pallas_call | solution.py:305
  89.8 3.2 %collective-permute-start.7 = (bf16[288,1280]{1,0:T(8,128)(2,1)}, bf16[288,1280]{1,0:T(8,128)(2,1)S(1)}, u32[]{:S(2)}, u32[]{:S(2)}) collective-permute-start(bf16[288,1280]{1,0:T(8,128)(2,1)} %add_updates.1), channel_id=1, source_target_pairs={{0,8},{1,9},{2,10},{3,11},{4,12},{5,13},{6,14},{7,15},{8,0},{9,1},... | collective-permute-start | bytes 2211848 | tf_op jit(solution)/shard_map/ppermute | solution.py:409
  93.0 2.1 %collective-permute-start.6 = (bf16[288,1280]{1,0:T(8,128)(2,1)}, bf16[288,1280]{1,0:T(8,128)(2,1)S(1)}, u32[]{:S(2)}, u32[]{:S(2)}) collective-permute-start(bf16[288,1280]{1,0:T(8,128)(2,1)} %get-tuple-element.40), channel_id=1, source_target_pairs={{0,1},{1,0},{2,3},{3,2},{4,5},{5,4},{6,7},{7,6},{8,9},{9,8},{10,11... | collective-permute-start | bytes 2211848 | tf_op jit(solution)/shard_map/ppermute | solution.py:407
  95.1 1.8 %sum_weight_grads.1 = bf16[640,128]{1,0:T(8,128)(2,1)S(1)} custom-call(bf16[8,128,640]{2,1,0:T(8,128)(2,1)} %all-to-all-done.3.refs_0_), custom_call_target="tpu_custom_call" | custom-call | flops 1000 | bytes 1000 | tf_op jit(solution)/shard_map/sum_weight_grads/pallas_call | solution.py:305
  97.5 15.2 %all-to-all-start.4 = ((bf16[16,40,128]{2,1,0:T(8,128)(2,1)}), bf16[16,40,128]{2,1,0:T(8,128)(2,1)S(1)}, u32[]{:S(2)}, u32[]{:S(2)}) async-start(bf16[16,40,128]{2,1,0:T(8,128)(2,1)} %bitcast.10), calls=%async_computation.4 | async-start | bytes 327680 | tf_op jit(solution)/shard_map/all_to_all | solution.py:415
  112.8 3.0 %final_rows.1 = (bf16[128,1280]{1,0:T(8,128)(2,1)}, bf16[128,1280]{1,0:T(8,128)(2,1)}, bf16[1,32,1280]{2,1,0:T(8,128)(2,1)}) custom-call(bf16[2,288,1280]{2,1,0:T(8,128)(2,1)S(1)} %copy-done.5, bf16[288,1280]{1,0:T(8,128)(2,1)S(1)} %collective-permute-done.6.refs_1_, bf16[288,1280]{1,0:T(8,128)(2,1)S(1)} %collective-permute-done.7.refs_2_, ...), custom_call_target="tpu_custom_call" | custom-call | flops 1000 | bytes 1000 | tf_op jit(solution)/shard_map/final_rows/pallas_call | solution.py:305
  115.8 12.4 %all-to-all-done.4.parts_ref = bf16[16,40,128]{2,1,0:T(8,128)(2,1)S(1)} async-done(((bf16[16,40,128]{2,1,0:T(8,128)(2,1)}), bf16[16,40,128]{2,1,0:T(8,128)(2,1)S(1)}, u32[]{:S(2)}, u32[]{:S(2)}) %all-to-all-start.4) | async-done | bytes 163872 | tf_op jit(solution)/shard_map/all_to_all | solution.py:415
  (51 shorter events, 3.2 us)
Async XLA Ops:
  3.0 4.6 %copy-start.6 = (bf16[128,1280]{1,0:T(8,128)(2,1)S(1)}, bf16[128,1280]{1,0:T(8,128)(2,1)}, u32[]{:S(2)}) copy-start(bf16[128,1280]{1,0:T(8,128)(2,1)} %refs_3_.1) | copy-start | bytes 983044
  3.0 4.6 %copy-start.18 = (bf16[128,1280]{1,0:T(8,128)(2,1)S(1)}, bf16[128,1280]{1,0:T(8,128)(2,1)}, u32[]{:S(2)}) copy-start(bf16[128,1280]{1,0:T(8,128)(2,1)} %param.25) | copy-start | bytes 983044
  3.0 26.0 %all-to-all-start = ((bf16[4,160,1280]{2,1,0:T(8,128)(2,1)}), bf16[4,160,1280]{2,1,0:T(8,128)(2,1)S(1)}, u32[]{:S(2)}, u32[]{:S(2)}) async-start(bf16[4,160,1280]{2,1,0:T(8,128)(2,1)} %pack_keys_values.1), calls=%async_computation | async-start | bytes 3276800 | tf_op jit(solution)/shard_map/all_to_all | solution.py:353
  8.6 28.8 %collective-permute-start = (bf16[2,128,1280]{2,1,0:T(8,128)(2,1)}, bf16[2,128,1280]{2,1,0:T(8,128)(2,1)}, u32[]{:S(2)}, u32[]{:S(2)}) collective-permute-start(bf16[2,128,1280]{2,1,0:T(8,128)(2,1)} %pad_maximum_fusion.refs_1_), channel_id=1, source_target_pairs={{0,8},{1,9},{2,10},{3,11},{4,12},{5,13},{6,14},{7,15},{8,0},{9,1},... | collective-permute-start | bytes 1966088 | tf_op jit(solution)/shard_map/ppermute | solution.py:363
  29.1 2.8 %copy-start = (bf16[4,160,1280]{2,1,0:T(8,128)(2,1)}, bf16[4,160,1280]{2,1,0:T(8,128)(2,1)S(1)}, u32[]{:S(2)}) copy-start(bf16[4,160,1280]{2,1,0:T(8,128)(2,1)S(1)} %all-to-all-done.refs_3_.refs_4_) | copy-start | bytes 4915204
  29.1 10.7 %collective-permute-start.3 = (bf16[4,32,1280]{2,1,0:T(8,128)(2,1)S(1)}, bf16[4,32,1280]{2,1,0:T(8,128)(2,1)}, u32[]{:S(2)}, u32[]{:S(2)}) collective-permute-start(bf16[4,32,1280]{2,1,0:T(8,128)(2,1)S(1)} %slice.3), channel_id=1, source_target_pairs={{0,8},{1,9},{2,10},{3,11},{4,12},{5,13},{6,14},{7,15},{8,0},{9,1},... | collective-permute-start | bytes 983048 | tf_op jit(solution)/shard_map/ppermute | solution.py:360
  31.9 20.2 %all-to-all-start.1 = ((bf16[4,128,1280]{2,1,0:T(8,128)(2,1)}), bf16[4,128,1280]{2,1,0:T(8,128)(2,1)S(1)}, u32[]{:S(2)}, u32[]{:S(2)}) async-start(bf16[4,128,1280]{2,1,0:T(8,128)(2,1)} %pack_queries_out.1), calls=%async_computation.1 | async-start | bytes 2621440 | tf_op jit(solution)/shard_map/all_to_all | solution.py:358
  35.4 7.4 %copy-start.19 = (s32[1,16]{1,0:T(1,128)S(1)}, s32[1,16]{1,0:T(1,128)}, u32[]{:S(2)}) copy-start(s32[1,16]{1,0:T(1,128)} %param.16) | copy-start | bytes 196
  35.4 7.4 %copy-start.20 = (s32[16]{0:T(128)S(1)}, s32[16]{0:T(128)}, u32[]{:S(2)}) copy-start(s32[16]{0:T(128)} %param.15) | copy-start | bytes 196
  35.4 8.0 %collective-permute-start.1 = (bf16[2,128,1280]{2,1,0:T(8,128)(2,1)}, bf16[2,128,1280]{2,1,0:T(8,128)(2,1)S(1)}, u32[]{:S(2)}, u32[]{:S(2)}) collective-permute-start(bf16[2,128,1280]{2,1,0:T(8,128)(2,1)} %pad_maximum_fusion.refs_1_), channel_id=1, source_target_pairs={{0,1},{1,0},{2,3},{3,2},{4,5},{5,4},{6,7},{7,6},{8,9},{9,8},{10,11... | collective-permute-start | bytes 1966088 | tf_op jit(solution)/shard_map/ppermute | solution.py:364
  37.4 6.0 %collective-permute-start.2 = (bf16[2,128,1280]{2,1,0:T(8,128)(2,1)}, bf16[2,128,1280]{2,1,0:T(8,128)(2,1)}, u32[]{:S(2)}, u32[]{:S(2)}) collective-permute-start(bf16[2,128,1280]{2,1,0:T(8,128)(2,1)} %collective-permute-done.refs_2_), channel_id=1, source_target_pairs={{0,1},{1,0},{2,3},{3,2},{4,5},{5,4},{6,7},{7,6},{8,9},{9,8},{10,11... | collective-permute-start | bytes 1966088 | tf_op jit(solution)/shard_map/ppermute | solution.py:365
  40.8 8.0 %copy-start.15 = (bf16[8,32,1280]{2,1,0:T(8,128)(2,1)}, bf16[8,32,1280]{2,1,0:T(8,128)(2,1)S(1)}, u32[]{:S(2)}) copy-start(bf16[8,32,1280]{2,1,0:T(8,128)(2,1)S(1)} %pad_maximum_fusion.1.refs_7_) | copy-start | bytes 1966084
  40.8 11.2 %collective-permute-start.4 = (bf16[8,32,1280]{2,1,0:T(8,128)(2,1)S(1)}, bf16[8,32,1280]{2,1,0:T(8,128)(2,1)S(1)}, u32[]{:S(2)}, u32[]{:S(2)}) collective-permute-start(bf16[8,32,1280]{2,1,0:T(8,128)(2,1)S(1)} %pad_maximum_fusion.1.refs_7_), channel_id=1, source_target_pairs={{0,1},{1,0},{2,3},{3,2},{4,5},{5,4},{6,7},{7,6},{8,9},{9,8},{10,11... | collective-permute-start | bytes 1966088 | tf_op jit(solution)/shard_map/ppermute | solution.py:361
  52.1 1.1 copy-start.2
  52.1 1.3 copy-start.17
  61.8 11.8 %all-to-all-start.2 = ((bf16[4,2,4,32,256]{4,3,2,1,0:T(8,128)(2,1)}), bf16[4,2,4,32,256]{4,3,2,1,0:T(8,128)(2,1)S(1)}, u32[]{:S(2)}, u32[]{:S(2)}) async-start(bf16[4,2,4,32,256]{4,3,2,1,0:T(8,128)(2,1)} %get-tuple-element.34), calls=%async_computation.2 | async-start | bytes 1048576 | tf_op jit(solution)/shard_map/all_to_all | solution.py:386
  65.3 13.7 %copy-start.3 = (bf16[4,128,1280]{2,1,0:T(8,128)(2,1)S(1)}, bf16[4,128,1280]{2,1,0:T(8,128)(2,1)}, u32[]{:S(2)}) copy-start(bf16[4,128,1280]{2,1,0:T(8,128)(2,1)} %copy-done.2) | copy-start | bytes 3932164
  69.4 9.6 %copy-start.1 = (bf16[4,160,1280]{2,1,0:T(8,128)(2,1)S(1)}, bf16[4,160,1280]{2,1,0:T(8,128)(2,1)}, u32[]{:S(2)}) copy-start(bf16[4,160,1280]{2,1,0:T(8,128)(2,1)} %copy-done) | copy-start | bytes 4915204
  69.4 9.6 %copy-start.14 = (s32[128]{0:T(128)S(1)}, s32[128]{0:T(128)}, u32[]{:S(2)}) copy-start(s32[128]{0:T(128)} %pad_add_fusion.refs_0_) | copy-start | bytes 1540
  73.5 21.5 %all-to-all-start.3 = ((bf16[8,128,640]{2,1,0:T(8,128)(2,1)}), bf16[8,128,640]{2,1,0:T(8,128)(2,1)}, u32[]{:S(2)}, u32[]{:S(2)}) async-start(bf16[8,128,640]{2,1,0:T(8,128)(2,1)} %weight_grads.1), calls=%async_computation.3 | async-start | bytes 2621440 | tf_op jit(solution)/shard_map/all_to_all | solution.py:395
  79.0 1.0 copy-start.8
  80.0 0.9 copy-start.9
  83.9 5.8 %copy-start.4 = (bf16[2,288,1280]{2,1,0:T(8,128)(2,1)}, bf16[2,288,1280]{2,1,0:T(8,128)(2,1)S(1)}, u32[]{:S(2)}) copy-start(bf16[2,288,1280]{2,1,0:T(8,128)(2,1)S(1)} %get-tuple-element.37.refs_0_) | copy-start | bytes 4423684
  83.9 4.1 %collective-permute-start.5 = (bf16[288,1280]{1,0:T(8,128)(2,1)S(1)}, bf16[288,1280]{1,0:T(8,128)(2,1)S(1)}, u32[]{:S(2)}, u32[]{:S(2)}) collective-permute-start(bf16[288,1280]{1,0:T(8,128)(2,1)S(1)} %get-tuple-element.38), channel_id=1, source_target_pairs={{0,1},{1,0},{2,3},{3,2},{4,5},{5,4},{6,7},{7,6},{8,9},{9,8},{10,11... | collective-permute-start | bytes 2211848 | tf_op jit(solution)/shard_map/ppermute | solution.py:406
  88.0 24.7 %copy-start.11 = (bf16[1,32,1280]{2,1,0:T(8,128)(2,1)S(1)}, bf16[1,32,1280]{2,1,0:T(8,128)(2,1)}, u32[]{:S(2)}) copy-start(bf16[1,32,1280]{2,1,0:T(8,128)(2,1)} %refs_5_.3) | copy-start | bytes 245764
  88.0 24.8 %copy-start.12 = (f32[1280]{0:T(1024)S(1)}, f32[1280]{0:T(1024)}, u32[]{:S(2)}) copy-start(f32[1280]{0:T(1024)} %refs_6_.3) | copy-start | bytes 15364
  88.0 24.8 %copy-start.13 = (f32[1280]{0:T(1024)S(1)}, f32[1280]{0:T(1024)}, u32[]{:S(2)}) copy-start(f32[1280]{0:T(1024)} %refs_4_.1) | copy-start | bytes 15364
  89.8 23.0 %copy-start.7 = (bf16[128,1280]{1,0:T(8,128)(2,1)S(1)}, bf16[128,1280]{1,0:T(8,128)(2,1)}, u32[]{:S(2)}) copy-start(bf16[128,1280]{1,0:T(8,128)(2,1)} %refs_3_.1) | copy-start | bytes 983044
  89.8 23.0 %collective-permute-start.7 = (bf16[288,1280]{1,0:T(8,128)(2,1)}, bf16[288,1280]{1,0:T(8,128)(2,1)S(1)}, u32[]{:S(2)}, u32[]{:S(2)}) collective-permute-start(bf16[288,1280]{1,0:T(8,128)(2,1)} %add_updates.1), channel_id=1, source_target_pairs={{0,8},{1,9},{2,10},{3,11},{4,12},{5,13},{6,14},{7,15},{8,0},{9,1},... | collective-permute-start | bytes 2211848 | tf_op jit(solution)/shard_map/ppermute | solution.py:409
  93.0 19.8 %copy-start.5 = (bf16[2,288,1280]{2,1,0:T(8,128)(2,1)S(1)}, bf16[2,288,1280]{2,1,0:T(8,128)(2,1)}, u32[]{:S(2)}) copy-start(bf16[2,288,1280]{2,1,0:T(8,128)(2,1)} %copy-done.4) | copy-start | bytes 4423684
  93.0 19.7 %collective-permute-start.6 = (bf16[288,1280]{1,0:T(8,128)(2,1)}, bf16[288,1280]{1,0:T(8,128)(2,1)S(1)}, u32[]{:S(2)}, u32[]{:S(2)}) collective-permute-start(bf16[288,1280]{1,0:T(8,128)(2,1)} %get-tuple-element.40), channel_id=1, source_target_pairs={{0,1},{1,0},{2,3},{3,2},{4,5},{5,4},{6,7},{7,6},{8,9},{9,8},{10,11... | collective-permute-start | bytes 2211848 | tf_op jit(solution)/shard_map/ppermute | solution.py:407
  97.5 30.6 %all-to-all-start.4 = ((bf16[16,40,128]{2,1,0:T(8,128)(2,1)}), bf16[16,40,128]{2,1,0:T(8,128)(2,1)S(1)}, u32[]{:S(2)}, u32[]{:S(2)}) async-start(bf16[16,40,128]{2,1,0:T(8,128)(2,1)} %bitcast.10), calls=%async_computation.4 | async-start | bytes 327680 | tf_op jit(solution)/shard_map/all_to_all | solution.py:415
  (2 other events, 1.6 us)

commit v3 on v2

--- a/solution.py
+++ b/solution.py
@@ -70,28 +70,51 @@
     return rows.reshape(WIDTH, w_ref.shape[2])
 
 
-def pack_kernel(io, *refs):
-    *blocks, out_ref = refs
-    io.take()
-    first = 0
-    for block in blocks:
+def pack_kernel(*refs):
+    count = len(refs) // 2 - 1
+    blocks, out_ref, held, sems = refs[:count], refs[count], refs[count + 1 : -1], refs[-1]
+    copies = [pltpu.make_async_copy(block, here, sems.at[k, HELD]) for k, (block, here) in enumerate(zip(blocks, held))]
+    for copy in copies:
+        copy.start()
+    sent, first = [], 0
+    for k, here in enumerate(held):
+        copies[k].wait()
         for target in range(HELD):
-            out_ref[target, first : first + block.shape[0], :] = block[...]
-        first += block.shape[0]
-
-
-def norm_kernel(io, meta, t0, t1, t2, t3, gain, bias, hid_ref, up_ref):
+            place = out_ref.at[target, pl.ds(first, here.shape[0])]
+            sent.append(pltpu.make_async_copy(here, place, sems.at[k, target]))
+            sent[-1].start()
+        first += here.shape[0]
+    for copy in sent:
+        copy.wait()
+
+
+def pack(name, *blocks):
+    rows = sum(block.shape[0] for block in blocks)
+    return pl.pallas_call(
+        pack_kernel,
+        out_shape=jax.ShapeDtypeStruct((HELD, rows, blocks[0].shape[1]), BF16),
+        in_specs=[HBM] * len(blocks),
+        out_specs=HBM,
+        scratch_shapes=[pltpu.VMEM(block.shape, BF16) for block in blocks]
+        + [pltpu.SemaphoreType.DMA((len(blocks), HELD + 1))],
+        compiler_params=params(BIG),
+        cost_estimate=COST,
+        name=name,
+    )(*blocks)
+
+
+def norm_kernel(first, io, meta, t0, t1, gain, bias, hid_ref, up_ref):
     width = hid_ref.shape[1]
-    io.take(0, 5, 6)
+    io.take(0, 3, 4)
     own = meta[0]
     positions = lax.broadcasted_iota(jnp.int32, (CAP, 1), 0)
     gain_row, bias_row = gain[...].reshape(1, width), bias[...].reshape(1, width)
-    for part, tokens in enumerate((t0, t1, t2, t3)):
-        io.take(1 + part)
-        span = slice(part * CAP, (part + 1) * CAP)
+    for place, tokens in enumerate((t0, t1)):
+        io.take(1 + place)
+        span = slice(place * CAP, (place + 1) * CAP)
         normed, _ = standardize(tokens[0].astype(F32))
         hid_ref[span, :] = (normed * gain_row + bias_row).astype(BF16)
-        live = positions < caption_length(meta, held_caption(own, part))
+        live = positions < caption_length(meta, held_caption(own, first + 2 * place))
         up_ref[span, :] = jnp.where(live, tokens[1].astype(F32), 0.0).astype(BF16)
 
 
@@ -101,24 +124,9 @@
     return dot(high, ones) + dot(low, ones)
 
 
-def attend_kernel(
-    io,
-    meta,
-    gain,
-    bias,
-    kv_ref,
-    qo_ref,
-    hid_ref,
-    up_ref,
-    near_ref,
-    other_ref,
-    dkv_ref,
-    att_ref,
-    dq_ref,
-    states_ref,
-):
-    width = hid_ref.shape[1]
-    io.take(0, 1, 2, 7, 8)
+def key_value_kernel(io, meta, gain, bias, kv_ref, near_ref, other_ref, out_ref, states_ref):
+    width = states_ref.shape[1]
+    io.take(0, 1, 2, 4, 5)
     own = meta[0]
     gain_row, bias_row = gain[...].reshape(1, width), bias[...].reshape(1, width)
     for part in range(HELD):
@@ -129,11 +137,18 @@
         normed, _ = standardize(frames)
         states_ref[part * FRAMES : (part + 1) * FRAMES, :] = (normed * gain_row + bias_row).astype(BF16)
     io.take(3)
-    keys = dot(states_ref[...], weight_of(kv_ref, 0), 1, 1).astype(BF16)
-    values = dot(states_ref[...], weight_of(kv_ref, 1), 1, 1).astype(BF16)
-    io.take(4, 5, 6)
-    queries = dot(hid_ref[...], weight_of(qo_ref, 0), 1, 1).astype(BF16)
-    d_attended = dot(up_ref[...], weight_of(qo_ref, 1), 1, 1).astype(BF16)
+    for kind in range(2):
+        out_ref[kind] = dot(states_ref[...], weight_of(kv_ref, kind), 1, 1).astype(BF16)
+
+
+def join(target, near, far):
+    for place in range(2):
+        rows = slice(place * CAP, (place + 1) * CAP)
+        target[2 * place * CAP : (2 * place + 1) * CAP, :] = near[rows, :]
+        target[(2 * place + 1) * CAP : (2 * place + 2) * CAP, :] = far[rows, :]
+
+
+def attend_kernel(io, kv_ref, qo_ref, h0, u0, h1, u1, dkv_ref, rows_ref, hid_ref, up_ref):
     scale = 1.0 / math.sqrt(HEAD_DIM)
     pairs = HELD * FRAMES
     row_head = lax.broadcasted_iota(jnp.int32, (pairs, WIDTH), 0) // FRAMES
@@ -142,6 +157,8 @@
     first = lax.broadcasted_iota(jnp.int32, (pairs, pairs), 0) // FRAMES
     second = lax.broadcasted_iota(jnp.int32, (pairs, pairs), 1) // FRAMES
     ones = jnp.where(first == second, 1.0, 0.0).astype(BF16)
+    parts = range(HELD)
+    spans = [slice(part * CAP, (part + 1) * CAP) for part in parts]
 
     def spread(rows):
         repeated = jnp.concatenate([rows.astype(F32)] * HELD, axis=0)
@@ -154,41 +171,74 @@
             total = total + kept[head * FRAMES : (head + 1) * FRAMES]
         return total.astype(BF16)
 
-    for part in range(HELD):
-        span = slice(part * CAP, (part + 1) * CAP)
-        frames = slice(part * FRAMES, (part + 1) * FRAMES)
-        key_block, value_block = spread(keys[frames]), spread(values[frames])
-        query = queries[span]
-        d_att = d_attended[span]
-        weights = jnp.exp(dot(query, key_block, 1, 1) * scale)
-        softmax = weights / segment_sum(weights, ones)
-        low = softmax.astype(BF16)
-        att_ref[span, :] = dot(low, value_block).astype(BF16)
-        d_softmax = dot(d_att, value_block, 1, 1)
-        inner = segment_sum(softmax * d_softmax, ones)
-        d_scores = (softmax * (d_softmax - inner) * scale).astype(BF16)
-        dq_ref[span, :] = dot(d_scores, key_block).astype(BF16)
-        d_keys = collect(dot(d_scores, query, 0, 0))
-        d_values = collect(dot(low, d_att, 0, 0))
-        for row in range(HELD):
-            dkv_ref[row, 0, part] = d_keys
-            dkv_ref[row, 1, part] = d_values
-
-
-def weight_grad_kernel(io, att_ref, dq_ref, hid_ref, up_ref, grad_ref):
-    io.take()
+    io.take(0)
+    blocks = [[spread(kv_ref[kind, part * FRAMES : (part + 1) * FRAMES]) for part in parts] for kind in range(2)]
+    keys, values = blocks
+    io.take(1, 2, 4)
+    join(hid_ref, h0, h1)
+    queries = dot(hid_ref[...], weight_of(qo_ref, 0), 1, 1).astype(BF16)
+    query = [queries[span] for span in spans]
+    io.take(3, 5)
+    join(up_ref, u0, u1)
+    d_attended = dot(up_ref[...], weight_of(qo_ref, 1), 1, 1).astype(BF16)
+    d_att = [d_attended[span] for span in spans]
+    weights = [jnp.exp(dot(query[part], keys[part], 1, 1) * scale) for part in parts]
+    d_softmax = [dot(d_att[part], values[part], 1, 1) for part in parts]
+    sums = [segment_sum(weights[part], ones) for part in parts]
+    softmax = [weights[part] / sums[part] for part in parts]
+    low = [softmax[part].astype(BF16) for part in parts]
+    inner = [segment_sum(softmax[part] * d_softmax[part], ones) for part in parts]
+    d_values = [dot(low[part], d_att[part], 0, 0) for part in parts]
+    d_scores = [(softmax[part] * (d_softmax[part] - inner[part]) * scale).astype(BF16) for part in parts]
+    d_keys = [dot(d_scores[part], query[part], 0, 0) for part in parts]
+    for kind, found in enumerate((d_keys, d_values)):
+        for part in parts:
+            block = collect(found[part])
+            for row in range(HELD):
+                dkv_ref[row, kind, part] = block
+    io.give(0)
+    for part in parts:
+        rows_ref[0, spans[part], :] = dot(low[part], values[part]).astype(BF16)
+        rows_ref[1, spans[part], :] = dot(d_scores[part], keys[part]).astype(BF16)
+
+
+def product_kernel(
+    io, rows_ref, h0, u0, h1, u1, qo_ref, grad_ref, send_x, send_own, keep_ref, hid_ref, up_ref
+):
+    io.take(0, 1, 2, 3, 4)
+    join(hid_ref, h0, h1)
+    join(up_ref, u0, u1)
     half = hid_ref.shape[1] // 2
-    for kind, (left, right) in enumerate(((dq_ref, hid_ref), (att_ref, up_ref))):
+    for kind, right in enumerate((hid_ref, up_ref)):
         for side in range(2):
-            product = dot(left[...], right[:, side * half : (side + 1) * half], 0, 0).astype(BF16)
+            product = dot(rows_ref[1 - kind], right[:, side * half : (side + 1) * half], 0, 0).astype(BF16)
             for head in range(HELD):
                 grad_ref[side * HELD + head, kind * HEAD_DIM : (kind + 1) * HEAD_DIM, :] = product[
                     head * HEAD_DIM : (head + 1) * HEAD_DIM
                 ]
-
-
-def update_kernel(io, meta, got_ref, att_ref, dq_ref, kv_ref, qo_ref, send_x, send_own, keep_ref, keys_ref, values_ref):
-    io.take()
+    io.give(0)
+    io.take(5)
+    w_query, w_out = weight_of(qo_ref, 0), weight_of(qo_ref, 1)
+    for part in range(HELD):
+        target = (keep_ref.at[0], keep_ref.at[1], send_own, send_x)[part]
+        span = slice(part * CAP, (part + 1) * CAP)
+        target[:CAP, :] = dot(rows_ref[0, span], w_out).astype(BF16)
+        target[CAP : 2 * CAP, :] = dot(rows_ref[1, span], w_query).astype(BF16)
+        target[2 * CAP :, :] = jnp.zeros((FRAMES, target.shape[1]), BF16)
+
+
+def state_kernel(
+    meta_in, got_in, kv_in, x_in, own_in, keep_in, x_out, own_out, keep_out, meta, got_ref, kv_ref, made, sems, keys_ref, values_ref
+):
+    del x_in, own_in, keep_in
+    copies = [
+        pltpu.make_async_copy(source, target, sems.at[place])
+        for place, (source, target) in enumerate(((meta_in, meta), (got_in, got_ref), (kv_in, kv_ref)))
+    ]
+    for copy in copies:
+        copy.start()
+    for copy in copies:
+        copy.wait()
     own = meta[0]
     for part in range(HELD):
         clip = held_caption(own, part)
@@ -200,16 +250,17 @@
         place = (apart >> 3) + 2 * (apart & 1)
         keys_ref[part * FRAMES : (part + 1) * FRAMES, :] = got_ref[row, 0, place]
         values_ref[part * FRAMES : (part + 1) * FRAMES, :] = got_ref[row, 1, place]
-    w_query, w_out = weight_of(qo_ref, 0), weight_of(qo_ref, 1)
-    d_states = dot(keys_ref[...], weight_of(kv_ref, 0)) + dot(values_ref[...], weight_of(kv_ref, 1))
-    for part in reversed(range(HELD)):
-        target = (keep_ref.at[0], keep_ref.at[1], send_own, send_x)[part]
-        span = slice(part * CAP, (part + 1) * CAP)
-        target[:CAP, :] = dot(att_ref[span, :], w_out).astype(BF16)
-        target[CAP : 2 * CAP, :] = dot(dq_ref[span, :], w_query).astype(BF16)
-        target[2 * CAP :, :] = d_states[part * FRAMES : (part + 1) * FRAMES].astype(BF16)
-        if part > 1:
-            io.give(3 - part)
+    total = dot(keys_ref[...], weight_of(kv_ref, 0)) + dot(values_ref[...], weight_of(kv_ref, 1))
+    copies = []
+    for part in range(HELD):
+        made[part] = total[part * FRAMES : (part + 1) * FRAMES].astype(BF16)
+        target = (keep_out.at[0], keep_out.at[1], own_out, x_out)[part]
+        copies.append(
+            pltpu.make_async_copy(made.at[part], target.at[pl.ds(2 * CAP, FRAMES)], sems.at[3 + part])
+        )
+        copies[-1].start()
+    for copy in copies:
+        copy.wait()
 
 
 def grad_sum_kernel(io, parts_ref, out_ref):
@@ -344,65 +395,80 @@
     swap_core = [(index, index ^ 1) for index in range(16)]
     swap_x = [(index, index ^ 8) for index in range(16)]
 
-    (kv_out,) = call(
-        pack_kernel,
-        "pack_keys_values",
-        [((HELD, 2 * HEAD_DIM + FRAMES, width), BF16)],
-        (w_key.T, w_value.T, (audio, 0)),
-    )
+    kv_out = pack("pack_keys_values", w_key.T, w_value.T, audio.reshape(FRAMES, width))
     kv_got = lax.all_to_all(kv_out, "mp", 0, 0, axis_index_groups=y_groups, tiled=True)
-    (qo_out,) = call(
-        pack_kernel, "pack_queries_out", [((HELD, 2 * HEAD_DIM, width), BF16)], (w_query.T, w_out)
-    )
-    kv_got, qo_out = lax.optimization_barrier((kv_got, qo_out))
+    qo_out = pack("pack_queries_out", w_query.T, w_out)
+    tokens_own = jnp.stack([captions, grad_update])
+    tokens_x = lax.ppermute(tokens_own, "mp", swap_x)
+    tokens_core = lax.ppermute(tokens_own, "mp", swap_core)
+
+    def norms(first, name, near, other):
+        return call(
+            functools.partial(norm_kernel, first),
+            name,
+            [((2 * CAP, width), BF16), ((2 * CAP, width), BF16)],
+            (meta, near, other, dec_gain, dec_bias),
+            scalars=1,
+        )
+
+    normed_near = norms(0, "norms_near", tokens_own, tokens_core)
+    kv_got, qo_out, *normed_near = lax.optimization_barrier((kv_got, qo_out, *normed_near))
     qo_got = lax.all_to_all(qo_out, "mp", 0, 0, axis_index_groups=y_groups, tiled=True)
     audio_y = kv_got[:, 2 * HEAD_DIM :]
     audio_near = jnp.concatenate([audio_y, lax.ppermute(audio_y, "mp", swap_x)])
     audio_other = lax.ppermute(audio_near, "mp", swap_core)
-    tokens_own = jnp.stack([captions, grad_update])
-    tokens_x = lax.ppermute(tokens_own, "mp", swap_x)
-    tokens_core = lax.ppermute(tokens_own, "mp", swap_core)
+    (keys_values,) = call(
+        key_value_kernel,
+        "keys_values",
+        [((2, HELD * FRAMES, WIDTH), BF16)],
+        (meta, enc_gain, enc_bias, kv_got, audio_near, audio_other),
+        scratch=[pltpu.VMEM((HELD * FRAMES, width), BF16)],
+        scalars=1,
+    )
     tokens_far = lax.ppermute(tokens_x, "mp", swap_core)
-    hidden, upstream = call(
-        norm_kernel,
-        "norms",
-        [((ROWS, width), BF16), ((ROWS, width), BF16)],
-        (meta, tokens_own, tokens_x, tokens_core, tokens_far, dec_gain, dec_bias),
-        scalars=1,
-    )
-
-    d_kv, attended, d_queries = call(
+    normed_far = norms(1, "norms_far", tokens_x, tokens_far)
+
+    d_kv, attended = call(
         attend_kernel,
         "attend",
+        [((HELD, 2, HELD, FRAMES, WIDTH), BF16), ((2, ROWS, WIDTH), BF16)],
+        (keys_values, qo_got, *normed_near, *normed_far),
+        scratch=[pltpu.VMEM((ROWS, width), BF16)] * 2,
+    )
+    d_kv_got = lax.all_to_all(d_kv, "mp", 0, 0, axis_index_groups=y_groups, tiled=True)
+    rows = 2 * CAP + FRAMES
+    weight_parts, send_x, send_own, keep = call(
+        product_kernel,
+        "products",
         [
-            ((HELD, 2, HELD, FRAMES, WIDTH), BF16),
-            ((ROWS, WIDTH), BF16),
-            ((ROWS, WIDTH), BF16),
+            ((2 * HELD, 2 * HEAD_DIM, width // 2), BF16),
+            ((rows, width), BF16),
+            ((rows, width), BF16),
+            ((2, rows, width), BF16),
         ],
-        (meta, enc_gain, enc_bias, kv_got, qo_got, hidden, upstream, audio_near, audio_other),
-        scratch=[pltpu.VMEM((HELD * FRAMES, width), BF16)],
-        scalars=1,
-    )
-    d_kv_got = lax.all_to_all(d_kv, "mp", 0, 0, axis_index_groups=y_groups, tiled=True)
-    (weight_parts,) = call(
-        weight_grad_kernel,
-        "weight_grads",
-        [((2 * HELD, 2 * HEAD_DIM, width // 2), BF16)],
-        (attended, d_queries, hidden, upstream),
-    )
-    weight_parts, d_kv_got = lax.optimization_barrier((weight_parts, d_kv_got))
-
+        (attended, *normed_near, *normed_far, qo_got),
+        scratch=[pltpu.VMEM((ROWS, width), BF16)] * 2,
+    )
+    d_kv_got, weight_parts = lax.optimization_barrier((d_kv_got, weight_parts))
     weight_got = lax.all_to_all(weight_parts, both, 0, 0, axis_index_groups=yx_groups, tiled=True)
-    rows = 2 * CAP + FRAMES
-    send_x, send_own, keep = call(
-        update_kernel,
-        "updates",
-        [((rows, width), BF16), ((rows, width), BF16), ((2, rows, width), BF16)],
-        (meta, d_kv_got, attended, d_queries, kv_got, qo_got),
-        mib=24,
-        scratch=[pltpu.VMEM((HELD * FRAMES, WIDTH), BF16), pltpu.VMEM((HELD * FRAMES, WIDTH), BF16)],
-        scalars=1,
-    )
+    send_x, send_own, keep = pl.pallas_call(
+        state_kernel,
+        out_shape=tuple(jax.ShapeDtypeStruct(array.shape, BF16) for array in (send_x, send_own, keep)),
+        in_specs=[HBM] * 6,
+        out_specs=(HBM,) * 3,
+        input_output_aliases={3: 0, 4: 1, 5: 2},
+        scratch_shapes=[
+            pltpu.SMEM(meta.shape, meta.dtype),
+            pltpu.VMEM(d_kv_got.shape, BF16),
+            pltpu.VMEM(kv_got.shape, BF16),
+            pltpu.VMEM((HELD, FRAMES, width), BF16),
+            pltpu.SemaphoreType.DMA((3 + HELD,)),
+        ]
+        + [pltpu.VMEM((HELD * FRAMES, WIDTH), BF16)] * 2,
+        compiler_params=params(BIG),
+        cost_estimate=COST,
+        name="state_grads",
+    )(meta, d_kv_got, kv_got, send_x, send_own, keep)
     core_x = lax.ppermute(send_x, "mp", swap_core)
     core_own = lax.ppermute(send_own, "mp", swap_core)
     (x_out,) = call(add_kernel, "add_updates", [((rows, width), BF16)], ((keep, 1), core_x), mib=8)

time: 130 us -> 124 us (0.954)
  waiting for transfers between devices: 37.5 us -> 31.9 us
  Pallas kernels: 31.7 us -> 33.8 us
  other arithmetic: 2.53 us -> 0.71 us
    pallas_call x0 -> x3, Pallas kernels: none -> 7.02 us  [the longest x2 4.32 us: pack(): pl.pallas_call(pack_kernel, out_shape=jax.ShapeDtypeStruct((HELD, rows, b...]
    all_to_all x1, waiting for transfers between devices: 15.6 us -> 10.1 us  [body(): lax.all_to_all(kv_out, 'mp', 0, 0, axis_index_groups=y_groups, tiled=True)]
    pallas_call x9 -> x8, Pallas kernels: 31 us -> 26.1 us  [call(): pl.pallas_call(copied, out_shape=tuple((jax.ShapeDtypeStruct(*out) for ou...]
    all_to_all x1, waiting for transfers between devices: 4.13 us -> 2.67 us  [body(): lax.all_to_all(d_kv, 'mp', 0, 0, axis_index_groups=y_groups, tiled=True)]
    unnamed x42 -> x32, local copies, waits for them, and re-layouts: 4.81 us -> 3.94 us
  transfers between devices with their start and end apart: 13 -> 13, of which waited for: 5 -> 6; matrix products, arithmetic and copies ran while one was open for 2% -> 1% of each run, Pallas kernels for 16% -> 21%
where the time goes in v3:
time: 124 us; the launch traced here: 123 us
  starting transfers between devices  51.4 us (41%)
  Pallas kernels  33.8 us (27%)
  waiting for transfers between devices  31.9 us (26%)
  local copies, waits for them, and re-layouts  3.96 us (3%)
    pallas_call x8, Pallas kernels, call(): pl.pallas_call(copied, out_shape=tuple((jax.ShapeDtypeStruct(*out) for ou...  26.1 us
    all_to_all x1, starting transfers between devices, body(): lax.all_to_all(weight_half.reshape(depth, width // (2 * depth), 2 * HEAD_...  15.2 us
    all_to_all x1, waiting for transfers between devices, body(): lax.all_to_all(weight_half.reshape(depth, width // (2 * depth), 2 * HEAD_...  11.9 us
    all_to_all x1, waiting for transfers between devices, body(): lax.all_to_all(kv_out, 'mp', 0, 0, axis_index_groups=y_groups, tiled=True)  10.1 us
    all_to_all x1, starting transfers between devices, body(): lax.all_to_all(weight_parts, both, 0, 0, axis_index_groups=yx_groups, til...  5.41 us
    all_to_all x1, starting transfers between devices, body(): lax.all_to_all(kv_out, 'mp', 0, 0, axis_index_groups=y_groups, tiled=True)  4.61 us
    pallas_call x2, Pallas kernels, pack(): pl.pallas_call(pack_kernel, out_shape=jax.ShapeDtypeStruct((HELD, rows, b...  4.32 us
    all_to_all x1, starting transfers between devices, body(): lax.all_to_all(qo_out, 'mp', 0, 0, axis_index_groups=y_groups, tiled=True)  4.32 us
  transfers between devices with their start and end apart: 13, of which 6 were waited for; matrix products, arithmetic and copies ran while one was open for 1% of the time, Pallas kernels for 21%

profile of v3, /device:TPU:38, one launch (start us, length us, event | category | flops | bytes accessed | tf_op | source)
XLA Modules:
  0.0 122.8 jit_solution(8642633598212562521)
XLA Ops:
  0.6 2.3 %pack_keys_values.1 = bf16[4,160,1280]{2,1,0:T(8,128)(2,1)} custom-call(bf16[64,1280]{1,0:T(8,128)(2,1)} %bitcast.14, bf16[64,1280]{1,0:T(8,128)(2,1)} %bitcast.15, bf16[32,1280]{1,0:T(8,128)(2,1)} %bitcast.11), custom_call_target="tpu_custom_call" | custom-call | flops 1000 | bytes 1000 | tf_op jit(solution)/shard_map/pack_keys_values/pallas_call | solution.py:93
  2.9 4.6 %all-to-all-start = ((bf16[4,160,1280]{2,1,0:T(8,128)(2,1)}), bf16[4,160,1280]{2,1,0:T(8,128)(2,1)S(1)}, u32[]{:S(2)}, u32[]{:S(2)}) async-start(bf16[4,160,1280]{2,1,0:T(8,128)(2,1)} %pack_keys_values.1), calls=%async_computation | async-start | bytes 3276800 | tf_op jit(solution)/shard_map/all_to_all | solution.py:399
  7.6 1.9 %collective-permute-start = (bf16[2,128,1280]{2,1,0:T(8,128)(2,1)S(1)}, bf16[2,128,1280]{2,1,0:T(8,128)(2,1)S(1)}, u32[]{:S(2)}, u32[]{:S(2)}) collective-permute-start(bf16[2,128,1280]{2,1,0:T(8,128)(2,1)S(1)} %pad_maximum_fusion.refs_1_), channel_id=1, source_target_pairs={{0,1},{1,0},{2,3},{3,2},{4,5},{5,4},{6,7},{7,6},{8,9},{9,8},{10,11... | collective-permute-start | bytes 1966088 | tf_op jit(solution)/shard_map/ppermute | solution.py:403
  9.6 2.7 %collective-permute-start.3 = (bf16[2,128,1280]{2,1,0:T(8,128)(2,1)S(1)}, bf16[2,128,1280]{2,1,0:T(8,128)(2,1)}, u32[]{:S(2)}, u32[]{:S(2)}) collective-permute-start(bf16[2,128,1280]{2,1,0:T(8,128)(2,1)S(1)} %pad_maximum_fusion.refs_1_), channel_id=1, source_target_pairs={{0,8},{1,9},{2,10},{3,11},{4,12},{5,13},{6,14},{7,15},{8,0},{9,1},... | collective-permute-start | bytes 1966088 | tf_op jit(solution)/shard_map/ppermute | solution.py:402
  12.3 2.1 %pack_queries_out.1 = bf16[4,128,1280]{2,1,0:T(8,128)(2,1)} custom-call(bf16[64,1280]{1,0:T(8,128)(2,1)} %bitcast.13, bf16[64,1280]{1,0:T(8,128)(2,1)} %refs_1_.2), custom_call_target="tpu_custom_call" | custom-call | flops 1000 | bytes 1000 | tf_op jit(solution)/shard_map/pack_queries_out/pallas_call | solution.py:93
  15.0 0.8 copy-done.11
  15.9 3.0 %norms_near.1 = (bf16[256,1280]{1,0:T(8,128)(2,1)}, bf16[256,1280]{1,0:T(8,128)(2,1)}) custom-call(s32[128]{0:T(128)} %pad_add_fusion.refs_0_.meta_in, bf16[2,128,1280]{2,1,0:T(8,128)(2,1)} %copy-done.8, bf16[2,128,1280]{2,1,0:T(8,128)(2,1)} %copy-done.11, f32[1280]{0:T(1024)} %refs_4_.5, f32[1280]{0:T(1024)} %refs_4_.4), custom_call_target="tpu_custom_call" | custom-call | flops 1000 | bytes 1000 | tf_op jit(solution)/shard_map/norms_near/pallas_call | solution.py:356
  18.8 10.1 %all-to-all-done.refs_3_.kv_in = bf16[4,160,1280]{2,1,0:T(8,128)(2,1)S(1)} async-done(((bf16[4,160,1280]{2,1,0:T(8,128)(2,1)}), bf16[4,160,1280]{2,1,0:T(8,128)(2,1)S(1)}, u32[]{:S(2)}, u32[]{:S(2)}) %all-to-all-start) | async-done | bytes 1638432 | tf_op jit(solution)/shard_map/all_to_all | solution.py:399
  29.0 2.7 %collective-permute-start.1 = (bf16[4,32,1280]{2,1,0:T(8,128)(2,1)S(1)}, bf16[4,32,1280]{2,1,0:T(8,128)(2,1)S(1)}, u32[]{:S(2)}, u32[]{:S(2)}) collective-permute-start(bf16[4,32,1280]{2,1,0:T(8,128)(2,1)S(1)} %slice.3), channel_id=1, source_target_pairs={{0,8},{1,9},{2,10},{3,11},{4,12},{5,13},{6,14},{7,15},{8,0},{9,1},... | collective-permute-start | bytes 983048 | tf_op jit(solution)/shard_map/ppermute | solution.py:418
  31.7 4.3 %all-to-all-start.1 = ((bf16[4,128,1280]{2,1,0:T(8,128)(2,1)}), bf16[4,128,1280]{2,1,0:T(8,128)(2,1)}, u32[]{:S(2)}, u32[]{:S(2)}) async-start(bf16[4,128,1280]{2,1,0:T(8,128)(2,1)} %pack_queries_out.1), calls=%async_computation.1 | async-start | bytes 2621440 | tf_op jit(solution)/shard_map/all_to_all | solution.py:416
  36.1 1.9 %collective-permute-start.4 = (bf16[2,128,1280]{2,1,0:T(8,128)(2,1)}, bf16[2,128,1280]{2,1,0:T(8,128)(2,1)S(1)}, u32[]{:S(2)}, u32[]{:S(2)}) collective-permute-start(bf16[2,128,1280]{2,1,0:T(8,128)(2,1)} %collective-permute-done.3.refs_1_), channel_id=1, source_target_pairs={{0,1},{1,0},{2,3},{3,2},{4,5},{5,4},{6,7},{7,6},{8,9},{9,8},{10,11... | collective-permute-start | bytes 1966088 | tf_op jit(solution)/shard_map/ppermute | solution.py:428
  38.0 1.1 collective-permute-done.1
  39.2 1.9 %collective-permute-start.2 = (bf16[8,32,1280]{2,1,0:T(8,128)(2,1)S(1)}, bf16[8,32,1280]{2,1,0:T(8,128)(2,1)S(1)}, u32[]{:S(2)}, u32[]{:S(2)}) collective-permute-start(bf16[8,32,1280]{2,1,0:T(8,128)(2,1)S(1)} %pad_maximum_fusion.1.refs_4_), channel_id=1, source_target_pairs={{0,1},{1,0},{2,3},{3,2},{4,5},{5,4},{6,7},{7,6},{8,9},{9,8},{10,11... | collective-permute-start | bytes 1966088 | tf_op jit(solution)/shard_map/ppermute | solution.py:419
  42.0 2.9 %norms_far.1 = (bf16[256,1280]{1,0:T(8,128)(2,1)}, bf16[256,1280]{1,0:T(8,128)(2,1)}) custom-call(s32[128]{0:T(128)} %pad_add_fusion.refs_0_.meta_in, bf16[2,128,1280]{2,1,0:T(8,128)(2,1)} %collective-permute-done.3.refs_1_, bf16[2,128,1280]{2,1,0:T(8,128)(2,1)} %copy-done.12, f32[1280]{0:T(1024)} %refs_4_.5, f32[1280]{0:T(1024)} %refs_4_.4), custom_call_target="tpu_custom_call" | custom-call | flops 1000 | bytes 1000 | tf_op jit(solution)/shard_map/norms_far/pallas_call | solution.py:356
  45.7 3.4 %keys_values.1.refs_0_ = bf16[2,128,256]{2,1,0:T(8,128)(2,1)} custom-call(s32[128]{0:T(128)} %pad_add_fusion.refs_0_.meta_in, f32[1280]{0:T(1024)} %refs_6_.1, f32[1280]{0:T(1024)} %refs_2_.1, bf16[4,160,1280]{2,1,0:T(8,128)(2,1)} %copy-done.6, bf16[8,32,1280]{2,1,0:T(8,128)(2,1)} %copy-done.7, bf16[8,32,1280]{2,1,0:T(8,128)(2,1)} %copy-done.10), custom_call_target="tpu_custom_call" | custom-call | flops 1000 | bytes 1000 | tf_op jit(solution)/shard_map/keys_values/pallas_call | solution.py:356
  49.1 3.7 %all-to-all-done.1.refs_1_.refs_5_ = bf16[4,128,1280]{2,1,0:T(8,128)(2,1)} async-done(((bf16[4,128,1280]{2,1,0:T(8,128)(2,1)}), bf16[4,128,1280]{2,1,0:T(8,128)(2,1)}, u32[]{:S(2)}, u32[]{:S(2)}) %all-to-all-start.1) | async-done | bytes 1310752 | tf_op jit(solution)/shard_map/all_to_all | solution.py:416
  52.8 5.3 %attend.1 = (bf16[4,2,4,32,256]{4,3,2,1,0:T(8,128)(2,1)}, bf16[2,512,256]{2,1,0:T(8,128)(2,1)}) custom-call(bf16[2,128,256]{2,1,0:T(8,128)(2,1)} %keys_values.1.refs_0_, bf16[4,128,1280]{2,1,0:T(8,128)(2,1)} %all-to-all-done.1.refs_1_.refs_5_, bf16[256,1280]{1,0:T(8,128)(2,1)} %get-tuple-element.39.refs_2_.refs_1_, ...), custom_call_target="tpu_custom_call" | custom-call | flops 1000 | bytes 1000 | tf_op jit(solution)/shard_map/attend/pallas_call | solution.py:356
  58.1 3.5 %all-to-all-start.2 = ((bf16[4,2,4,32,256]{4,3,2,1,0:T(8,128)(2,1)}), bf16[4,2,4,32,256]{4,3,2,1,0:T(8,128)(2,1)S(1)}, u32[]{:S(2)}, u32[]{:S(2)}) async-start(bf16[4,2,4,32,256]{4,3,2,1,0:T(8,128)(2,1)} %get-tuple-element.43), calls=%async_computation.2 | async-start | bytes 1048576 | tf_op jit(solution)/shard_map/all_to_all | solution.py:438
  61.6 5.4 %products.1 = (bf16[8,128,640]{2,1,0:T(8,128)(2,1)}, bf16[288,1280]{1,0:T(8,128)(2,1)}, bf16[288,1280]{1,0:T(8,128)(2,1)}, bf16[2,288,1280]{2,1,0:T(8,128)(2,1)}) custom-call(bf16[2,512,256]{2,1,0:T(8,128)(2,1)} %get-tuple-element.44.refs_0_, bf16[256,1280]{1,0:T(8,128)(2,1)} %get-tuple-element.39.refs_2_.refs_1_, ...), custom_call_target="tpu_custom_call" | custom-call | flops 1000 | bytes 1000 | tf_op jit(solution)/shard_map/products/pallas_call | solution.py:356
  67.0 2.7 %all-to-all-done.2.got_in = bf16[4,2,4,32,256]{4,3,2,1,0:T(8,128)(2,1)S(1)} async-done(((bf16[4,2,4,32,256]{4,3,2,1,0:T(8,128)(2,1)}), bf16[4,2,4,32,256]{4,3,2,1,0:T(8,128)(2,1)S(1)}, u32[]{:S(2)}, u32[]{:S(2)}) %all-to-all-start.2) | async-done | bytes 524320 | tf_op jit(solution)/shard_map/all_to_all | solution.py:438
  69.7 5.4 %all-to-all-start.3 = ((bf16[8,128,640]{2,1,0:T(8,128)(2,1)}), bf16[8,128,640]{2,1,0:T(8,128)(2,1)S(1)}, u32[]{:S(2)}, u32[]{:S(2)}) async-start(bf16[8,128,640]{2,1,0:T(8,128)(2,1)} %get-tuple-element.46), calls=%async_computation.3 | async-start | bytes 2621440 | tf_op jit(solution)/shard_map/all_to_all | solution.py:453
  75.1 2.7 %state_grads.1 = (bf16[288,1280]{1,0:T(8,128)(2,1)}, bf16[288,1280]{1,0:T(8,128)(2,1)}, bf16[2,288,1280]{2,1,0:T(8,128)(2,1)}) custom-call(s32[128]{0:T(128)} %pad_add_fusion.refs_0_.meta_in, bf16[4,2,4,32,256]{4,3,2,1,0:T(8,128)(2,1)} %copy-done.9, bf16[4,160,1280]{2,1,0:T(8,128)(2,1)} %copy-done.6, ...), custom_call_target="tpu_custom_call", output_to_operand_aliasing={{0}: (3, {}), {1}: (4, {}), {2}: (5, {})} | custom-call | flops 1000 | bytes 1000 | tf_op jit(solution)/shard_map/state_grads/pallas_call | solution.py:454
  77.8 1.9 %collective-permute-start.5 = (bf16[288,1280]{1,0:T(8,128)(2,1)}, bf16[288,1280]{1,0:T(8,128)(2,1)S(1)}, u32[]{:S(2)}, u32[]{:S(2)}) collective-permute-start(bf16[288,1280]{1,0:T(8,128)(2,1)} %get-tuple-element.52), channel_id=1, source_target_pairs={{0,1},{1,0},{2,3},{3,2},{4,5},{5,4},{6,7},{7,6},{8,9},{9,8},{10,11... | collective-permute-start | bytes 2211848 | tf_op jit(solution)/shard_map/ppermute | solution.py:472
  79.7 2.4 %collective-permute-done.5.refs_1_ = bf16[288,1280]{1,0:T(8,128)(2,1)S(1)} collective-permute-done((bf16[288,1280]{1,0:T(8,128)(2,1)}, bf16[288,1280]{1,0:T(8,128)(2,1)S(1)}, u32[]{:S(2)}, u32[]{:S(2)}) %collective-permute-start.5) | collective-permute-done | bytes 737312 | tf_op jit(solution)/shard_map/ppermute | solution.py:472
  82.1 1.4 %copy-done = bf16[2,288,1280]{2,1,0:T(8,128)(2,1)S(1)} copy-done((bf16[2,288,1280]{2,1,0:T(8,128)(2,1)S(1)}, bf16[2,288,1280]{2,1,0:T(8,128)(2,1)}, u32[]{:S(2)}) %copy-start) | copy-done | bytes 1474584
  83.5 1.7 %add_updates.1 = bf16[288,1280]{1,0:T(8,128)(2,1)} custom-call(bf16[2,288,1280]{2,1,0:T(8,128)(2,1)S(1)} %copy-done, bf16[288,1280]{1,0:T(8,128)(2,1)S(1)} %collective-permute-done.5.refs_1_), custom_call_target="tpu_custom_call" | custom-call | flops 1000 | bytes 1000 | tf_op jit(solution)/shard_map/add_updates/pallas_call | solution.py:356
  85.2 3.2 %collective-permute-start.7 = (bf16[288,1280]{1,0:T(8,128)(2,1)}, bf16[288,1280]{1,0:T(8,128)(2,1)}, u32[]{:S(2)}, u32[]{:S(2)}) collective-permute-start(bf16[288,1280]{1,0:T(8,128)(2,1)} %add_updates.1), channel_id=1, source_target_pairs={{0,8},{1,9},{2,10},{3,11},{4,12},{5,13},{6,14},{7,15},{8,0},{9,1},... | collective-permute-start | bytes 2211848 | tf_op jit(solution)/shard_map/ppermute | solution.py:475
  88.5 1.9 %collective-permute-start.6 = (bf16[288,1280]{1,0:T(8,128)(2,1)}, bf16[288,1280]{1,0:T(8,128)(2,1)}, u32[]{:S(2)}, u32[]{:S(2)}) collective-permute-start(bf16[288,1280]{1,0:T(8,128)(2,1)} %get-tuple-element.54), channel_id=1, source_target_pairs={{0,1},{1,0},{2,3},{3,2},{4,5},{5,4},{6,7},{7,6},{8,9},{9,8},{10,11... | collective-permute-start | bytes 2211848 | tf_op jit(solution)/shard_map/ppermute | solution.py:473
  90.4 1.0 sum_weight_grads.1
  91.4 15.2 %all-to-all-start.4 = ((bf16[16,40,128]{2,1,0:T(8,128)(2,1)}), bf16[16,40,128]{2,1,0:T(8,128)(2,1)S(1)}, u32[]{:S(2)}, u32[]{:S(2)}) async-start(bf16[16,40,128]{2,1,0:T(8,128)(2,1)} %bitcast.8), calls=%async_computation.4 | async-start | bytes 327680 | tf_op jit(solution)/shard_map/all_to_all | solution.py:481
  106.7 3.5 %final_rows.1 = (bf16[128,1280]{1,0:T(8,128)(2,1)}, bf16[128,1280]{1,0:T(8,128)(2,1)}, bf16[1,32,1280]{2,1,0:T(8,128)(2,1)}) custom-call(bf16[2,288,1280]{2,1,0:T(8,128)(2,1)S(1)} %copy-done.1, bf16[288,1280]{1,0:T(8,128)(2,1)} %collective-permute-done.6.refs_1_, bf16[288,1280]{1,0:T(8,128)(2,1)} %collective-permute-done.7.refs_2_, ...), custom_call_target="tpu_custom_call" | custom-call | flops 1000 | bytes 1000 | tf_op jit(solution)/shard_map/final_rows/pallas_call | solution.py:356
  110.2 11.9 %all-to-all-done.4.parts_ref = bf16[16,40,128]{2,1,0:T(8,128)(2,1)S(1)} async-done(((bf16[16,40,128]{2,1,0:T(8,128)(2,1)}), bf16[16,40,128]{2,1,0:T(8,128)(2,1)S(1)}, u32[]{:S(2)}, u32[]{:S(2)}) %all-to-all-start.4) | async-done | bytes 163872 | tf_op jit(solution)/shard_map/all_to_all | solution.py:481
  (43 shorter events, 3.2 us)
Async XLA Ops:
  2.9 4.6 %copy-start.2 = (bf16[128,1280]{1,0:T(8,128)(2,1)S(1)}, bf16[128,1280]{1,0:T(8,128)(2,1)}, u32[]{:S(2)}) copy-start(bf16[128,1280]{1,0:T(8,128)(2,1)} %refs_3_.5) | copy-start | bytes 983044
  2.9 4.6 %copy-start.13 = (bf16[128,1280]{1,0:T(8,128)(2,1)S(1)}, bf16[128,1280]{1,0:T(8,128)(2,1)}, u32[]{:S(2)}) copy-start(bf16[128,1280]{1,0:T(8,128)(2,1)} %param.25) | copy-start | bytes 983044
  2.9 26.0 %all-to-all-start = ((bf16[4,160,1280]{2,1,0:T(8,128)(2,1)}), bf16[4,160,1280]{2,1,0:T(8,128)(2,1)S(1)}, u32[]{:S(2)}, u32[]{:S(2)}) async-start(bf16[4,160,1280]{2,1,0:T(8,128)(2,1)} %pack_keys_values.1), calls=%async_computation | async-start | bytes 3276800 | tf_op jit(solution)/shard_map/all_to_all | solution.py:399
  7.5 6.9 %copy-start.14 = (s32[1,16]{1,0:T(1,128)S(1)}, s32[1,16]{1,0:T(1,128)}, u32[]{:S(2)}) copy-start(s32[1,16]{1,0:T(1,128)} %param.16) | copy-start | bytes 196
  7.5 6.9 %copy-start.15 = (s32[16]{0:T(128)S(1)}, s32[16]{0:T(128)}, u32[]{:S(2)}) copy-start(s32[16]{0:T(128)} %param.15) | copy-start | bytes 196
  7.6 7.4 %copy-start.8 = (bf16[2,128,1280]{2,1,0:T(8,128)(2,1)}, bf16[2,128,1280]{2,1,0:T(8,128)(2,1)S(1)}, u32[]{:S(2)}) copy-start(bf16[2,128,1280]{2,1,0:T(8,128)(2,1)S(1)} %pad_maximum_fusion.refs_1_) | copy-start | bytes 1966084
  7.6 7.4 %collective-permute-start = (bf16[2,128,1280]{2,1,0:T(8,128)(2,1)S(1)}, bf16[2,128,1280]{2,1,0:T(8,128)(2,1)S(1)}, u32[]{:S(2)}, u32[]{:S(2)}) collective-permute-start(bf16[2,128,1280]{2,1,0:T(8,128)(2,1)S(1)} %pad_maximum_fusion.refs_1_), channel_id=1, source_target_pairs={{0,1},{1,0},{2,3},{3,2},{4,5},{5,4},{6,7},{7,6},{8,9},{9,8},{10,11... | collective-permute-start | bytes 1966088 | tf_op jit(solution)/shard_map/ppermute | solution.py:403
  9.6 26.5 %collective-permute-start.3 = (bf16[2,128,1280]{2,1,0:T(8,128)(2,1)S(1)}, bf16[2,128,1280]{2,1,0:T(8,128)(2,1)}, u32[]{:S(2)}, u32[]{:S(2)}) collective-permute-start(bf16[2,128,1280]{2,1,0:T(8,128)(2,1)S(1)} %pad_maximum_fusion.refs_1_), channel_id=1, source_target_pairs={{0,8},{1,9},{2,10},{3,11},{4,12},{5,13},{6,14},{7,15},{8,0},{9,1},... | collective-permute-start | bytes 1966088 | tf_op jit(solution)/shard_map/ppermute | solution.py:402
  15.0 0.8 copy-start.11
  29.0 2.8 %copy-start.6 = (bf16[4,160,1280]{2,1,0:T(8,128)(2,1)}, bf16[4,160,1280]{2,1,0:T(8,128)(2,1)S(1)}, u32[]{:S(2)}) copy-start(bf16[4,160,1280]{2,1,0:T(8,128)(2,1)S(1)} %all-to-all-done.refs_3_.kv_in) | copy-start | bytes 4915204
  29.0 10.2 %collective-permute-start.1 = (bf16[4,32,1280]{2,1,0:T(8,128)(2,1)S(1)}, bf16[4,32,1280]{2,1,0:T(8,128)(2,1)S(1)}, u32[]{:S(2)}, u32[]{:S(2)}) collective-permute-start(bf16[4,32,1280]{2,1,0:T(8,128)(2,1)S(1)} %slice.3), channel_id=1, source_target_pairs={{0,8},{1,9},{2,10},{3,11},{4,12},{5,13},{6,14},{7,15},{8,0},{9,1},... | collective-permute-start | bytes 983048 | tf_op jit(solution)/shard_map/ppermute | solution.py:418
  31.7 21.1 %all-to-all-start.1 = ((bf16[4,128,1280]{2,1,0:T(8,128)(2,1)}), bf16[4,128,1280]{2,1,0:T(8,128)(2,1)}, u32[]{:S(2)}, u32[]{:S(2)}) async-start(bf16[4,128,1280]{2,1,0:T(8,128)(2,1)} %pack_queries_out.1), calls=%async_computation.1 | async-start | bytes 2621440 | tf_op jit(solution)/shard_map/all_to_all | solution.py:416
  36.1 5.1 %collective-permute-start.4 = (bf16[2,128,1280]{2,1,0:T(8,128)(2,1)}, bf16[2,128,1280]{2,1,0:T(8,128)(2,1)S(1)}, u32[]{:S(2)}, u32[]{:S(2)}) collective-permute-start(bf16[2,128,1280]{2,1,0:T(8,128)(2,1)} %collective-permute-done.3.refs_1_), channel_id=1, source_target_pairs={{0,1},{1,0},{2,3},{3,2},{4,5},{5,4},{6,7},{7,6},{8,9},{9,8},{10,11... | collective-permute-start | bytes 1966088 | tf_op jit(solution)/shard_map/ppermute | solution.py:428
  39.2 5.7 %copy-start.7 = (bf16[8,32,1280]{2,1,0:T(8,128)(2,1)}, bf16[8,32,1280]{2,1,0:T(8,128)(2,1)S(1)}, u32[]{:S(2)}) copy-start(bf16[8,32,1280]{2,1,0:T(8,128)(2,1)S(1)} %pad_maximum_fusion.1.refs_4_) | copy-start | bytes 1966084
  39.2 5.7 %collective-permute-start.2 = (bf16[8,32,1280]{2,1,0:T(8,128)(2,1)S(1)}, bf16[8,32,1280]{2,1,0:T(8,128)(2,1)S(1)}, u32[]{:S(2)}, u32[]{:S(2)}) collective-permute-start(bf16[8,32,1280]{2,1,0:T(8,128)(2,1)S(1)} %pad_maximum_fusion.1.refs_4_), channel_id=1, source_target_pairs={{0,1},{1,0},{2,3},{3,2},{4,5},{5,4},{6,7},{7,6},{8,9},{9,8},{10,11... | collective-permute-start | bytes 1966088 | tf_op jit(solution)/shard_map/ppermute | solution.py:419
  41.1 0.8 copy-start.12
  44.9 0.8 copy-start.10
  58.1 11.5 %all-to-all-start.2 = ((bf16[4,2,4,32,256]{4,3,2,1,0:T(8,128)(2,1)}), bf16[4,2,4,32,256]{4,3,2,1,0:T(8,128)(2,1)S(1)}, u32[]{:S(2)}, u32[]{:S(2)}) async-start(bf16[4,2,4,32,256]{4,3,2,1,0:T(8,128)(2,1)} %get-tuple-element.43), calls=%async_computation.2 | async-start | bytes 1048576 | tf_op jit(solution)/shard_map/all_to_all | solution.py:438
  69.7 5.4 %copy-start.9 = (bf16[4,2,4,32,256]{4,3,2,1,0:T(8,128)(2,1)}, bf16[4,2,4,32,256]{4,3,2,1,0:T(8,128)(2,1)S(1)}, u32[]{:S(2)}) copy-start(bf16[4,2,4,32,256]{4,3,2,1,0:T(8,128)(2,1)S(1)} %all-to-all-done.2.got_in) | copy-start | bytes 1572868
  69.7 20.7 %all-to-all-start.3 = ((bf16[8,128,640]{2,1,0:T(8,128)(2,1)}), bf16[8,128,640]{2,1,0:T(8,128)(2,1)S(1)}, u32[]{:S(2)}, u32[]{:S(2)}) async-start(bf16[8,128,640]{2,1,0:T(8,128)(2,1)} %get-tuple-element.46), calls=%async_computation.3 | async-start | bytes 2621440 | tf_op jit(solution)/shard_map/all_to_all | solution.py:453
  77.8 4.3 %collective-permute-start.5 = (bf16[288,1280]{1,0:T(8,128)(2,1)}, bf16[288,1280]{1,0:T(8,128)(2,1)S(1)}, u32[]{:S(2)}, u32[]{:S(2)}) collective-permute-start(bf16[288,1280]{1,0:T(8,128)(2,1)} %get-tuple-element.52), channel_id=1, source_target_pairs={{0,1},{1,0},{2,3},{3,2},{4,5},{5,4},{6,7},{7,6},{8,9},{9,8},{10,11... | collective-permute-start | bytes 2211848 | tf_op jit(solution)/shard_map/ppermute | solution.py:472
  82.1 1.4 %copy-start = (bf16[2,288,1280]{2,1,0:T(8,128)(2,1)S(1)}, bf16[2,288,1280]{2,1,0:T(8,128)(2,1)}, u32[]{:S(2)}) copy-start(bf16[2,288,1280]{2,1,0:T(8,128)(2,1)} %get-tuple-element.51.refs_0_) | copy-start | bytes 4423684
  85.2 21.5 %copy-start.1 = (bf16[2,288,1280]{2,1,0:T(8,128)(2,1)S(1)}, bf16[2,288,1280]{2,1,0:T(8,128)(2,1)}, u32[]{:S(2)}) copy-start(bf16[2,288,1280]{2,1,0:T(8,128)(2,1)} %get-tuple-element.51.refs_0_) | copy-start | bytes 4423684
  85.2 21.5 %copy-start.3 = (bf16[1,32,1280]{2,1,0:T(8,128)(2,1)S(1)}, bf16[1,32,1280]{2,1,0:T(8,128)(2,1)}, u32[]{:S(2)}) copy-start(bf16[1,32,1280]{2,1,0:T(8,128)(2,1)} %refs_5_.1) | copy-start | bytes 245764
  85.2 21.5 %copy-start.4 = (f32[1280]{0:T(1024)S(1)}, f32[1280]{0:T(1024)}, u32[]{:S(2)}) copy-start(f32[1280]{0:T(1024)} %refs_4_.5) | copy-start | bytes 15364
  85.2 21.5 %copy-start.5 = (f32[1280]{0:T(1024)S(1)}, f32[1280]{0:T(1024)}, u32[]{:S(2)}) copy-start(f32[1280]{0:T(1024)} %refs_6_.1) | copy-start | bytes 15364
  85.2 21.5 %collective-permute-start.7 = (bf16[288,1280]{1,0:T(8,128)(2,1)}, bf16[288,1280]{1,0:T(8,128)(2,1)}, u32[]{:S(2)}, u32[]{:S(2)}) collective-permute-start(bf16[288,1280]{1,0:T(8,128)(2,1)} %add_updates.1), channel_id=1, source_target_pairs={{0,8},{1,9},{2,10},{3,11},{4,12},{5,13},{6,14},{7,15},{8,0},{9,1},... | collective-permute-start | bytes 2211848 | tf_op jit(solution)/shard_map/ppermute | solution.py:475
  88.5 18.2 %collective-permute-start.6 = (bf16[288,1280]{1,0:T(8,128)(2,1)}, bf16[288,1280]{1,0:T(8,128)(2,1)}, u32[]{:S(2)}, u32[]{:S(2)}) collective-permute-start(bf16[288,1280]{1,0:T(8,128)(2,1)} %get-tuple-element.54), channel_id=1, source_target_pairs={{0,1},{1,0},{2,3},{3,2},{4,5},{5,4},{6,7},{7,6},{8,9},{9,8},{10,11... | collective-permute-start | bytes 2211848 | tf_op jit(solution)/shard_map/ppermute | solution.py:473
  91.4 30.6 %all-to-all-start.4 = ((bf16[16,40,128]{2,1,0:T(8,128)(2,1)}), bf16[16,40,128]{2,1,0:T(8,128)(2,1)S(1)}, u32[]{:S(2)}, u32[]{:S(2)}) async-start(bf16[16,40,128]{2,1,0:T(8,128)(2,1)} %bitcast.8), calls=%async_computation.4 | async-start | bytes 327680 | tf_op jit(solution)/shard_map/all_to_all | solution.py:481

commit v4 on v3

--- a/solution.py
+++ b/solution.py
@@ -203,7 +203,7 @@
 
 
 def product_kernel(
-    io, rows_ref, h0, u0, h1, u1, qo_ref, grad_ref, send_x, send_own, keep_ref, hid_ref, up_ref
+    io, rows_ref, h0, u0, h1, u1, qo_ref, grad_ref, send_x, send_update, send_rest, keep_ref, hid_ref, up_ref
 ):
     io.take(0, 1, 2, 3, 4)
     join(hid_ref, h0, h1)
@@ -219,18 +219,18 @@
     io.give(0)
     io.take(5)
     w_query, w_out = weight_of(qo_ref, 0), weight_of(qo_ref, 1)
-    for part in range(HELD):
-        target = (keep_ref.at[0], keep_ref.at[1], send_own, send_x)[part]
+    for part, (first, second) in enumerate(
+        ((keep_ref.at[0], None), (keep_ref.at[1], None), (send_update, send_rest), (send_x, None))
+    ):
         span = slice(part * CAP, (part + 1) * CAP)
-        target[:CAP, :] = dot(rows_ref[0, span], w_out).astype(BF16)
-        target[CAP : 2 * CAP, :] = dot(rows_ref[1, span], w_query).astype(BF16)
-        target[2 * CAP :, :] = jnp.zeros((FRAMES, target.shape[1]), BF16)
-
-
-def state_kernel(
-    meta_in, got_in, kv_in, x_in, own_in, keep_in, x_out, own_out, keep_out, meta, got_ref, kv_ref, made, sems, keys_ref, values_ref
-):
-    del x_in, own_in, keep_in
+        first[:CAP, :] = dot(rows_ref[0, span], w_out).astype(BF16)
+        rest, start = (first, CAP) if second is None else (second, 0)
+        rest[start : start + CAP, :] = dot(rows_ref[1, span], w_query).astype(BF16)
+        rest[start + CAP :, :] = jnp.zeros((FRAMES, rest.shape[1]), BF16)
+
+
+def state_kernel(meta_in, got_in, kv_in, *refs):
+    send_x, send_rest, keep_ref, meta, got_ref, kv_ref, made, sems, keys_ref, values_ref = refs[3:]
     copies = [
         pltpu.make_async_copy(source, target, sems.at[place])
         for place, (source, target) in enumerate(((meta_in, meta), (got_in, got_ref), (kv_in, kv_ref)))
@@ -254,9 +254,9 @@
     copies = []
     for part in range(HELD):
         made[part] = total[part * FRAMES : (part + 1) * FRAMES].astype(BF16)
-        target = (keep_out.at[0], keep_out.at[1], own_out, x_out)[part]
+        target = (keep_ref.at[0], keep_ref.at[1], send_rest, send_x)[part]
         copies.append(
-            pltpu.make_async_copy(made.at[part], target.at[pl.ds(2 * CAP, FRAMES)], sems.at[3 + part])
+            pltpu.make_async_copy(made.at[part], target.at[pl.ds(target.shape[0] - FRAMES, FRAMES)], sems.at[3 + part])
         )
         copies[-1].start()
     for copy in copies:
@@ -285,13 +285,25 @@
 
 
 def final_kernel(
-    io, keep_ref, core_ref, x_ref, caption_ref, dec_gain, audio_ref, enc_gain, update_ref, grad_ref, out_ref
+    io,
+    keep_ref,
+    core_update,
+    core_rest,
+    x_ref,
+    caption_ref,
+    dec_gain,
+    audio_ref,
+    enc_gain,
+    update_ref,
+    grad_ref,
+    out_ref,
 ):
     io.take()
     width = caption_ref.shape[1]
 
     def total(start, stop):
-        near = keep_ref[start:stop].astype(F32) + core_ref[start:stop].astype(F32)
+        core_ref, first = (core_update, 0) if start == 0 else (core_rest, CAP)
+        near = keep_ref[start:stop].astype(F32) + core_ref[start - first : stop - first].astype(F32)
         return near + x_ref[start:stop].astype(F32)
 
     update_ref[...] = total(0, CAP).astype(BF16)
@@ -437,13 +449,14 @@
     )
     d_kv_got = lax.all_to_all(d_kv, "mp", 0, 0, axis_index_groups=y_groups, tiled=True)
     rows = 2 * CAP + FRAMES
-    weight_parts, send_x, send_own, keep = call(
+    weight_parts, send_x, send_update, *partials = call(
         product_kernel,
         "products",
         [
             ((2 * HELD, 2 * HEAD_DIM, width // 2), BF16),
             ((rows, width), BF16),
-            ((rows, width), BF16),
+            ((CAP, width), BF16),
+            ((rows - CAP, width), BF16),
             ((2, rows, width), BF16),
         ],
         (attended, *normed_near, *normed_far, qo_got),
@@ -451,12 +464,13 @@
     )
     d_kv_got, weight_parts = lax.optimization_barrier((d_kv_got, weight_parts))
     weight_got = lax.all_to_all(weight_parts, both, 0, 0, axis_index_groups=yx_groups, tiled=True)
-    send_x, send_own, keep = pl.pallas_call(
+    partials = (send_x, *partials)
+    send_x, send_rest, keep = pl.pallas_call(
         state_kernel,
-        out_shape=tuple(jax.ShapeDtypeStruct(array.shape, BF16) for array in (send_x, send_own, keep)),
+        out_shape=tuple(jax.ShapeDtypeStruct(array.shape, BF16) for array in partials),
         in_specs=[HBM] * 6,
         out_specs=(HBM,) * 3,
-        input_output_aliases={3: 0, 4: 1, 5: 2},
+        input_output_aliases={3 + place: place for place in range(3)},
         scratch_shapes=[
             pltpu.SMEM(meta.shape, meta.dtype),
             pltpu.VMEM(d_kv_got.shape, BF16),
@@ -468,9 +482,8 @@
         compiler_params=params(BIG),
         cost_estimate=COST,
         name="state_grads",
-    )(meta, d_kv_got, kv_got, send_x, send_own, keep)
+    )(meta, d_kv_got, kv_got, *partials)
     core_x = lax.ppermute(send_x, "mp", swap_core)
-    core_own = lax.ppermute(send_own, "mp", swap_core)
     (x_out,) = call(add_kernel, "add_updates", [((rows, width), BF16)], ((keep, 1), core_x), mib=8)
     x_parts = lax.ppermute(x_out, "mp", swap_x)
     weight_got, _ = lax.optimization_barrier((weight_got, x_out))
@@ -486,12 +499,14 @@
         axis_index_groups=z_groups,
         tiled=True,
     )
-    x_parts, _ = lax.optimization_barrier((x_parts, weight_half))
+    send_update, send_rest, _ = lax.optimization_barrier((send_update, send_rest, weight_half))
+    core_update = lax.ppermute(send_update, "mp", swap_core)
+    core_rest = lax.ppermute(send_rest, "mp", swap_core)
     cross_update, grad_captions, grad_audio = call(
         final_kernel,
         "final_rows",
         [((CAP, width), BF16), ((CAP, width), BF16), ((1, FRAMES, width), BF16)],
-        ((keep, 0), core_own, x_parts, captions, dec_gain, audio, enc_gain),
+        ((keep, 0), core_update, core_rest, x_parts, captions, dec_gain, audio, enc_gain),
         mib=16,
     )
     weight_last, cross_update, grad_captions, grad_audio = lax.optimization_barrier(

time: 124 us -> 123 us (level)
  the two profiles are of different devices: /device:TPU:38 before, /device:TPU:4 now
where the time goes in v4:
time: 123 us; the launch traced here: 122 us
  starting transfers between devices  54.1 us (44%)
  Pallas kernels  33.9 us (28%)
  waiting for transfers between devices  28.1 us (23%)
  local copies, waits for them, and re-layouts  3.99 us (3%)
    pallas_call x8, Pallas kernels, call(): pl.pallas_call(copied, out_shape=tuple((jax.ShapeDtypeStruct(*out) for ou...  26.2 us
    all_to_all x1, starting transfers between devices, body(): lax.all_to_all(weight_half.reshape(depth, width // (2 * depth), 2 * HEAD_...  15.2 us
    all_to_all x1, waiting for transfers between devices, body(): lax.all_to_all(kv_out, 'mp', 0, 0, axis_index_groups=y_groups, tiled=True)  9.8 us
    all_to_all x1, waiting for transfers between devices, body(): lax.all_to_all(weight_half.reshape(depth, width // (2 * depth), 2 * HEAD_...  6.18 us
    all_to_all x1, starting transfers between devices, body(): lax.all_to_all(weight_parts, both, 0, 0, axis_index_groups=yx_groups, til...  5.41 us
    all_to_all x1, starting transfers between devices, body(): lax.all_to_all(kv_out, 'mp', 0, 0, axis_index_groups=y_groups, tiled=True)  4.61 us
    all_to_all x1, starting transfers between devices, body(): lax.all_to_all(qo_out, 'mp', 0, 0, axis_index_groups=y_groups, tiled=True)  4.29 us
    pallas_call x2, Pallas kernels, pack(): pl.pallas_call(pack_kernel, out_shape=jax.ShapeDtypeStruct((HELD, rows, b...  4.29 us
  transfers between devices with their start and end apart: 14, of which 8 were waited for; matrix products, arithmetic and copies ran while one was open for 1% of the time, Pallas kernels for 21%

profile of v4, /device:TPU:4, one launch (start us, length us, event | category | flops | bytes accessed | tf_op | source)
XLA Modules:
  0.0 121.8 jit_solution(14613996413399135160)
XLA Ops:
  0.6 2.2 %pack_keys_values.1 = bf16[4,160,1280]{2,1,0:T(8,128)(2,1)} custom-call(bf16[64,1280]{1,0:T(8,128)(2,1)} %bitcast.14, bf16[64,1280]{1,0:T(8,128)(2,1)} %bitcast.15, bf16[32,1280]{1,0:T(8,128)(2,1)} %bitcast.11), custom_call_target="tpu_custom_call" | custom-call | flops 1000 | bytes 1000 | tf_op jit(solution)/shard_map/pack_keys_values/pallas_call | solution.py:93
  2.9 4.6 %all-to-all-start = ((bf16[4,160,1280]{2,1,0:T(8,128)(2,1)}), bf16[4,160,1280]{2,1,0:T(8,128)(2,1)S(1)}, u32[]{:S(2)}, u32[]{:S(2)}) async-start(bf16[4,160,1280]{2,1,0:T(8,128)(2,1)} %pack_keys_values.1), calls=%async_computation | async-start | bytes 3276800 | tf_op jit(solution)/shard_map/all_to_all | solution.py:411
  7.6 1.9 %collective-permute-start = (bf16[2,128,1280]{2,1,0:T(8,128)(2,1)S(1)}, bf16[2,128,1280]{2,1,0:T(8,128)(2,1)S(1)}, u32[]{:S(2)}, u32[]{:S(2)}) collective-permute-start(bf16[2,128,1280]{2,1,0:T(8,128)(2,1)S(1)} %pad_maximum_fusion.refs_1_), channel_id=1, source_target_pairs={{0,1},{1,0},{2,3},{3,2},{4,5},{5,4},{6,7},{7,6},{8,9},{9,8},{10,11... | collective-permute-start | bytes 1966088 | tf_op jit(solution)/shard_map/ppermute | solution.py:415
  9.5 3.1 %collective-permute-start.3 = (bf16[2,128,1280]{2,1,0:T(8,128)(2,1)S(1)}, bf16[2,128,1280]{2,1,0:T(8,128)(2,1)}, u32[]{:S(2)}, u32[]{:S(2)}) collective-permute-start(bf16[2,128,1280]{2,1,0:T(8,128)(2,1)S(1)} %pad_maximum_fusion.refs_1_), channel_id=1, source_target_pairs={{0,8},{1,9},{2,10},{3,11},{4,12},{5,13},{6,14},{7,15},{8,0},{9,1},... | collective-permute-start | bytes 1966088 | tf_op jit(solution)/shard_map/ppermute | solution.py:414
  12.7 2.1 %pack_queries_out.1 = bf16[4,128,1280]{2,1,0:T(8,128)(2,1)} custom-call(bf16[64,1280]{1,0:T(8,128)(2,1)} %bitcast.13, bf16[64,1280]{1,0:T(8,128)(2,1)} %refs_1_.2), custom_call_target="tpu_custom_call" | custom-call | flops 1000 | bytes 1000 | tf_op jit(solution)/shard_map/pack_queries_out/pallas_call | solution.py:93
  16.2 2.9 %norms_near.1 = (bf16[256,1280]{1,0:T(8,128)(2,1)}, bf16[256,1280]{1,0:T(8,128)(2,1)}) custom-call(s32[128]{0:T(128)} %pad_add_fusion.refs_0_.meta_in, bf16[2,128,1280]{2,1,0:T(8,128)(2,1)} %copy-done.8, bf16[2,128,1280]{2,1,0:T(8,128)(2,1)} %copy-done.11, f32[1280]{0:T(1024)} %refs_5_.1, f32[1280]{0:T(1024)} %refs_4_.4), custom_call_target="tpu_custom_call" | custom-call | flops 1000 | bytes 1000 | tf_op jit(solution)/shard_map/norms_near/pallas_call | solution.py:368
  19.1 9.8 %all-to-all-done.refs_3_.kv_in = bf16[4,160,1280]{2,1,0:T(8,128)(2,1)S(1)} async-done(((bf16[4,160,1280]{2,1,0:T(8,128)(2,1)}), bf16[4,160,1280]{2,1,0:T(8,128)(2,1)S(1)}, u32[]{:S(2)}, u32[]{:S(2)}) %all-to-all-start) | async-done | bytes 1638432 | tf_op jit(solution)/shard_map/all_to_all | solution.py:411
  28.9 3.1 %collective-permute-start.1 = (bf16[4,32,1280]{2,1,0:T(8,128)(2,1)S(1)}, bf16[4,32,1280]{2,1,0:T(8,128)(2,1)S(1)}, u32[]{:S(2)}, u32[]{:S(2)}) collective-permute-start(bf16[4,32,1280]{2,1,0:T(8,128)(2,1)S(1)} %slice.3), channel_id=1, source_target_pairs={{0,8},{1,9},{2,10},{3,11},{4,12},{5,13},{6,14},{7,15},{8,0},{9,1},... | collective-permute-start | bytes 983048 | tf_op jit(solution)/shard_map/ppermute | solution.py:430
  32.1 4.3 %all-to-all-start.1 = ((bf16[4,128,1280]{2,1,0:T(8,128)(2,1)}), bf16[4,128,1280]{2,1,0:T(8,128)(2,1)}, u32[]{:S(2)}, u32[]{:S(2)}) async-start(bf16[4,128,1280]{2,1,0:T(8,128)(2,1)} %pack_queries_out.1), calls=%async_computation.1 | async-start | bytes 2621440 | tf_op jit(solution)/shard_map/all_to_all | solution.py:428
  36.4 1.9 %collective-permute-start.4 = (bf16[2,128,1280]{2,1,0:T(8,128)(2,1)}, bf16[2,128,1280]{2,1,0:T(8,128)(2,1)S(1)}, u32[]{:S(2)}, u32[]{:S(2)}) collective-permute-start(bf16[2,128,1280]{2,1,0:T(8,128)(2,1)} %collective-permute-done.3.refs_1_), channel_id=1, source_target_pairs={{0,1},{1,0},{2,3},{3,2},{4,5},{5,4},{6,7},{7,6},{8,9},{9,8},{10,11... | collective-permute-start | bytes 1966088 | tf_op jit(solution)/shard_map/ppermute | solution.py:440
  39.2 1.9 %collective-permute-start.2 = (bf16[8,32,1280]{2,1,0:T(8,128)(2,1)S(1)}, bf16[8,32,1280]{2,1,0:T(8,128)(2,1)S(1)}, u32[]{:S(2)}, u32[]{:S(2)}) collective-permute-start(bf16[8,32,1280]{2,1,0:T(8,128)(2,1)S(1)} %pad_maximum_fusion.1.refs_4_), channel_id=1, source_target_pairs={{0,1},{1,0},{2,3},{3,2},{4,5},{5,4},{6,7},{7,6},{8,9},{9,8},{10,11... | collective-permute-start | bytes 1966088 | tf_op jit(solution)/shard_map/ppermute | solution.py:431
  42.0 3.0 %norms_far.1 = (bf16[256,1280]{1,0:T(8,128)(2,1)}, bf16[256,1280]{1,0:T(8,128)(2,1)}) custom-call(s32[128]{0:T(128)} %pad_add_fusion.refs_0_.meta_in, bf16[2,128,1280]{2,1,0:T(8,128)(2,1)} %collective-permute-done.3.refs_1_, bf16[2,128,1280]{2,1,0:T(8,128)(2,1)} %copy-done.12, f32[1280]{0:T(1024)} %refs_5_.1, f32[1280]{0:T(1024)} %refs_4_.4), custom_call_target="tpu_custom_call" | custom-call | flops 1000 | bytes 1000 | tf_op jit(solution)/shard_map/norms_far/pallas_call | solution.py:368
  45.8 3.4 %keys_values.1.refs_0_ = bf16[2,128,256]{2,1,0:T(8,128)(2,1)} custom-call(s32[128]{0:T(128)} %pad_add_fusion.refs_0_.meta_in, f32[1280]{0:T(1024)} %refs_7_.1, f32[1280]{0:T(1024)} %refs_2_.1, bf16[4,160,1280]{2,1,0:T(8,128)(2,1)} %copy-done.6, bf16[8,32,1280]{2,1,0:T(8,128)(2,1)} %copy-done.7, bf16[8,32,1280]{2,1,0:T(8,128)(2,1)} %copy-done.10), custom_call_target="tpu_custom_call" | custom-call | flops 1000 | bytes 1000 | tf_op jit(solution)/shard_map/keys_values/pallas_call | solution.py:368
  49.2 4.0 %all-to-all-done.1.refs_1_.refs_5_ = bf16[4,128,1280]{2,1,0:T(8,128)(2,1)} async-done(((bf16[4,128,1280]{2,1,0:T(8,128)(2,1)}), bf16[4,128,1280]{2,1,0:T(8,128)(2,1)}, u32[]{:S(2)}, u32[]{:S(2)}) %all-to-all-start.1) | async-done | bytes 1310752 | tf_op jit(solution)/shard_map/all_to_all | solution.py:428
  53.1 5.3 %attend.1 = (bf16[4,2,4,32,256]{4,3,2,1,0:T(8,128)(2,1)}, bf16[2,512,256]{2,1,0:T(8,128)(2,1)}) custom-call(bf16[2,128,256]{2,1,0:T(8,128)(2,1)} %keys_values.1.refs_0_, bf16[4,128,1280]{2,1,0:T(8,128)(2,1)} %all-to-all-done.1.refs_1_.refs_5_, bf16[256,1280]{1,0:T(8,128)(2,1)} %get-tuple-element.41.refs_2_.refs_1_, ...), custom_call_target="tpu_custom_call" | custom-call | flops 1000 | bytes 1000 | tf_op jit(solution)/shard_map/attend/pallas_call | solution.py:368
  58.5 3.5 %all-to-all-start.2 = ((bf16[4,2,4,32,256]{4,3,2,1,0:T(8,128)(2,1)}), bf16[4,2,4,32,256]{4,3,2,1,0:T(8,128)(2,1)S(1)}, u32[]{:S(2)}, u32[]{:S(2)}) async-start(bf16[4,2,4,32,256]{4,3,2,1,0:T(8,128)(2,1)} %get-tuple-element.45), calls=%async_computation.2 | async-start | bytes 1048576 | tf_op jit(solution)/shard_map/all_to_all | solution.py:450
  61.9 5.4 %products.1 = (bf16[8,128,640]{2,1,0:T(8,128)(2,1)}, bf16[288,1280]{1,0:T(8,128)(2,1)}, bf16[128,1280]{1,0:T(8,128)(2,1)}, bf16[160,1280]{1,0:T(8,128)(2,1)}, bf16[2,288,1280]{2,1,0:T(8,128)(2,1)}) custom-call(bf16[2,512,256]{2,1,0:T(8,128)(2,1)} %get-tuple-element.46.refs_0_, bf16[256,1280]{1,0:T(8,128)(2,1)} %get-tuple-element.41.refs_2_.refs_1_, ...), custom_call_target="tpu_custom_call" | custom-call | flops 1000 | bytes 1000 | tf_op jit(solution)/shard_map/products/pallas_call | solution.py:368
  67.4 2.6 %all-to-all-done.2.got_in = bf16[4,2,4,32,256]{4,3,2,1,0:T(8,128)(2,1)S(1)} async-done(((bf16[4,2,4,32,256]{4,3,2,1,0:T(8,128)(2,1)}), bf16[4,2,4,32,256]{4,3,2,1,0:T(8,128)(2,1)S(1)}, u32[]{:S(2)}, u32[]{:S(2)}) %all-to-all-start.2) | async-done | bytes 524320 | tf_op jit(solution)/shard_map/all_to_all | solution.py:450
  70.0 5.4 %all-to-all-start.3 = ((bf16[8,128,640]{2,1,0:T(8,128)(2,1)}), bf16[8,128,640]{2,1,0:T(8,128)(2,1)S(1)}, u32[]{:S(2)}, u32[]{:S(2)}) async-start(bf16[8,128,640]{2,1,0:T(8,128)(2,1)} %get-tuple-element.48), calls=%async_computation.3 | async-start | bytes 2621440 | tf_op jit(solution)/shard_map/all_to_all | solution.py:466
  75.4 2.7 %state_grads.1 = (bf16[288,1280]{1,0:T(8,128)(2,1)}, bf16[160,1280]{1,0:T(8,128)(2,1)}, bf16[2,288,1280]{2,1,0:T(8,128)(2,1)}) custom-call(s32[128]{0:T(128)} %pad_add_fusion.refs_0_.meta_in, bf16[4,2,4,32,256]{4,3,2,1,0:T(8,128)(2,1)} %copy-done.9, bf16[4,160,1280]{2,1,0:T(8,128)(2,1)} %copy-done.6, ...), custom_call_target="tpu_custom_call", output_to_operand_aliasing={{0}: (3, {}), {1}: (4, {}), {2}: (5, {})} | custom-call | flops 1000 | bytes 1000 | tf_op jit(solution)/shard_map/state_grads/pallas_call | solution.py:468
  78.1 1.9 %collective-permute-start.5 = (bf16[288,1280]{1,0:T(8,128)(2,1)}, bf16[288,1280]{1,0:T(8,128)(2,1)S(1)}, u32[]{:S(2)}, u32[]{:S(2)}) collective-permute-start(bf16[288,1280]{1,0:T(8,128)(2,1)} %get-tuple-element.54), channel_id=1, source_target_pairs={{0,1},{1,0},{2,3},{3,2},{4,5},{5,4},{6,7},{7,6},{8,9},{9,8},{10,11... | collective-permute-start | bytes 2211848 | tf_op jit(solution)/shard_map/ppermute | solution.py:486
  80.1 2.4 %collective-permute-done.5.refs_1_ = bf16[288,1280]{1,0:T(8,128)(2,1)S(1)} collective-permute-done((bf16[288,1280]{1,0:T(8,128)(2,1)}, bf16[288,1280]{1,0:T(8,128)(2,1)S(1)}, u32[]{:S(2)}, u32[]{:S(2)}) %collective-permute-start.5) | collective-permute-done | bytes 737312 | tf_op jit(solution)/shard_map/ppermute | solution.py:486
  82.4 1.4 %copy-done = bf16[2,288,1280]{2,1,0:T(8,128)(2,1)S(1)} copy-done((bf16[2,288,1280]{2,1,0:T(8,128)(2,1)S(1)}, bf16[2,288,1280]{2,1,0:T(8,128)(2,1)}, u32[]{:S(2)}) %copy-start) | copy-done | bytes 1474584
  83.8 1.7 %add_updates.1 = bf16[288,1280]{1,0:T(8,128)(2,1)} custom-call(bf16[2,288,1280]{2,1,0:T(8,128)(2,1)S(1)} %copy-done, bf16[288,1280]{1,0:T(8,128)(2,1)S(1)} %collective-permute-done.5.refs_1_), custom_call_target="tpu_custom_call" | custom-call | flops 1000 | bytes 1000 | tf_op jit(solution)/shard_map/add_updates/pallas_call | solution.py:368
  85.6 2.9 %collective-permute-start.8 = (bf16[288,1280]{1,0:T(8,128)(2,1)}, bf16[288,1280]{1,0:T(8,128)(2,1)}, u32[]{:S(2)}, u32[]{:S(2)}) collective-permute-start(bf16[288,1280]{1,0:T(8,128)(2,1)} %add_updates.1), channel_id=1, source_target_pairs={{0,8},{1,9},{2,10},{3,11},{4,12},{5,13},{6,14},{7,15},{8,0},{9,1},... | collective-permute-start | bytes 2211848 | tf_op jit(solution)/shard_map/ppermute | solution.py:488
  88.4 1.1 all-to-all-done.3.refs_0_
  90.5 15.2 %all-to-all-start.4 = ((bf16[16,40,128]{2,1,0:T(8,128)(2,1)}), bf16[16,40,128]{2,1,0:T(8,128)(2,1)S(1)}, u32[]{:S(2)}, u32[]{:S(2)}) async-start(bf16[16,40,128]{2,1,0:T(8,128)(2,1)} %bitcast.8), calls=%async_computation.4 | async-start | bytes 327680 | tf_op jit(solution)/shard_map/all_to_all | solution.py:494
  105.7 1.9 %collective-permute-start.7 = (bf16[160,1280]{1,0:T(8,128)(2,1)}, bf16[160,1280]{1,0:T(8,128)(2,1)S(1)}, u32[]{:S(2)}, u32[]{:S(2)}) collective-permute-start(bf16[160,1280]{1,0:T(8,128)(2,1)} %get-tuple-element.59), channel_id=1, source_target_pairs={{0,1},{1,0},{2,3},{3,2},{4,5},{5,4},{6,7},{7,6},{8,9},{9,8},{10,11... | collective-permute-start | bytes 1228808 | tf_op jit(solution)/shard_map/ppermute | solution.py:504
  107.7 2.4 %collective-permute-start.6 = (bf16[128,1280]{1,0:T(8,128)(2,1)S(1)}, bf16[128,1280]{1,0:T(8,128)(2,1)S(1)}, u32[]{:S(2)}, u32[]{:S(2)}) collective-permute-start(bf16[128,1280]{1,0:T(8,128)(2,1)S(1)} %copy-done.16), channel_id=1, source_target_pairs={{0,1},{1,0},{2,3},{3,2},{4,5},{5,4},{6,7},{7,6},{8,9},{9,8},{10,11... | collective-permute-start | bytes 983048 | tf_op jit(solution)/shard_map/ppermute | solution.py:503
  110.1 1.2 %collective-permute-done.6.refs_1_ = bf16[128,1280]{1,0:T(8,128)(2,1)S(1)} collective-permute-done((bf16[128,1280]{1,0:T(8,128)(2,1)S(1)}, bf16[128,1280]{1,0:T(8,128)(2,1)S(1)}, u32[]{:S(2)}, u32[]{:S(2)}) %collective-permute-start.6) | collective-permute-done | bytes 327712 | tf_op jit(solution)/shard_map/ppermute | solution.py:503
  111.4 3.5 %final_rows.1 = (bf16[128,1280]{1,0:T(8,128)(2,1)}, bf16[128,1280]{1,0:T(8,128)(2,1)}, bf16[1,32,1280]{2,1,0:T(8,128)(2,1)}) custom-call(bf16[2,288,1280]{2,1,0:T(8,128)(2,1)S(1)} %copy-done.1, bf16[128,1280]{1,0:T(8,128)(2,1)S(1)} %collective-permute-done.6.refs_1_, bf16[160,1280]{1,0:T(8,128)(2,1)S(1)} %collective-permute-done.7.refs_2_, ...), custom_call_target="tpu_custom_call" | custom-call | flops 1000 | bytes 1000 | tf_op jit(solution)/shard_map/final_rows/pallas_call | solution.py:368
  114.9 6.2 %all-to-all-done.4.parts_ref = bf16[16,40,128]{2,1,0:T(8,128)(2,1)S(1)} async-done(((bf16[16,40,128]{2,1,0:T(8,128)(2,1)}), bf16[16,40,128]{2,1,0:T(8,128)(2,1)S(1)}, u32[]{:S(2)}, u32[]{:S(2)}) %all-to-all-start.4) | async-done | bytes 163872 | tf_op jit(solution)/shard_map/all_to_all | solution.py:494
  (47 shorter events, 5.8 us)
Async XLA Ops:
  2.9 4.6 %copy-start.2 = (bf16[128,1280]{1,0:T(8,128)(2,1)S(1)}, bf16[128,1280]{1,0:T(8,128)(2,1)}, u32[]{:S(2)}) copy-start(bf16[128,1280]{1,0:T(8,128)(2,1)} %refs_4_.5) | copy-start | bytes 983044
  2.9 4.6 %copy-start.13 = (bf16[128,1280]{1,0:T(8,128)(2,1)S(1)}, bf16[128,1280]{1,0:T(8,128)(2,1)}, u32[]{:S(2)}) copy-start(bf16[128,1280]{1,0:T(8,128)(2,1)} %param.25) | copy-start | bytes 983044
  2.9 26.0 %all-to-all-start = ((bf16[4,160,1280]{2,1,0:T(8,128)(2,1)}), bf16[4,160,1280]{2,1,0:T(8,128)(2,1)S(1)}, u32[]{:S(2)}, u32[]{:S(2)}) async-start(bf16[4,160,1280]{2,1,0:T(8,128)(2,1)} %pack_keys_values.1), calls=%async_computation | async-start | bytes 3276800 | tf_op jit(solution)/shard_map/all_to_all | solution.py:411
  7.5 7.2 %copy-start.14 = (s32[1,16]{1,0:T(1,128)S(1)}, s32[1,16]{1,0:T(1,128)}, u32[]{:S(2)}) copy-start(s32[1,16]{1,0:T(1,128)} %param.16) | copy-start | bytes 196
  7.5 7.2 %copy-start.15 = (s32[16]{0:T(128)S(1)}, s32[16]{0:T(128)}, u32[]{:S(2)}) copy-start(s32[16]{0:T(128)} %param.15) | copy-start | bytes 196
  7.6 7.7 %copy-start.8 = (bf16[2,128,1280]{2,1,0:T(8,128)(2,1)}, bf16[2,128,1280]{2,1,0:T(8,128)(2,1)S(1)}, u32[]{:S(2)}) copy-start(bf16[2,128,1280]{2,1,0:T(8,128)(2,1)S(1)} %pad_maximum_fusion.refs_1_) | copy-start | bytes 1966084
  7.6 7.7 %collective-permute-start = (bf16[2,128,1280]{2,1,0:T(8,128)(2,1)S(1)}, bf16[2,128,1280]{2,1,0:T(8,128)(2,1)S(1)}, u32[]{:S(2)}, u32[]{:S(2)}) collective-permute-start(bf16[2,128,1280]{2,1,0:T(8,128)(2,1)S(1)} %pad_maximum_fusion.refs_1_), channel_id=1, source_target_pairs={{0,1},{1,0},{2,3},{3,2},{4,5},{5,4},{6,7},{7,6},{8,9},{9,8},{10,11... | collective-permute-start | bytes 1966088 | tf_op jit(solution)/shard_map/ppermute | solution.py:415
  9.5 26.8 %collective-permute-start.3 = (bf16[2,128,1280]{2,1,0:T(8,128)(2,1)S(1)}, bf16[2,128,1280]{2,1,0:T(8,128)(2,1)}, u32[]{:S(2)}, u32[]{:S(2)}) collective-permute-start(bf16[2,128,1280]{2,1,0:T(8,128)(2,1)S(1)} %pad_maximum_fusion.refs_1_), channel_id=1, source_target_pairs={{0,8},{1,9},{2,10},{3,11},{4,12},{5,13},{6,14},{7,15},{8,0},{9,1},... | collective-permute-start | bytes 1966088 | tf_op jit(solution)/shard_map/ppermute | solution.py:414
  15.3 0.8 copy-start.11
  28.9 3.1 %copy-start.6 = (bf16[4,160,1280]{2,1,0:T(8,128)(2,1)}, bf16[4,160,1280]{2,1,0:T(8,128)(2,1)S(1)}, u32[]{:S(2)}) copy-start(bf16[4,160,1280]{2,1,0:T(8,128)(2,1)S(1)} %all-to-all-done.refs_3_.kv_in) | copy-start | bytes 4915204
  28.9 10.2 %collective-permute-start.1 = (bf16[4,32,1280]{2,1,0:T(8,128)(2,1)S(1)}, bf16[4,32,1280]{2,1,0:T(8,128)(2,1)S(1)}, u32[]{:S(2)}, u32[]{:S(2)}) collective-permute-start(bf16[4,32,1280]{2,1,0:T(8,128)(2,1)S(1)} %slice.3), channel_id=1, source_target_pairs={{0,8},{1,9},{2,10},{3,11},{4,12},{5,13},{6,14},{7,15},{8,0},{9,1},... | collective-permute-start | bytes 983048 | tf_op jit(solution)/shard_map/ppermute | solution.py:430
  32.1 21.1 %all-to-all-start.1 = ((bf16[4,128,1280]{2,1,0:T(8,128)(2,1)}), bf16[4,128,1280]{2,1,0:T(8,128)(2,1)}, u32[]{:S(2)}, u32[]{:S(2)}) async-start(bf16[4,128,1280]{2,1,0:T(8,128)(2,1)} %pack_queries_out.1), calls=%async_computation.1 | async-start | bytes 2621440 | tf_op jit(solution)/shard_map/all_to_all | solution.py:428
  36.4 4.7 %collective-permute-start.4 = (bf16[2,128,1280]{2,1,0:T(8,128)(2,1)}, bf16[2,128,1280]{2,1,0:T(8,128)(2,1)S(1)}, u32[]{:S(2)}, u32[]{:S(2)}) collective-permute-start(bf16[2,128,1280]{2,1,0:T(8,128)(2,1)} %collective-permute-done.3.refs_1_), channel_id=1, source_target_pairs={{0,1},{1,0},{2,3},{3,2},{4,5},{5,4},{6,7},{7,6},{8,9},{9,8},{10,11... | collective-permute-start | bytes 1966088 | tf_op jit(solution)/shard_map/ppermute | solution.py:440
  39.2 5.8 %copy-start.7 = (bf16[8,32,1280]{2,1,0:T(8,128)(2,1)}, bf16[8,32,1280]{2,1,0:T(8,128)(2,1)S(1)}, u32[]{:S(2)}) copy-start(bf16[8,32,1280]{2,1,0:T(8,128)(2,1)S(1)} %pad_maximum_fusion.1.refs_4_) | copy-start | bytes 1966084
  39.2 5.7 %collective-permute-start.2 = (bf16[8,32,1280]{2,1,0:T(8,128)(2,1)S(1)}, bf16[8,32,1280]{2,1,0:T(8,128)(2,1)S(1)}, u32[]{:S(2)}, u32[]{:S(2)}) collective-permute-start(bf16[8,32,1280]{2,1,0:T(8,128)(2,1)S(1)} %pad_maximum_fusion.1.refs_4_), channel_id=1, source_target_pairs={{0,1},{1,0},{2,3},{3,2},{4,5},{5,4},{6,7},{7,6},{8,9},{9,8},{10,11... | collective-permute-start | bytes 1966088 | tf_op jit(solution)/shard_map/ppermute | solution.py:431
  41.1 0.8 copy-start.12
  44.9 0.8 copy-start.10
  58.5 11.5 %all-to-all-start.2 = ((bf16[4,2,4,32,256]{4,3,2,1,0:T(8,128)(2,1)}), bf16[4,2,4,32,256]{4,3,2,1,0:T(8,128)(2,1)S(1)}, u32[]{:S(2)}, u32[]{:S(2)}) async-start(bf16[4,2,4,32,256]{4,3,2,1,0:T(8,128)(2,1)} %get-tuple-element.45), calls=%async_computation.2 | async-start | bytes 1048576 | tf_op jit(solution)/shard_map/all_to_all | solution.py:450
  70.0 5.4 %copy-start.9 = (bf16[4,2,4,32,256]{4,3,2,1,0:T(8,128)(2,1)}, bf16[4,2,4,32,256]{4,3,2,1,0:T(8,128)(2,1)S(1)}, u32[]{:S(2)}) copy-start(bf16[4,2,4,32,256]{4,3,2,1,0:T(8,128)(2,1)S(1)} %all-to-all-done.2.got_in) | copy-start | bytes 1572868
  70.0 19.5 %all-to-all-start.3 = ((bf16[8,128,640]{2,1,0:T(8,128)(2,1)}), bf16[8,128,640]{2,1,0:T(8,128)(2,1)S(1)}, u32[]{:S(2)}, u32[]{:S(2)}) async-start(bf16[8,128,640]{2,1,0:T(8,128)(2,1)} %get-tuple-element.48), calls=%async_computation.3 | async-start | bytes 2621440 | tf_op jit(solution)/shard_map/all_to_all | solution.py:466
  78.1 4.3 %collective-permute-start.5 = (bf16[288,1280]{1,0:T(8,128)(2,1)}, bf16[288,1280]{1,0:T(8,128)(2,1)S(1)}, u32[]{:S(2)}, u32[]{:S(2)}) collective-permute-start(bf16[288,1280]{1,0:T(8,128)(2,1)} %get-tuple-element.54), channel_id=1, source_target_pairs={{0,1},{1,0},{2,3},{3,2},{4,5},{5,4},{6,7},{7,6},{8,9},{9,8},{10,11... | collective-permute-start | bytes 2211848 | tf_op jit(solution)/shard_map/ppermute | solution.py:486
  82.4 1.4 %copy-start = (bf16[2,288,1280]{2,1,0:T(8,128)(2,1)S(1)}, bf16[2,288,1280]{2,1,0:T(8,128)(2,1)}, u32[]{:S(2)}) copy-start(bf16[2,288,1280]{2,1,0:T(8,128)(2,1)} %get-tuple-element.53.refs_0_) | copy-start | bytes 4423684
  83.8 23.8 %copy-start.16 = (bf16[128,1280]{1,0:T(8,128)(2,1)S(1)}, bf16[128,1280]{1,0:T(8,128)(2,1)}, u32[]{:S(2)}) copy-start(bf16[128,1280]{1,0:T(8,128)(2,1)} %get-tuple-element.58) | copy-start | bytes 983044
  85.5 25.8 %copy-start.1 = (bf16[2,288,1280]{2,1,0:T(8,128)(2,1)S(1)}, bf16[2,288,1280]{2,1,0:T(8,128)(2,1)}, u32[]{:S(2)}) copy-start(bf16[2,288,1280]{2,1,0:T(8,128)(2,1)} %get-tuple-element.53.refs_0_) | copy-start | bytes 4423684
  85.5 25.8 %copy-start.3 = (bf16[1,32,1280]{2,1,0:T(8,128)(2,1)S(1)}, bf16[1,32,1280]{2,1,0:T(8,128)(2,1)}, u32[]{:S(2)}) copy-start(bf16[1,32,1280]{2,1,0:T(8,128)(2,1)} %refs_6_.1) | copy-start | bytes 245764
  85.5 25.8 %copy-start.4 = (f32[1280]{0:T(1024)S(1)}, f32[1280]{0:T(1024)}, u32[]{:S(2)}) copy-start(f32[1280]{0:T(1024)} %refs_5_.1) | copy-start | bytes 15364
  85.5 25.8 %copy-start.5 = (f32[1280]{0:T(1024)S(1)}, f32[1280]{0:T(1024)}, u32[]{:S(2)}) copy-start(f32[1280]{0:T(1024)} %refs_7_.1) | copy-start | bytes 15364
  85.6 25.8 %collective-permute-start.8 = (bf16[288,1280]{1,0:T(8,128)(2,1)}, bf16[288,1280]{1,0:T(8,128)(2,1)}, u32[]{:S(2)}, u32[]{:S(2)}) collective-permute-start(bf16[288,1280]{1,0:T(8,128)(2,1)} %add_updates.1), channel_id=1, source_target_pairs={{0,8},{1,9},{2,10},{3,11},{4,12},{5,13},{6,14},{7,15},{8,0},{9,1},... | collective-permute-start | bytes 2211848 | tf_op jit(solution)/shard_map/ppermute | solution.py:488
  90.5 30.6 %all-to-all-start.4 = ((bf16[16,40,128]{2,1,0:T(8,128)(2,1)}), bf16[16,40,128]{2,1,0:T(8,128)(2,1)S(1)}, u32[]{:S(2)}, u32[]{:S(2)}) async-start(bf16[16,40,128]{2,1,0:T(8,128)(2,1)} %bitcast.8), calls=%async_computation.4 | async-start | bytes 327680 | tf_op jit(solution)/shard_map/all_to_all | solution.py:494
  105.7 5.6 %collective-permute-start.7 = (bf16[160,1280]{1,0:T(8,128)(2,1)}, bf16[160,1280]{1,0:T(8,128)(2,1)S(1)}, u32[]{:S(2)}, u32[]{:S(2)}) collective-permute-start(bf16[160,1280]{1,0:T(8,128)(2,1)} %get-tuple-element.59), channel_id=1, source_target_pairs={{0,1},{1,0},{2,3},{3,2},{4,5},{5,4},{6,7},{7,6},{8,9},{9,8},{10,11... | collective-permute-start | bytes 1228808 | tf_op jit(solution)/shard_map/ppermute | solution.py:504
  107.7 3.6 %collective-permute-start.6 = (bf16[128,1280]{1,0:T(8,128)(2,1)S(1)}, bf16[128,1280]{1,0:T(8,128)(2,1)S(1)}, u32[]{:S(2)}, u32[]{:S(2)}) collective-permute-start(bf16[128,1280]{1,0:T(8,128)(2,1)S(1)} %copy-done.16), channel_id=1, source_target_pairs={{0,1},{1,0},{2,3},{3,2},{4,5},{5,4},{6,7},{7,6},{8,9},{9,8},{10,11... | collective-permute-start | bytes 983048 | tf_op jit(solution)/shard_map/ppermute | solution.py:503

commit v5 on v4

--- a/solution.py
+++ b/solution.py
@@ -148,7 +148,7 @@
         target[(2 * place + 1) * CAP : (2 * place + 2) * CAP, :] = far[rows, :]
 
 
-def attend_kernel(io, kv_ref, qo_ref, h0, u0, h1, u1, dkv_ref, rows_ref, hid_ref, up_ref):
+def attend_kernel(io, kv_ref, qo_ref, h0, u0, h1, u1, dkv_ref, rows_ref):
     scale = 1.0 / math.sqrt(HEAD_DIM)
     pairs = HELD * FRAMES
     row_head = lax.broadcasted_iota(jnp.int32, (pairs, WIDTH), 0) // FRAMES
@@ -174,14 +174,17 @@
     io.take(0)
     blocks = [[spread(kv_ref[kind, part * FRAMES : (part + 1) * FRAMES]) for part in parts] for kind in range(2)]
     keys, values = blocks
-    io.take(1, 2, 4)
-    join(hid_ref, h0, h1)
-    queries = dot(hid_ref[...], weight_of(qo_ref, 0), 1, 1).astype(BF16)
-    query = [queries[span] for span in spans]
-    io.take(3, 5)
-    join(up_ref, u0, u1)
-    d_attended = dot(up_ref[...], weight_of(qo_ref, 1), 1, 1).astype(BF16)
-    d_att = [d_attended[span] for span in spans]
+    io.take(1)
+
+    def project(near, far, kind):
+        found = []
+        for place, rows_in in zip((2 + kind, 4 + kind), (near, far)):
+            io.take(place)
+            found.append(dot(rows_in[...], weight_of(qo_ref, kind), 1, 1).astype(BF16))
+        return [found[part & 1][spans[part >> 1]] for part in parts]
+
+    query = project(h0, h1, 0)
+    d_att = project(u0, u1, 1)
     weights = [jnp.exp(dot(query[part], keys[part], 1, 1) * scale) for part in parts]
     d_softmax = [dot(d_att[part], values[part], 1, 1) for part in parts]
     sums = [segment_sum(weights[part], ones) for part in parts]
@@ -445,7 +448,6 @@
         "attend",
         [((HELD, 2, HELD, FRAMES, WIDTH), BF16), ((2, ROWS, WIDTH), BF16)],
         (keys_values, qo_got, *normed_near, *normed_far),
-        scratch=[pltpu.VMEM((ROWS, width), BF16)] * 2,
     )
     d_kv_got = lax.all_to_all(d_kv, "mp", 0, 0, axis_index_groups=y_groups, tiled=True)
     rows = 2 * CAP + FRAMES

time: 123 us -> 123 us (level)
  no operation moved by 1% of the time
where the time goes in v5:
time: 123 us; the launch traced here: 122 us
  starting transfers between devices  54.1 us (44%)
  Pallas kernels  33.9 us (28%)
  waiting for transfers between devices  28.1 us (23%)
  local copies, waits for them, and re-layouts  3.99 us (3%)
    pallas_call x8, Pallas kernels, call(): pl.pallas_call(copied, out_shape=tuple((jax.ShapeDtypeStruct(*out) for ou...  26.2 us
    all_to_all x1, starting transfers between devices, body(): lax.all_to_all(weight_half.reshape(depth, width // (2 * depth), 2 * HEAD_...  15.2 us
    all_to_all x1, waiting for transfers between devices, body(): lax.all_to_all(kv_out, 'mp', 0, 0, axis_index_groups=y_groups, tiled=True)  9.8 us
    all_to_all x1, waiting for transfers between devices, body(): lax.all_to_all(weight_half.reshape(depth, width // (2 * depth), 2 * HEAD_...  6.18 us
    all_to_all x1, starting transfers between devices, body(): lax.all_to_all(weight_parts, both, 0, 0, axis_index_groups=yx_groups, til...  5.41 us
    all_to_all x1, starting transfers between devices, body(): lax.all_to_all(kv_out, 'mp', 0, 0, axis_index_groups=y_groups, tiled=True)  4.61 us
    all_to_all x1, starting transfers between devices, body(): lax.all_to_all(qo_out, 'mp', 0, 0, axis_index_groups=y_groups, tiled=True)  4.29 us
    pallas_call x2, Pallas kernels, pack(): pl.pallas_call(pack_kernel, out_shape=jax.ShapeDtypeStruct((HELD, rows, b...  4.29 us
  transfers between devices with their start and end apart: 14, of which 8 were waited for; matrix products, arithmetic and copies ran while one was open for 1% of the time, Pallas kernels for 21%

profile of v5, /device:TPU:4, one launch (start us, length us, event | category | flops | bytes accessed | tf_op | source)
XLA Modules:
  0.0 121.8 jit_solution(605595898218270683)
XLA Ops:
  0.6 2.2 %pack_keys_values.1 = bf16[4,160,1280]{2,1,0:T(8,128)(2,1)} custom-call(bf16[64,1280]{1,0:T(8,128)(2,1)} %bitcast.14, bf16[64,1280]{1,0:T(8,128)(2,1)} %bitcast.15, bf16[32,1280]{1,0:T(8,128)(2,1)} %bitcast.11), custom_call_target="tpu_custom_call" | custom-call | flops 1000 | bytes 1000 | tf_op jit(solution)/shard_map/pack_keys_values/pallas_call | solution.py:93
  2.9 4.6 %all-to-all-start = ((bf16[4,160,1280]{2,1,0:T(8,128)(2,1)}), bf16[4,160,1280]{2,1,0:T(8,128)(2,1)S(1)}, u32[]{:S(2)}, u32[]{:S(2)}) async-start(bf16[4,160,1280]{2,1,0:T(8,128)(2,1)} %pack_keys_values.1), calls=%async_computation | async-start | bytes 3276800 | tf_op jit(solution)/shard_map/all_to_all | solution.py:414
  7.6 1.9 %collective-permute-start = (bf16[2,128,1280]{2,1,0:T(8,128)(2,1)S(1)}, bf16[2,128,1280]{2,1,0:T(8,128)(2,1)S(1)}, u32[]{:S(2)}, u32[]{:S(2)}) collective-permute-start(bf16[2,128,1280]{2,1,0:T(8,128)(2,1)S(1)} %pad_maximum_fusion.refs_1_), channel_id=1, source_target_pairs={{0,1},{1,0},{2,3},{3,2},{4,5},{5,4},{6,7},{7,6},{8,9},{9,8},{10,11... | collective-permute-start | bytes 1966088 | tf_op jit(solution)/shard_map/ppermute | solution.py:418
  9.5 3.1 %collective-permute-start.3 = (bf16[2,128,1280]{2,1,0:T(8,128)(2,1)S(1)}, bf16[2,128,1280]{2,1,0:T(8,128)(2,1)}, u32[]{:S(2)}, u32[]{:S(2)}) collective-permute-start(bf16[2,128,1280]{2,1,0:T(8,128)(2,1)S(1)} %pad_maximum_fusion.refs_1_), channel_id=1, source_target_pairs={{0,8},{1,9},{2,10},{3,11},{4,12},{5,13},{6,14},{7,15},{8,0},{9,1},... | collective-permute-start | bytes 1966088 | tf_op jit(solution)/shard_map/ppermute | solution.py:417
  12.7 2.1 %pack_queries_out.1 = bf16[4,128,1280]{2,1,0:T(8,128)(2,1)} custom-call(bf16[64,1280]{1,0:T(8,128)(2,1)} %bitcast.13, bf16[64,1280]{1,0:T(8,128)(2,1)} %refs_1_.2), custom_call_target="tpu_custom_call" | custom-call | flops 1000 | bytes 1000 | tf_op jit(solution)/shard_map/pack_queries_out/pallas_call | solution.py:93
  16.2 2.9 %norms_near.1 = (bf16[256,1280]{1,0:T(8,128)(2,1)}, bf16[256,1280]{1,0:T(8,128)(2,1)}) custom-call(s32[128]{0:T(128)} %pad_add_fusion.refs_0_.meta_in, bf16[2,128,1280]{2,1,0:T(8,128)(2,1)} %copy-done.8, bf16[2,128,1280]{2,1,0:T(8,128)(2,1)} %copy-done.11, f32[1280]{0:T(1024)} %refs_5_.1, f32[1280]{0:T(1024)} %refs_4_.4), custom_call_target="tpu_custom_call" | custom-call | flops 1000 | bytes 1000 | tf_op jit(solution)/shard_map/norms_near/pallas_call | solution.py:371
  19.1 9.8 %all-to-all-done.refs_3_.kv_in = bf16[4,160,1280]{2,1,0:T(8,128)(2,1)S(1)} async-done(((bf16[4,160,1280]{2,1,0:T(8,128)(2,1)}), bf16[4,160,1280]{2,1,0:T(8,128)(2,1)S(1)}, u32[]{:S(2)}, u32[]{:S(2)}) %all-to-all-start) | async-done | bytes 1638432 | tf_op jit(solution)/shard_map/all_to_all | solution.py:414
  28.9 3.1 %collective-permute-start.1 = (bf16[4,32,1280]{2,1,0:T(8,128)(2,1)S(1)}, bf16[4,32,1280]{2,1,0:T(8,128)(2,1)S(1)}, u32[]{:S(2)}, u32[]{:S(2)}) collective-permute-start(bf16[4,32,1280]{2,1,0:T(8,128)(2,1)S(1)} %slice.3), channel_id=1, source_target_pairs={{0,8},{1,9},{2,10},{3,11},{4,12},{5,13},{6,14},{7,15},{8,0},{9,1},... | collective-permute-start | bytes 983048 | tf_op jit(solution)/shard_map/ppermute | solution.py:433
  32.1 4.3 %all-to-all-start.1 = ((bf16[4,128,1280]{2,1,0:T(8,128)(2,1)}), bf16[4,128,1280]{2,1,0:T(8,128)(2,1)}, u32[]{:S(2)}, u32[]{:S(2)}) async-start(bf16[4,128,1280]{2,1,0:T(8,128)(2,1)} %pack_queries_out.1), calls=%async_computation.1 | async-start | bytes 2621440 | tf_op jit(solution)/shard_map/all_to_all | solution.py:431
  36.4 1.9 %collective-permute-start.4 = (bf16[2,128,1280]{2,1,0:T(8,128)(2,1)}, bf16[2,128,1280]{2,1,0:T(8,128)(2,1)S(1)}, u32[]{:S(2)}, u32[]{:S(2)}) collective-permute-start(bf16[2,128,1280]{2,1,0:T(8,128)(2,1)} %collective-permute-done.3.refs_1_), channel_id=1, source_target_pairs={{0,1},{1,0},{2,3},{3,2},{4,5},{5,4},{6,7},{7,6},{8,9},{9,8},{10,11... | collective-permute-start | bytes 1966088 | tf_op jit(solution)/shard_map/ppermute | solution.py:443
  39.2 1.9 %collective-permute-start.2 = (bf16[8,32,1280]{2,1,0:T(8,128)(2,1)S(1)}, bf16[8,32,1280]{2,1,0:T(8,128)(2,1)S(1)}, u32[]{:S(2)}, u32[]{:S(2)}) collective-permute-start(bf16[8,32,1280]{2,1,0:T(8,128)(2,1)S(1)} %pad_maximum_fusion.1.refs_4_), channel_id=1, source_target_pairs={{0,1},{1,0},{2,3},{3,2},{4,5},{5,4},{6,7},{7,6},{8,9},{9,8},{10,11... | collective-permute-start | bytes 1966088 | tf_op jit(solution)/shard_map/ppermute | solution.py:434
  42.0 3.0 %norms_far.1 = (bf16[256,1280]{1,0:T(8,128)(2,1)}, bf16[256,1280]{1,0:T(8,128)(2,1)}) custom-call(s32[128]{0:T(128)} %pad_add_fusion.refs_0_.meta_in, bf16[2,128,1280]{2,1,0:T(8,128)(2,1)} %collective-permute-done.3.refs_1_, bf16[2,128,1280]{2,1,0:T(8,128)(2,1)} %copy-done.12, f32[1280]{0:T(1024)} %refs_5_.1, f32[1280]{0:T(1024)} %refs_4_.4), custom_call_target="tpu_custom_call" | custom-call | flops 1000 | bytes 1000 | tf_op jit(solution)/shard_map/norms_far/pallas_call | solution.py:371
  45.8 3.4 %keys_values.1.refs_0_ = bf16[2,128,256]{2,1,0:T(8,128)(2,1)} custom-call(s32[128]{0:T(128)} %pad_add_fusion.refs_0_.meta_in, f32[1280]{0:T(1024)} %refs_7_.1, f32[1280]{0:T(1024)} %refs_2_.1, bf16[4,160,1280]{2,1,0:T(8,128)(2,1)} %copy-done.6, bf16[8,32,1280]{2,1,0:T(8,128)(2,1)} %copy-done.7, bf16[8,32,1280]{2,1,0:T(8,128)(2,1)} %copy-done.10), custom_call_target="tpu_custom_call" | custom-call | flops 1000 | bytes 1000 | tf_op jit(solution)/shard_map/keys_values/pallas_call | solution.py:371
  49.2 4.0 %all-to-all-done.1.refs_1_.refs_5_ = bf16[4,128,1280]{2,1,0:T(8,128)(2,1)} async-done(((bf16[4,128,1280]{2,1,0:T(8,128)(2,1)}), bf16[4,128,1280]{2,1,0:T(8,128)(2,1)}, u32[]{:S(2)}, u32[]{:S(2)}) %all-to-all-start.1) | async-done | bytes 1310752 | tf_op jit(solution)/shard_map/all_to_all | solution.py:431
  53.1 5.3 %attend.1 = (bf16[4,2,4,32,256]{4,3,2,1,0:T(8,128)(2,1)}, bf16[2,512,256]{2,1,0:T(8,128)(2,1)}) custom-call(bf16[2,128,256]{2,1,0:T(8,128)(2,1)} %keys_values.1.refs_0_, bf16[4,128,1280]{2,1,0:T(8,128)(2,1)} %all-to-all-done.1.refs_1_.refs_5_, bf16[256,1280]{1,0:T(8,128)(2,1)} %get-tuple-element.41.refs_2_.refs_1_, ...), custom_call_target="tpu_custom_call" | custom-call | flops 1000 | bytes 1000 | tf_op jit(solution)/shard_map/attend/pallas_call | solution.py:371
  58.5 3.5 %all-to-all-start.2 = ((bf16[4,2,4,32,256]{4,3,2,1,0:T(8,128)(2,1)}), bf16[4,2,4,32,256]{4,3,2,1,0:T(8,128)(2,1)S(1)}, u32[]{:S(2)}, u32[]{:S(2)}) async-start(bf16[4,2,4,32,256]{4,3,2,1,0:T(8,128)(2,1)} %get-tuple-element.45), calls=%async_computation.2 | async-start | bytes 1048576 | tf_op jit(solution)/shard_map/all_to_all | solution.py:452
  61.9 5.4 %products.1 = (bf16[8,128,640]{2,1,0:T(8,128)(2,1)}, bf16[288,1280]{1,0:T(8,128)(2,1)}, bf16[128,1280]{1,0:T(8,128)(2,1)}, bf16[160,1280]{1,0:T(8,128)(2,1)}, bf16[2,288,1280]{2,1,0:T(8,128)(2,1)}) custom-call(bf16[2,512,256]{2,1,0:T(8,128)(2,1)} %get-tuple-element.46.refs_0_, bf16[256,1280]{1,0:T(8,128)(2,1)} %get-tuple-element.41.refs_2_.refs_1_, ...), custom_call_target="tpu_custom_call" | custom-call | flops 1000 | bytes 1000 | tf_op jit(solution)/shard_map/products/pallas_call | solution.py:371
  67.4 2.6 %all-to-all-done.2.got_in = bf16[4,2,4,32,256]{4,3,2,1,0:T(8,128)(2,1)S(1)} async-done(((bf16[4,2,4,32,256]{4,3,2,1,0:T(8,128)(2,1)}), bf16[4,2,4,32,256]{4,3,2,1,0:T(8,128)(2,1)S(1)}, u32[]{:S(2)}, u32[]{:S(2)}) %all-to-all-start.2) | async-done | bytes 524320 | tf_op jit(solution)/shard_map/all_to_all | solution.py:452
  70.0 5.4 %all-to-all-start.3 = ((bf16[8,128,640]{2,1,0:T(8,128)(2,1)}), bf16[8,128,640]{2,1,0:T(8,128)(2,1)S(1)}, u32[]{:S(2)}, u32[]{:S(2)}) async-start(bf16[8,128,640]{2,1,0:T(8,128)(2,1)} %get-tuple-element.48), calls=%async_computation.3 | async-start | bytes 2621440 | tf_op jit(solution)/shard_map/all_to_all | solution.py:468
  75.4 2.7 %state_grads.1 = (bf16[288,1280]{1,0:T(8,128)(2,1)}, bf16[160,1280]{1,0:T(8,128)(2,1)}, bf16[2,288,1280]{2,1,0:T(8,128)(2,1)}) custom-call(s32[128]{0:T(128)} %pad_add_fusion.refs_0_.meta_in, bf16[4,2,4,32,256]{4,3,2,1,0:T(8,128)(2,1)} %copy-done.9, bf16[4,160,1280]{2,1,0:T(8,128)(2,1)} %copy-done.6, ...), custom_call_target="tpu_custom_call", output_to_operand_aliasing={{0}: (3, {}), {1}: (4, {}), {2}: (5, {})} | custom-call | flops 1000 | bytes 1000 | tf_op jit(solution)/shard_map/state_grads/pallas_call | solution.py:470
  78.1 1.9 %collective-permute-start.5 = (bf16[288,1280]{1,0:T(8,128)(2,1)}, bf16[288,1280]{1,0:T(8,128)(2,1)S(1)}, u32[]{:S(2)}, u32[]{:S(2)}) collective-permute-start(bf16[288,1280]{1,0:T(8,128)(2,1)} %get-tuple-element.54), channel_id=1, source_target_pairs={{0,1},{1,0},{2,3},{3,2},{4,5},{5,4},{6,7},{7,6},{8,9},{9,8},{10,11... | collective-permute-start | bytes 2211848 | tf_op jit(solution)/shard_map/ppermute | solution.py:488
  80.0 2.4 %collective-permute-done.5.refs_1_ = bf16[288,1280]{1,0:T(8,128)(2,1)S(1)} collective-permute-done((bf16[288,1280]{1,0:T(8,128)(2,1)}, bf16[288,1280]{1,0:T(8,128)(2,1)S(1)}, u32[]{:S(2)}, u32[]{:S(2)}) %collective-permute-start.5) | collective-permute-done | bytes 737312 | tf_op jit(solution)/shard_map/ppermute | solution.py:488
  82.4 1.4 %copy-done = bf16[2,288,1280]{2,1,0:T(8,128)(2,1)S(1)} copy-done((bf16[2,288,1280]{2,1,0:T(8,128)(2,1)S(1)}, bf16[2,288,1280]{2,1,0:T(8,128)(2,1)}, u32[]{:S(2)}) %copy-start) | copy-done | bytes 1474584
  83.8 1.7 %add_updates.1 = bf16[288,1280]{1,0:T(8,128)(2,1)} custom-call(bf16[2,288,1280]{2,1,0:T(8,128)(2,1)S(1)} %copy-done, bf16[288,1280]{1,0:T(8,128)(2,1)S(1)} %collective-permute-done.5.refs_1_), custom_call_target="tpu_custom_call" | custom-call | flops 1000 | bytes 1000 | tf_op jit(solution)/shard_map/add_updates/pallas_call | solution.py:371
  85.6 2.9 %collective-permute-start.8 = (bf16[288,1280]{1,0:T(8,128)(2,1)}, bf16[288,1280]{1,0:T(8,128)(2,1)}, u32[]{:S(2)}, u32[]{:S(2)}) collective-permute-start(bf16[288,1280]{1,0:T(8,128)(2,1)} %add_updates.1), channel_id=1, source_target_pairs={{0,8},{1,9},{2,10},{3,11},{4,12},{5,13},{6,14},{7,15},{8,0},{9,1},... | collective-permute-start | bytes 2211848 | tf_op jit(solution)/shard_map/ppermute | solution.py:490
  88.4 1.1 all-to-all-done.3.refs_0_
  90.5 15.2 %all-to-all-start.4 = ((bf16[16,40,128]{2,1,0:T(8,128)(2,1)}), bf16[16,40,128]{2,1,0:T(8,128)(2,1)S(1)}, u32[]{:S(2)}, u32[]{:S(2)}) async-start(bf16[16,40,128]{2,1,0:T(8,128)(2,1)} %bitcast.8), calls=%async_computation.4 | async-start | bytes 327680 | tf_op jit(solution)/shard_map/all_to_all | solution.py:496
  105.7 1.9 %collective-permute-start.7 = (bf16[160,1280]{1,0:T(8,128)(2,1)}, bf16[160,1280]{1,0:T(8,128)(2,1)S(1)}, u32[]{:S(2)}, u32[]{:S(2)}) collective-permute-start(bf16[160,1280]{1,0:T(8,128)(2,1)} %get-tuple-element.59), channel_id=1, source_target_pairs={{0,1},{1,0},{2,3},{3,2},{4,5},{5,4},{6,7},{7,6},{8,9},{9,8},{10,11... | collective-permute-start | bytes 1228808 | tf_op jit(solution)/shard_map/ppermute | solution.py:506
  107.7 2.4 %collective-permute-start.6 = (bf16[128,1280]{1,0:T(8,128)(2,1)S(1)}, bf16[128,1280]{1,0:T(8,128)(2,1)S(1)}, u32[]{:S(2)}, u32[]{:S(2)}) collective-permute-start(bf16[128,1280]{1,0:T(8,128)(2,1)S(1)} %copy-done.16), channel_id=1, source_target_pairs={{0,1},{1,0},{2,3},{3,2},{4,5},{5,4},{6,7},{7,6},{8,9},{9,8},{10,11... | collective-permute-start | bytes 983048 | tf_op jit(solution)/shard_map/ppermute | solution.py:505
  110.1 1.2 %collective-permute-done.6.refs_1_ = bf16[128,1280]{1,0:T(8,128)(2,1)S(1)} collective-permute-done((bf16[128,1280]{1,0:T(8,128)(2,1)S(1)}, bf16[128,1280]{1,0:T(8,128)(2,1)S(1)}, u32[]{:S(2)}, u32[]{:S(2)}) %collective-permute-start.6) | collective-permute-done | bytes 327712 | tf_op jit(solution)/shard_map/ppermute | solution.py:505
  111.4 3.5 %final_rows.1 = (bf16[128,1280]{1,0:T(8,128)(2,1)}, bf16[128,1280]{1,0:T(8,128)(2,1)}, bf16[1,32,1280]{2,1,0:T(8,128)(2,1)}) custom-call(bf16[2,288,1280]{2,1,0:T(8,128)(2,1)S(1)} %copy-done.1, bf16[128,1280]{1,0:T(8,128)(2,1)S(1)} %collective-permute-done.6.refs_1_, bf16[160,1280]{1,0:T(8,128)(2,1)S(1)} %collective-permute-done.7.refs_2_, ...), custom_call_target="tpu_custom_call" | custom-call | flops 1000 | bytes 1000 | tf_op jit(solution)/shard_map/final_rows/pallas_call | solution.py:371
  114.9 6.2 %all-to-all-done.4.parts_ref = bf16[16,40,128]{2,1,0:T(8,128)(2,1)S(1)} async-done(((bf16[16,40,128]{2,1,0:T(8,128)(2,1)}), bf16[16,40,128]{2,1,0:T(8,128)(2,1)S(1)}, u32[]{:S(2)}, u32[]{:S(2)}) %all-to-all-start.4) | async-done | bytes 163872 | tf_op jit(solution)/shard_map/all_to_all | solution.py:496
  (47 shorter events, 5.8 us)
Async XLA Ops:
  2.9 4.6 %copy-start.2 = (bf16[128,1280]{1,0:T(8,128)(2,1)S(1)}, bf16[128,1280]{1,0:T(8,128)(2,1)}, u32[]{:S(2)}) copy-start(bf16[128,1280]{1,0:T(8,128)(2,1)} %refs_4_.5) | copy-start | bytes 983044
  2.9 4.6 %copy-start.13 = (bf16[128,1280]{1,0:T(8,128)(2,1)S(1)}, bf16[128,1280]{1,0:T(8,128)(2,1)}, u32[]{:S(2)}) copy-start(bf16[128,1280]{1,0:T(8,128)(2,1)} %param.25) | copy-start | bytes 983044
  2.9 26.0 %all-to-all-start = ((bf16[4,160,1280]{2,1,0:T(8,128)(2,1)}), bf16[4,160,1280]{2,1,0:T(8,128)(2,1)S(1)}, u32[]{:S(2)}, u32[]{:S(2)}) async-start(bf16[4,160,1280]{2,1,0:T(8,128)(2,1)} %pack_keys_values.1), calls=%async_computation | async-start | bytes 3276800 | tf_op jit(solution)/shard_map/all_to_all | solution.py:414
  7.5 7.2 %copy-start.14 = (s32[1,16]{1,0:T(1,128)S(1)}, s32[1,16]{1,0:T(1,128)}, u32[]{:S(2)}) copy-start(s32[1,16]{1,0:T(1,128)} %param.16) | copy-start | bytes 196
  7.5 7.2 %copy-start.15 = (s32[16]{0:T(128)S(1)}, s32[16]{0:T(128)}, u32[]{:S(2)}) copy-start(s32[16]{0:T(128)} %param.15) | copy-start | bytes 196
  7.6 7.7 %copy-start.8 = (bf16[2,128,1280]{2,1,0:T(8,128)(2,1)}, bf16[2,128,1280]{2,1,0:T(8,128)(2,1)S(1)}, u32[]{:S(2)}) copy-start(bf16[2,128,1280]{2,1,0:T(8,128)(2,1)S(1)} %pad_maximum_fusion.refs_1_) | copy-start | bytes 1966084
  7.6 7.7 %collective-permute-start = (bf16[2,128,1280]{2,1,0:T(8,128)(2,1)S(1)}, bf16[2,128,1280]{2,1,0:T(8,128)(2,1)S(1)}, u32[]{:S(2)}, u32[]{:S(2)}) collective-permute-start(bf16[2,128,1280]{2,1,0:T(8,128)(2,1)S(1)} %pad_maximum_fusion.refs_1_), channel_id=1, source_target_pairs={{0,1},{1,0},{2,3},{3,2},{4,5},{5,4},{6,7},{7,6},{8,9},{9,8},{10,11... | collective-permute-start | bytes 1966088 | tf_op jit(solution)/shard_map/ppermute | solution.py:418
  9.5 26.8 %collective-permute-start.3 = (bf16[2,128,1280]{2,1,0:T(8,128)(2,1)S(1)}, bf16[2,128,1280]{2,1,0:T(8,128)(2,1)}, u32[]{:S(2)}, u32[]{:S(2)}) collective-permute-start(bf16[2,128,1280]{2,1,0:T(8,128)(2,1)S(1)} %pad_maximum_fusion.refs_1_), channel_id=1, source_target_pairs={{0,8},{1,9},{2,10},{3,11},{4,12},{5,13},{6,14},{7,15},{8,0},{9,1},... | collective-permute-start | bytes 1966088 | tf_op jit(solution)/shard_map/ppermute | solution.py:417
  15.3 0.8 copy-start.11
  28.9 3.1 %copy-start.6 = (bf16[4,160,1280]{2,1,0:T(8,128)(2,1)}, bf16[4,160,1280]{2,1,0:T(8,128)(2,1)S(1)}, u32[]{:S(2)}) copy-start(bf16[4,160,1280]{2,1,0:T(8,128)(2,1)S(1)} %all-to-all-done.refs_3_.kv_in) | copy-start | bytes 4915204
  28.9 10.2 %collective-permute-start.1 = (bf16[4,32,1280]{2,1,0:T(8,128)(2,1)S(1)}, bf16[4,32,1280]{2,1,0:T(8,128)(2,1)S(1)}, u32[]{:S(2)}, u32[]{:S(2)}) collective-permute-start(bf16[4,32,1280]{2,1,0:T(8,128)(2,1)S(1)} %slice.3), channel_id=1, source_target_pairs={{0,8},{1,9},{2,10},{3,11},{4,12},{5,13},{6,14},{7,15},{8,0},{9,1},... | collective-permute-start | bytes 983048 | tf_op jit(solution)/shard_map/ppermute | solution.py:433
  32.1 21.1 %all-to-all-start.1 = ((bf16[4,128,1280]{2,1,0:T(8,128)(2,1)}), bf16[4,128,1280]{2,1,0:T(8,128)(2,1)}, u32[]{:S(2)}, u32[]{:S(2)}) async-start(bf16[4,128,1280]{2,1,0:T(8,128)(2,1)} %pack_queries_out.1), calls=%async_computation.1 | async-start | bytes 2621440 | tf_op jit(solution)/shard_map/all_to_all | solution.py:431
  36.4 4.7 %collective-permute-start.4 = (bf16[2,128,1280]{2,1,0:T(8,128)(2,1)}, bf16[2,128,1280]{2,1,0:T(8,128)(2,1)S(1)}, u32[]{:S(2)}, u32[]{:S(2)}) collective-permute-start(bf16[2,128,1280]{2,1,0:T(8,128)(2,1)} %collective-permute-done.3.refs_1_), channel_id=1, source_target_pairs={{0,1},{1,0},{2,3},{3,2},{4,5},{5,4},{6,7},{7,6},{8,9},{9,8},{10,11... | collective-permute-start | bytes 1966088 | tf_op jit(solution)/shard_map/ppermute | solution.py:443
  39.2 5.8 %copy-start.7 = (bf16[8,32,1280]{2,1,0:T(8,128)(2,1)}, bf16[8,32,1280]{2,1,0:T(8,128)(2,1)S(1)}, u32[]{:S(2)}) copy-start(bf16[8,32,1280]{2,1,0:T(8,128)(2,1)S(1)} %pad_maximum_fusion.1.refs_4_) | copy-start | bytes 1966084
  39.2 5.7 %collective-permute-start.2 = (bf16[8,32,1280]{2,1,0:T(8,128)(2,1)S(1)}, bf16[8,32,1280]{2,1,0:T(8,128)(2,1)S(1)}, u32[]{:S(2)}, u32[]{:S(2)}) collective-permute-start(bf16[8,32,1280]{2,1,0:T(8,128)(2,1)S(1)} %pad_maximum_fusion.1.refs_4_), channel_id=1, source_target_pairs={{0,1},{1,0},{2,3},{3,2},{4,5},{5,4},{6,7},{7,6},{8,9},{9,8},{10,11... | collective-permute-start | bytes 1966088 | tf_op jit(solution)/shard_map/ppermute | solution.py:434
  41.1 0.8 copy-start.12
  44.9 0.8 copy-start.10
  58.5 11.5 %all-to-all-start.2 = ((bf16[4,2,4,32,256]{4,3,2,1,0:T(8,128)(2,1)}), bf16[4,2,4,32,256]{4,3,2,1,0:T(8,128)(2,1)S(1)}, u32[]{:S(2)}, u32[]{:S(2)}) async-start(bf16[4,2,4,32,256]{4,3,2,1,0:T(8,128)(2,1)} %get-tuple-element.45), calls=%async_computation.2 | async-start | bytes 1048576 | tf_op jit(solution)/shard_map/all_to_all | solution.py:452
  70.0 5.4 %copy-start.9 = (bf16[4,2,4,32,256]{4,3,2,1,0:T(8,128)(2,1)}, bf16[4,2,4,32,256]{4,3,2,1,0:T(8,128)(2,1)S(1)}, u32[]{:S(2)}) copy-start(bf16[4,2,4,32,256]{4,3,2,1,0:T(8,128)(2,1)S(1)} %all-to-all-done.2.got_in) | copy-start | bytes 1572868
  70.0 19.5 %all-to-all-start.3 = ((bf16[8,128,640]{2,1,0:T(8,128)(2,1)}), bf16[8,128,640]{2,1,0:T(8,128)(2,1)S(1)}, u32[]{:S(2)}, u32[]{:S(2)}) async-start(bf16[8,128,640]{2,1,0:T(8,128)(2,1)} %get-tuple-element.48), calls=%async_computation.3 | async-start | bytes 2621440 | tf_op jit(solution)/shard_map/all_to_all | solution.py:468
  78.1 4.3 %collective-permute-start.5 = (bf16[288,1280]{1,0:T(8,128)(2,1)}, bf16[288,1280]{1,0:T(8,128)(2,1)S(1)}, u32[]{:S(2)}, u32[]{:S(2)}) collective-permute-start(bf16[288,1280]{1,0:T(8,128)(2,1)} %get-tuple-element.54), channel_id=1, source_target_pairs={{0,1},{1,0},{2,3},{3,2},{4,5},{5,4},{6,7},{7,6},{8,9},{9,8},{10,11... | collective-permute-start | bytes 2211848 | tf_op jit(solution)/shard_map/ppermute | solution.py:488
  82.4 1.4 %copy-start = (bf16[2,288,1280]{2,1,0:T(8,128)(2,1)S(1)}, bf16[2,288,1280]{2,1,0:T(8,128)(2,1)}, u32[]{:S(2)}) copy-start(bf16[2,288,1280]{2,1,0:T(8,128)(2,1)} %get-tuple-element.53.refs_0_) | copy-start | bytes 4423684
  83.8 23.8 %copy-start.16 = (bf16[128,1280]{1,0:T(8,128)(2,1)S(1)}, bf16[128,1280]{1,0:T(8,128)(2,1)}, u32[]{:S(2)}) copy-start(bf16[128,1280]{1,0:T(8,128)(2,1)} %get-tuple-element.58) | copy-start | bytes 983044
  85.5 25.8 %copy-start.1 = (bf16[2,288,1280]{2,1,0:T(8,128)(2,1)S(1)}, bf16[2,288,1280]{2,1,0:T(8,128)(2,1)}, u32[]{:S(2)}) copy-start(bf16[2,288,1280]{2,1,0:T(8,128)(2,1)} %get-tuple-element.53.refs_0_) | copy-start | bytes 4423684
  85.5 25.8 %copy-start.3 = (bf16[1,32,1280]{2,1,0:T(8,128)(2,1)S(1)}, bf16[1,32,1280]{2,1,0:T(8,128)(2,1)}, u32[]{:S(2)}) copy-start(bf16[1,32,1280]{2,1,0:T(8,128)(2,1)} %refs_6_.1) | copy-start | bytes 245764
  85.5 25.8 %copy-start.4 = (f32[1280]{0:T(1024)S(1)}, f32[1280]{0:T(1024)}, u32[]{:S(2)}) copy-start(f32[1280]{0:T(1024)} %refs_5_.1) | copy-start | bytes 15364
  85.5 25.8 %copy-start.5 = (f32[1280]{0:T(1024)S(1)}, f32[1280]{0:T(1024)}, u32[]{:S(2)}) copy-start(f32[1280]{0:T(1024)} %refs_7_.1) | copy-start | bytes 15364
  85.6 25.8 %collective-permute-start.8 = (bf16[288,1280]{1,0:T(8,128)(2,1)}, bf16[288,1280]{1,0:T(8,128)(2,1)}, u32[]{:S(2)}, u32[]{:S(2)}) collective-permute-start(bf16[288,1280]{1,0:T(8,128)(2,1)} %add_updates.1), channel_id=1, source_target_pairs={{0,8},{1,9},{2,10},{3,11},{4,12},{5,13},{6,14},{7,15},{8,0},{9,1},... | collective-permute-start | bytes 2211848 | tf_op jit(solution)/shard_map/ppermute | solution.py:490
  90.5 30.6 %all-to-all-start.4 = ((bf16[16,40,128]{2,1,0:T(8,128)(2,1)}), bf16[16,40,128]{2,1,0:T(8,128)(2,1)S(1)}, u32[]{:S(2)}, u32[]{:S(2)}) async-start(bf16[16,40,128]{2,1,0:T(8,128)(2,1)} %bitcast.8), calls=%async_computation.4 | async-start | bytes 327680 | tf_op jit(solution)/shard_map/all_to_all | solution.py:496
  105.7 5.6 %collective-permute-start.7 = (bf16[160,1280]{1,0:T(8,128)(2,1)}, bf16[160,1280]{1,0:T(8,128)(2,1)S(1)}, u32[]{:S(2)}, u32[]{:S(2)}) collective-permute-start(bf16[160,1280]{1,0:T(8,128)(2,1)} %get-tuple-element.59), channel_id=1, source_target_pairs={{0,1},{1,0},{2,3},{3,2},{4,5},{5,4},{6,7},{7,6},{8,9},{9,8},{10,11... | collective-permute-start | bytes 1228808 | tf_op jit(solution)/shard_map/ppermute | solution.py:506
  107.7 3.6 %collective-permute-start.6 = (bf16[128,1280]{1,0:T(8,128)(2,1)S(1)}, bf16[128,1280]{1,0:T(8,128)(2,1)S(1)}, u32[]{:S(2)}, u32[]{:S(2)}) collective-permute-start(bf16[128,1280]{1,0:T(8,128)(2,1)S(1)} %copy-done.16), channel_id=1, source_target_pairs={{0,1},{1,0},{2,3},{3,2},{4,5},{5,4},{6,7},{7,6},{8,9},{9,8},{10,11... | collective-permute-start | bytes 983048 | tf_op jit(solution)/shard_map/ppermute | solution.py:505
